TPU v7x, 32 devices: a whole 2x2x4 slice. The times are simulated.
32 devices in a mesh: groups: 2 (over x), ta: 4 (over y, core), xy: 4 (over z).
Axes of the slice: x: 2, y: 2, z: 4, core: 2. Of those that a mesh axis runs over, the one named last changes fastest.
Arguments:
- sources: bfloat16 [8, 4, 4, 8, 96, 256], P('groups', 'ta', 'xy'), parts along dimension 0, may hold values from -24 to 24
- coarse_links: bfloat16 [18, 4, 4, 4, 8, 96, 96], P('groups', None, 'ta', 'xy'), parts along dimension 0, may hold values from -0.119628906 to 0.119628906
Outputs:
- solution: float32 [8, 4, 4, 8, 96, 256], P('groups', 'ta', 'xy'), parts along dimension 0
There are 2 independent parts, one for each index of `groups`. A program takes and returns all parts, laid end to end along the dimension named above; each array names one. Nothing has to cross between parts.
All inputs are finite; a program needn't handle non-finite values.
Results may differ from a plain program's by a relative error of at most 0.0019.
The roundings to bfloat16 on the way count: a program that leaves them out, or rounds other values in their place, can miss the bound.
Values may be sent and summed in bfloat16 or wider, within the bound.
No kernel may reach another device: no remote copies, remote signals or barrier semaphores. Data moves between devices by JAX's collectives and lax.ppermute only.
A program may use at most 128 MiB of HBM per device.

v0:
```python
import jax
import jax.numpy as jnp
from jax import lax
from jax.sharding import PartitionSpec as P

ITERS = 2


mass_term = 2.0


def with_halo(cells, sides, width):
    for axis, dim in sides:
        count = lax.axis_size(axis)
        head = lax.slice_in_dim(cells, 0, width, axis=dim)
        tail = lax.slice_in_dim(cells, cells.shape[dim] - width, cells.shape[dim], axis=dim)
        cells = jnp.concatenate(
            [
                lax.ppermute(tail, axis, [(i, (i + 1) % count) for i in range(count)]),
                cells,
                lax.ppermute(head, axis, [((i + 1) % count, i) for i in range(count)]),
            ],
            axis=dim,
        )
    return cells


def link_product(link_field, vector, flipped):
    einsum_form = "abcdio,abcdir->abcdor" if flipped else "abcdoi,abcdir->abcdor"
    return jnp.einsum(einsum_form, link_field, vector, preferred_element_type=jnp.float32)


def widen(vector):
    return with_halo(vector, (("ta", 1), ("xy", 2)), 1)


def apply_forward(rounded, coarse_links):
    padded = widen(rounded)
    neighbours = (
        padded[:, 2:, 1:-1],
        padded[:, :-2, 1:-1],
        padded[:, 1:-1, 2:],
        padded[:, 1:-1, :-2],
        jnp.roll(rounded, -1, 0),
        jnp.roll(rounded, 1, 0),
        jnp.roll(rounded, -1, 3),
        jnp.roll(rounded, 1, 3),
    )
    summed = mass_term * rounded.astype(jnp.float32) + link_product(coarse_links[0], rounded, False)
    for number in range(8):
        summed = summed + link_product(coarse_links[number + 1], neighbours[number], False)
    return summed


def local_adjoint(image_vec, coarse_links):
    summed = mass_term * image_vec.astype(jnp.float32) + link_product(
        coarse_links[0], image_vec, True
    )
    plane_moves = ((4, 1, 0), (5, -1, 0), (6, 1, 3), (7, -1, 3))
    for number, sign_value, axis_number in plane_moves:
        adjoint_term = link_product(coarse_links[number + 1], image_vec, True).astype(jnp.bfloat16)
        summed = summed + jnp.roll(adjoint_term, sign_value, axis_number).astype(jnp.float32)
    return summed


def adjoint_products(image_vec, coarse_links):
    summed = local_adjoint(image_vec, coarse_links)
    adjoint_terms = [
        link_product(coarse_links[number + 1], image_vec, True).astype(jnp.bfloat16)
        for number in range(4)
    ]
    rim_time = jnp.concatenate((adjoint_terms[1], adjoint_terms[0]), axis=1)
    ext_time = with_halo(rim_time, (("ta", 1),), 1)
    rim_space = jnp.concatenate((adjoint_terms[3], adjoint_terms[2]), axis=2)
    ext_space = with_halo(rim_space, (("xy", 2),), 1)
    shifted = (
        jnp.concatenate((ext_time[:, :1], adjoint_terms[0][:, :-1]), axis=1),
        jnp.concatenate((adjoint_terms[1][:, 1:], ext_time[:, -1:]), axis=1),
        jnp.concatenate((ext_space[:, :, :1], adjoint_terms[2][:, :, :-1]), axis=2),
        jnp.concatenate((adjoint_terms[3][:, :, 1:], ext_space[:, :, -1:]), axis=2),
    )
    for moved_term in shifted:
        summed = summed + moved_term.astype(jnp.float32)
    return summed


def gram(left_vec, right_vec):
    left_rows = left_vec.reshape((-1,) + left_vec.shape[-2:])
    right_rows = right_vec.reshape((-1,) + right_vec.shape[-2:])
    return jnp.einsum("sir,sit->rt", left_rows, right_rows, precision=lax.Precision.HIGHEST)


def combine(vector, coefficients):
    return jnp.einsum("abcdir,rt->abcdit", vector, coefficients, precision=lax.Precision.HIGHEST)


def solve_spd(matrix, right_side):
    factor = jnp.linalg.cholesky(matrix)
    return jax.scipy.linalg.cho_solve((factor, True), right_side)


def residual_norms(residual):
    return lax.psum(gram(residual, residual), ("ta", "xy"))


def body(sources, coarse_links):
    residual = sources.astype(jnp.float32)
    solution = jnp.zeros_like(residual)
    search = residual
    energy = residual_norms(residual)
    for iteration in range(ITERS):
        rounded = search.astype(jnp.bfloat16)
        image_vec = apply_forward(rounded, coarse_links).astype(jnp.bfloat16)
        normal_image = adjoint_products(image_vec, coarse_links)
        curvature, cross_term, image_gram = lax.psum(
            (
                gram(search, normal_image),
                gram(residual, normal_image),
                gram(normal_image, normal_image),
            ),
            ("ta", "xy"),
        )
        alpha_step = solve_spd(curvature, energy)
        solution = solution + combine(search, alpha_step)
        if iteration + 1 < ITERS:
            residual = residual - combine(normal_image, alpha_step)
            mixed_term = jnp.dot(cross_term, alpha_step, precision=lax.Precision.HIGHEST)
            quadratic = jnp.dot(
                alpha_step.T,
                jnp.dot(image_gram, alpha_step, precision=lax.Precision.HIGHEST),
                precision=lax.Precision.HIGHEST,
            )
            fresh_energy = energy - mixed_term - mixed_term.T + quadratic
            beta_step = solve_spd(energy, fresh_energy)
            search = residual + combine(search, beta_step)
            energy = fresh_energy
    return solution


def solution(mesh):
    return jax.shard_map(
        body,
        mesh=mesh,
        in_specs=(
            P("groups", "ta", "xy", None, None, None),
            P("groups", None, "ta", "xy", None, None, None),
        ),
        out_specs=P("groups", "ta", "xy", None, None, None),
        check_vma=False,
    )
```

profile of v0, /device:TPU:0, one launch (start us, length us, event | category | flops | bytes accessed | tf_op | source)
XLA Modules:
  0.0 1093.9 jit_solution(8653942792856709858)
XLA Ops:
  8.9 35.1 %collective-permute-done = bf16[4,1,1,8,96,256]{5,4,3,0,2,1:T(8,128)(2,1)S(1)} collective-permute-done((bf16[4,1,1,8,96,256]{5,4,3,0,2,1:T(8,128)(2,1)}, bf16[4,1,1,8,96,256]{5,4,3,0,2,1:T(8,128)(2,1)S(1)}, u32[]{:S(2)}, u32[]{:S(2)}) %collective-permute-start) | collective-permute-done | bytes 1572896 | tf_op jit(solution)/shard_map/ppermute | solution.py:21
  65.1 87.7 %collective-permute-done.2 = bf16[4,3,1,8,96,256]{5,4,3,0,2,1:T(8,128)(2,1)S(1)} collective-permute-done((bf16[4,3,1,8,96,256]{5,4,3,0,2,1:T(8,128)(2,1)S(1)}, bf16[4,3,1,8,96,256]{5,4,3,0,2,1:T(8,128)(2,1)S(1)}, u32[]{:S(2)}, u32[]{:S(2)}) %collective-permute-start.2) | collective-permute-done | bytes 4718624 | tf_op jit(solution)/shard_map/ppermute | solution.py:21
  155.1 98.1 %collective-permute-done.3 = bf16[4,3,1,8,96,256]{5,4,3,0,2,1:T(8,128)(2,1)} collective-permute-done((bf16[4,3,1,8,96,256]{5,4,3,0,2,1:T(8,128)(2,1)S(1)}, bf16[4,3,1,8,96,256]{5,4,3,0,2,1:T(8,128)(2,1)}, u32[]{:S(2)}, u32[]{:S(2)}) %collective-permute-start.3) | collective-permute-done | bytes 4718624 | tf_op jit(solution)/shard_map/ppermute | solution.py:19
  253.2 8.8 fusion.9
  274.2 24.5 %collective-permute-done.4 = bf16[4,1,1,8,96,256]{5,4,3,0,2,1:T(8,128)(2,1)S(1)} collective-permute-done((bf16[4,1,1,8,96,256]{5,4,3,0,2,1:T(8,128)(2,1)S(1)}, bf16[4,1,1,8,96,256]{5,4,3,0,2,1:T(8,128)(2,1)S(1)}, u32[]{:S(2)}, u32[]{:S(2)}) %collective-permute-start.4) | collective-permute-done | bytes 1572896 | tf_op jit(solution)/shard_map/ppermute | solution.py:19
  305.3 33.0 %collective-permute-done.7 = bf16[4,1,1,8,96,256]{5,4,3,0,2,1:T(8,128)(2,1)S(1)} collective-permute-done((bf16[4,1,1,8,96,256]{5,4,3,0,2,1:T(8,128)(2,1)S(1)}, bf16[4,1,1,8,96,256]{5,4,3,0,2,1:T(8,128)(2,1)S(1)}, u32[]{:S(2)}, u32[]{:S(2)}) %collective-permute-start.7) | collective-permute-done | bytes 1572896 | tf_op jit(solution)/shard_map/ppermute | solution.py:21
  344.2 6.4 convolution_bitcast_fusion.3
  350.7 91.2 %all-reduce.7.cloned.1.call-done = (f32[256,256]{0,1:T(8,128)}, f32[256,256]{0,1:T(8,128)}, f32[256,256]{1,0:T(8,128)}) async-done(((f32[256,256]{0,1:T(8,128)}, f32[256,256]{0,1:T(8,128)}, f32[256,256]{1,0:T(8,128)}), (f32[256,256]{0,1:T(8,128)}, f32[256,256]{0,1:T(8,128)}, f32[256,256]{1,0:T(8,128)})) %all-reduce.7.cloned.1.call-update) | async-done | bytes 786448 | tf_op jit(solution)/shard_map/psum | solution.py:103
  444.1 11.7 %cholesky.206 = f32[128,128]{1,0:T(8,128)S(1)} custom-call(f32[128,128]{1,0:T(8,128)S(1)} %cholesky.273), custom_call_target="Cholesky" | custom-call | tf_op jit(solution)/shard_map/jit(cholesky)/cholesky | solution.py:98
  455.9 9.8 custom-call.19
  466.2 11.7 %cholesky.223 = f32[128,128]{1,0:T(8,128)S(1)} custom-call(f32[128,128]{1,0:T(8,128)S(1)} %convolution_subtract_fusion.7), custom_call_target="Cholesky" | custom-call | tf_op jit(solution)/shard_map/jit(cholesky)/cholesky | solution.py:98
  485.0 19.7 %custom-call.20 = f32[2,128,128]{1,2,0:T(8,128)S(1)} custom-call(f32[2,128,128]{2,1,0:T(8,128)S(1)} %get-tuple-element.28), custom_call_target="InvertDiagBlocksLowerTriangular" | custom-call | tf_op jit(solution)/shard_map/jit(_cho_solve)/triangular_solve | solution.py:99
  504.9 11.7 %cholesky.172 = f32[128,128]{1,0:T(8,128)S(1)} custom-call(f32[128,128]{1,0:T(8,128)S(1)} %cholesky.270), custom_call_target="Cholesky" | custom-call | tf_op jit(solution)/shard_map/jit(cholesky)/cholesky | solution.py:98
  516.7 9.8 custom-call.17
  527.0 11.7 %cholesky.189 = f32[128,128]{1,0:T(8,128)S(1)} custom-call(f32[128,128]{1,0:T(8,128)S(1)} %convolution_subtract_fusion.8), custom_call_target="Cholesky" | custom-call | tf_op jit(solution)/shard_map/jit(cholesky)/cholesky | solution.py:98
  545.2 20.1 %custom-call.18 = f32[2,128,128]{1,2,0:T(8,128)S(1)} custom-call(f32[2,128,128]{2,1,0:T(8,128)S(1)} %get-tuple-element.27), custom_call_target="InvertDiagBlocksLowerTriangular" | custom-call | tf_op jit(solution)/shard_map/jit(_cho_solve)/triangular_solve | solution.py:99
  577.1 33.4 %collective-permute-done.8 = bf16[4,1,1,8,96,256]{5,4,3,0,2,1:T(8,128)(2,1)S(1)} collective-permute-done((bf16[4,1,1,8,96,256]{5,4,3,0,2,1:T(8,128)(2,1)S(1)}, bf16[4,1,1,8,96,256]{5,4,3,0,2,1:T(8,128)(2,1)S(1)}, u32[]{:S(2)}, u32[]{:S(2)}) %collective-permute-start.8) | collective-permute-done | bytes 1572896 | tf_op jit(solution)/shard_map/ppermute | solution.py:21
  630.9 87.0 %collective-permute-done.10 = bf16[4,3,1,8,96,256]{5,4,3,0,2,1:T(8,128)(2,1)S(1)} collective-permute-done((bf16[4,3,1,8,96,256]{5,4,3,0,2,1:T(8,128)(2,1)S(1)}, bf16[4,3,1,8,96,256]{5,4,3,0,2,1:T(8,128)(2,1)S(1)}, u32[]{:S(2)}, u32[]{:S(2)}) %collective-permute-start.10) | collective-permute-done | bytes 4718624 | tf_op jit(solution)/shard_map/ppermute | solution.py:21
  720.1 99.5 %collective-permute-done.11 = bf16[4,3,1,8,96,256]{5,4,3,0,2,1:T(8,128)(2,1)} collective-permute-done((bf16[4,3,1,8,96,256]{5,4,3,0,2,1:T(8,128)(2,1)S(1)}, bf16[4,3,1,8,96,256]{5,4,3,0,2,1:T(8,128)(2,1)}, u32[]{:S(2)}, u32[]{:S(2)}) %collective-permute-start.11) | collective-permute-done | bytes 4718624 | tf_op jit(solution)/shard_map/ppermute | solution.py:19
  819.7 9.6 fusion.19
  841.3 29.0 %collective-permute-done.12 = bf16[4,1,1,8,96,256]{5,4,3,0,2,1:T(8,128)(2,1)S(1)} collective-permute-done((bf16[4,1,1,8,96,256]{5,4,3,0,2,1:T(8,128)(2,1)S(1)}, bf16[4,1,1,8,96,256]{5,4,3,0,2,1:T(8,128)(2,1)S(1)}, u32[]{:S(2)}, u32[]{:S(2)}) %collective-permute-start.12) | collective-permute-done | bytes 1572896 | tf_op jit(solution)/shard_map/ppermute | solution.py:19
  870.3 4.8 collective-permute-done.14
  876.2 30.3 %collective-permute-done.15 = bf16[4,1,1,8,96,256]{5,4,3,0,2,1:T(8,128)(2,1)} collective-permute-done((bf16[4,1,1,8,96,256]{5,4,3,0,2,1:T(8,128)(2,1)S(1)}, bf16[4,1,1,8,96,256]{5,4,3,0,2,1:T(8,128)(2,1)}, u32[]{:S(2)}, u32[]{:S(2)}) %collective-permute-start.15) | collective-permute-done | bytes 1572896 | tf_op jit(solution)/shard_map/ppermute | solution.py:21
  906.6 4.7 fusion.18
  911.3 6.0 convolution_bitcast_fusion.2
  920.4 85.2 %all-reduce.5.cloned.1.call-done = f32[256,256]{0,1:T(8,128)} async-done(((f32[256,256]{0,1:T(8,128)}), f32[256,256]{0,1:T(8,128)}) %all-reduce.5.cloned.1.call-update) | async-done | bytes 262160 | tf_op jit(solution)/shard_map/psum | solution.py:115
  1009.2 11.7 %cholesky.240 = f32[128,128]{1,0:T(8,128)S(1)} custom-call(f32[128,128]{1,0:T(8,128)S(1)} %cholesky.276), custom_call_target="Cholesky" | custom-call | tf_op jit(solution)/shard_map/jit(cholesky)/cholesky | solution.py:98
  1021.6 10.0 custom-call.21
  1034.5 11.7 %cholesky.257 = f32[128,128]{1,0:T(8,128)S(1)} custom-call(f32[128,128]{1,0:T(8,128)S(1)} %convolution_subtract_fusion.6), custom_call_target="Cholesky" | custom-call | tf_op jit(solution)/shard_map/jit(cholesky)/cholesky | solution.py:98
  1051.0 5.6 while.8
  1057.2 20.5 %custom-call.22 = f32[2,128,128]{1,2,0:T(8,128)S(1)} custom-call(f32[2,128,128]{2,1,0:T(8,128)} %copy-done.13), custom_call_target="InvertDiagBlocksLowerTriangular" | custom-call | tf_op jit(solution)/shard_map/jit(_cho_solve)/triangular_solve | solution.py:99
  1081.2 5.4 fusion.32
  (217 shorter events, 143.4 us)
Async XLA Ops:
  6.5 435.4 %all-reduce.7.cloned.1.call-start = ((), (), s32[]{:S(2)}) async-start(), calls=%async_computation.1 | async-start | bytes 1572864 | tf_op jit(solution)/shard_map/psum | solution.py:103
  6.5 37.5 %collective-permute-start = (bf16[4,1,1,8,96,256]{5,4,3,0,2,1:T(8,128)(2,1)}, bf16[4,1,1,8,96,256]{5,4,3,0,2,1:T(8,128)(2,1)S(1)}, u32[]{:S(2)}, u32[]{:S(2)}) collective-permute-start(bf16[4,1,1,8,96,256]{5,4,3,0,2,1:T(8,128)(2,1)} %bitcast.587), channel_id=1, source_target_pairs={{4,0},{8,4},{12,8},{0,12},{5,1},{9,5},{13,9},{1,13},{6,2},{10,6},{... | collective-permute-start | bytes 4718600 | tf_op jit(solution)/shard_map/ppermute | solution.py:21
  8.9 36.1 %collective-permute-start.1 = (bf16[4,1,1,8,96,256]{5,4,3,0,2,1:T(8,128)(2,1)}, bf16[4,1,1,8,96,256]{5,4,3,0,2,1:T(8,128)(2,1)S(1)}, u32[]{:S(2)}, u32[]{:S(2)}) collective-permute-start(bf16[4,1,1,8,96,256]{5,4,3,0,2,1:T(8,128)(2,1)} %bitcast.588), channel_id=1, source_target_pairs={{0,4},{4,8},{8,12},{12,0},{1,5},{5,9},{9,13},{13,1},{2,6},{6,10},{... | collective-permute-start | bytes 4718600 | tf_op jit(solution)/shard_map/ppermute | solution.py:19
  46.9 105.9 %collective-permute-start.2 = (bf16[4,3,1,8,96,256]{5,4,3,0,2,1:T(8,128)(2,1)S(1)}, bf16[4,3,1,8,96,256]{5,4,3,0,2,1:T(8,128)(2,1)S(1)}, u32[]{:S(2)}, u32[]{:S(2)}) collective-permute-start(bf16[4,3,1,8,96,256]{5,4,3,0,2,1:T(8,128)(2,1)S(1)} %pad_maximum_fusion), channel_id=1, source_target_pairs={{1,0},{2,1},{3,2},{0,3},{5,4},{6,5},{7,6},{4,7},{9,8},{10,9},{11,1... | collective-permute-start | bytes 14155784 | tf_op jit(solution)/shard_map/ppermute | solution.py:21
  50.5 202.7 %collective-permute-start.3 = (bf16[4,3,1,8,96,256]{5,4,3,0,2,1:T(8,128)(2,1)S(1)}, bf16[4,3,1,8,96,256]{5,4,3,0,2,1:T(8,128)(2,1)}, u32[]{:S(2)}, u32[]{:S(2)}) collective-permute-start(bf16[4,3,1,8,96,256]{5,4,3,0,2,1:T(8,128)(2,1)S(1)} %pad_maximum_fusion), channel_id=1, source_target_pairs={{0,1},{1,2},{2,3},{3,0},{4,5},{5,6},{6,7},{7,4},{8,9},{9,10},{10,1... | collective-permute-start | bytes 14155784 | tf_op jit(solution)/shard_map/ppermute | solution.py:19
  264.5 34.2 %collective-permute-start.4 = (bf16[4,1,1,8,96,256]{5,4,3,0,2,1:T(8,128)(2,1)S(1)}, bf16[4,1,1,8,96,256]{5,4,3,0,2,1:T(8,128)(2,1)S(1)}, u32[]{:S(2)}, u32[]{:S(2)}) collective-permute-start(bf16[4,1,1,8,96,256]{5,4,3,0,2,1:T(8,128)(2,1)S(1)} %fusion.109), channel_id=1, source_target_pairs={{0,4},{4,8},{8,12},{12,0},{1,5},{5,9},{9,13},{13,1},{2,6},{6,10},{... | collective-permute-start | bytes 4718600 | tf_op jit(solution)/shard_map/ppermute | solution.py:19
  264.6 36.4 %collective-permute-start.5 = (bf16[4,1,1,8,96,256]{5,4,3,0,2,1:T(8,128)(2,1)S(1)}, bf16[4,1,1,8,96,256]{5,4,3,0,2,1:T(8,128)(2,1)S(1)}, u32[]{:S(2)}, u32[]{:S(2)}) collective-permute-start(bf16[4,1,1,8,96,256]{5,4,3,0,2,1:T(8,128)(2,1)S(1)} %fusion.112), channel_id=1, source_target_pairs={{4,0},{8,4},{12,8},{0,12},{5,1},{9,5},{13,9},{1,13},{6,2},{10,6},{... | collective-permute-start | bytes 4718600 | tf_op jit(solution)/shard_map/ppermute | solution.py:21
  266.3 39.0 %collective-permute-start.6 = (bf16[4,1,1,8,96,256]{5,4,3,0,2,1:T(8,128)(2,1)S(1)}, bf16[4,1,1,8,96,256]{5,4,3,0,2,1:T(8,128)(2,1)S(1)}, u32[]{:S(2)}, u32[]{:S(2)}) collective-permute-start(bf16[4,1,1,8,96,256]{5,4,3,0,2,1:T(8,128)(2,1)S(1)} %fusion.115), channel_id=1, source_target_pairs={{0,1},{1,2},{2,3},{3,0},{4,5},{5,6},{6,7},{7,4},{8,9},{9,10},{10,1... | collective-permute-start | bytes 4718600 | tf_op jit(solution)/shard_map/ppermute | solution.py:19
  267.9 70.4 %collective-permute-start.7 = (bf16[4,1,1,8,96,256]{5,4,3,0,2,1:T(8,128)(2,1)S(1)}, bf16[4,1,1,8,96,256]{5,4,3,0,2,1:T(8,128)(2,1)S(1)}, u32[]{:S(2)}, u32[]{:S(2)}) collective-permute-start(bf16[4,1,1,8,96,256]{5,4,3,0,2,1:T(8,128)(2,1)S(1)} %fusion.118), channel_id=1, source_target_pairs={{1,0},{2,1},{3,2},{0,3},{5,4},{6,5},{7,6},{4,7},{9,8},{10,9},{11,1... | collective-permute-start | bytes 4718600 | tf_op jit(solution)/shard_map/ppermute | solution.py:21
  273.9 64.5 %slice-start.8 = ((bf16[4,1,1,8,96,256]{5,4,3,0,2,1:T(8,128)(2,1)}), bf16[4,1,1,7,96,256]{5,4,3,0,2,1:T(8,128)(2,1)S(1)}, s32[]{:S(2)}) async-start(bf16[4,1,1,8,96,256]{5,4,3,0,2,1:T(8,128)(2,1)} %copy-done.7), calls=%async_computation.10 | async-start | bytes 2752512 | tf_op jit(solution)/shard_map/jit(_roll_static)/slice | solution.py:62
  273.9 64.5 %slice-start.9 = ((bf16[4,1,1,8,96,256]{5,4,3,0,2,1:T(8,128)(2,1)}), bf16[4,1,1,1,96,256]{5,4,3,0,2,1:T(8,128)(2,1)S(1)}, s32[]{:S(2)}) async-start(bf16[4,1,1,8,96,256]{5,4,3,0,2,1:T(8,128)(2,1)} %copy-done.7), calls=%async_computation.11 | async-start | bytes 393216 | tf_op jit(solution)/shard_map/jit(_roll_static)/slice | solution.py:62
  273.9 64.5 %slice-start.10 = ((bf16[4,1,1,8,96,256]{5,4,3,0,2,1:T(8,128)(2,1)}), bf16[4,1,1,7,96,256]{5,4,3,0,2,1:T(8,128)(2,1)S(1)}, s32[]{:S(2)}) async-start(bf16[4,1,1,8,96,256]{5,4,3,0,2,1:T(8,128)(2,1)} %copy-done.8), calls=%async_computation.12 | async-start | bytes 2752512 | tf_op jit(solution)/shard_map/jit(_roll_static)/slice | solution.py:62
  273.9 64.5 %slice-start.11 = ((bf16[4,1,1,8,96,256]{5,4,3,0,2,1:T(8,128)(2,1)}), bf16[4,1,1,1,96,256]{5,4,3,0,2,1:T(8,128)(2,1)S(1)}, s32[]{:S(2)}) async-start(bf16[4,1,1,8,96,256]{5,4,3,0,2,1:T(8,128)(2,1)} %copy-done.8), calls=%async_computation.13 | async-start | bytes 393216 | tf_op jit(solution)/shard_map/jit(_roll_static)/slice | solution.py:62
  350.6 654.9 %all-reduce.5.cloned.1.call-start = ((), (), s32[]{:S(2)}) async-start(), calls=%async_computation | async-start | bytes 524288 | tf_op jit(solution)/shard_map/psum | solution.py:115
  441.9 62.7 %copy-start.10 = (f32[256,256]{0,1:T(8,128)S(1)}, f32[256,256]{0,1:T(8,128)}, u32[]{:S(2)}) copy-start(f32[256,256]{0,1:T(8,128)} %get-tuple-element.55) | copy-start | bytes 786436
  455.8 109.5 %copy-start.9 = (f32[256,256]{0,1:T(8,128)S(1)}, f32[256,256]{0,1:T(8,128)}, u32[]{:S(2)}) copy-start(f32[256,256]{0,1:T(8,128)} %get-tuple-element.54) | copy-start | bytes 786436
  504.9 63.1 %copy-start.12 = (f32[256,256]{1,0:T(8,128)S(1)}, f32[256,256]{1,0:T(8,128)}, u32[]{:S(2)}) copy-start(f32[256,256]{1,0:T(8,128)} %get-tuple-element.56) | copy-start | bytes 786436
  572.3 44.1 %slice-start.2 = ((s8[7077888]{0:T(1024)(128)(4,1)}), s8[4194304]{0:T(1024)(128)(4,1)S(1)}, s32[]{:S(2)}) async-start(s8[7077888]{0:T(1024)(128)(4,1)} %bitcast.616), calls=%async_computation.4 | async-start | bytes 8388608
  576.6 33.9 %collective-permute-start.8 = (bf16[4,1,1,8,96,256]{5,4,3,0,2,1:T(8,128)(2,1)S(1)}, bf16[4,1,1,8,96,256]{5,4,3,0,2,1:T(8,128)(2,1)S(1)}, u32[]{:S(2)}, u32[]{:S(2)}) collective-permute-start(bf16[4,1,1,8,96,256]{5,4,3,0,2,1:T(8,128)(2,1)S(1)} %get-tuple-element.95), channel_id=1, source_target_pairs={{4,0},{8,4},{12,8},{0,12},{5,1},{9,5},{13,9},{1,13},{6,2},{10,6},{... | collective-permute-start | bytes 4718600 | tf_op jit(solution)/shard_map/ppermute | solution.py:21
  576.6 36.7 %collective-permute-start.9 = (bf16[4,1,1,8,96,256]{5,4,3,0,2,1:T(8,128)(2,1)S(1)}, bf16[4,1,1,8,96,256]{5,4,3,0,2,1:T(8,128)(2,1)S(1)}, u32[]{:S(2)}, u32[]{:S(2)}) collective-permute-start(bf16[4,1,1,8,96,256]{5,4,3,0,2,1:T(8,128)(2,1)S(1)} %get-tuple-element.95), channel_id=1, source_target_pairs={{0,4},{4,8},{8,12},{12,0},{1,5},{5,9},{9,13},{13,1},{2,6},{6,10},{... | collective-permute-start | bytes 4718600 | tf_op jit(solution)/shard_map/ppermute | solution.py:19
  613.8 104.1 %collective-permute-start.10 = (bf16[4,3,1,8,96,256]{5,4,3,0,2,1:T(8,128)(2,1)S(1)}, bf16[4,3,1,8,96,256]{5,4,3,0,2,1:T(8,128)(2,1)S(1)}, u32[]{:S(2)}, u32[]{:S(2)}) collective-permute-start(bf16[4,3,1,8,96,256]{5,4,3,0,2,1:T(8,128)(2,1)S(1)} %pad_maximum_fusion.1), channel_id=1, source_target_pairs={{1,0},{2,1},{3,2},{0,3},{5,4},{6,5},{7,6},{4,7},{9,8},{10,9},{11,1... | collective-permute-start | bytes 14155784 | tf_op jit(solution)/shard_map/ppermute | solution.py:21
  615.2 204.4 %collective-permute-start.11 = (bf16[4,3,1,8,96,256]{5,4,3,0,2,1:T(8,128)(2,1)S(1)}, bf16[4,3,1,8,96,256]{5,4,3,0,2,1:T(8,128)(2,1)}, u32[]{:S(2)}, u32[]{:S(2)}) collective-permute-start(bf16[4,3,1,8,96,256]{5,4,3,0,2,1:T(8,128)(2,1)S(1)} %pad_maximum_fusion.1), channel_id=1, source_target_pairs={{0,1},{1,2},{2,3},{3,0},{4,5},{5,6},{6,7},{7,4},{8,9},{9,10},{10,1... | collective-permute-start | bytes 14155784 | tf_op jit(solution)/shard_map/ppermute | solution.py:19
  834.2 36.1 %collective-permute-start.12 = (bf16[4,1,1,8,96,256]{5,4,3,0,2,1:T(8,128)(2,1)S(1)}, bf16[4,1,1,8,96,256]{5,4,3,0,2,1:T(8,128)(2,1)S(1)}, u32[]{:S(2)}, u32[]{:S(2)}) collective-permute-start(bf16[4,1,1,8,96,256]{5,4,3,0,2,1:T(8,128)(2,1)S(1)} %fusion.133), channel_id=1, source_target_pairs={{0,4},{4,8},{8,12},{12,0},{1,5},{5,9},{9,13},{13,1},{2,6},{6,10},{... | collective-permute-start | bytes 4718600 | tf_op jit(solution)/shard_map/ppermute | solution.py:19
  834.2 36.1 %collective-permute-start.13 = (bf16[4,1,1,8,96,256]{5,4,3,0,2,1:T(8,128)(2,1)S(1)}, bf16[4,1,1,8,96,256]{5,4,3,0,2,1:T(8,128)(2,1)S(1)}, u32[]{:S(2)}, u32[]{:S(2)}) collective-permute-start(bf16[4,1,1,8,96,256]{5,4,3,0,2,1:T(8,128)(2,1)S(1)} %fusion.136), channel_id=1, source_target_pairs={{4,0},{8,4},{12,8},{0,12},{5,1},{9,5},{13,9},{1,13},{6,2},{10,6},{... | collective-permute-start | bytes 4718600 | tf_op jit(solution)/shard_map/ppermute | solution.py:21
  835.9 39.1 %collective-permute-start.14 = (bf16[4,1,1,8,96,256]{5,4,3,0,2,1:T(8,128)(2,1)S(1)}, bf16[4,1,1,8,96,256]{5,4,3,0,2,1:T(8,128)(2,1)S(1)}, u32[]{:S(2)}, u32[]{:S(2)}) collective-permute-start(bf16[4,1,1,8,96,256]{5,4,3,0,2,1:T(8,128)(2,1)S(1)} %fusion.139), channel_id=1, source_target_pairs={{0,1},{1,2},{2,3},{3,0},{4,5},{5,6},{6,7},{7,4},{8,9},{9,10},{10,1... | collective-permute-start | bytes 4718600 | tf_op jit(solution)/shard_map/ppermute | solution.py:19
  835.9 70.6 %collective-permute-start.15 = (bf16[4,1,1,8,96,256]{5,4,3,0,2,1:T(8,128)(2,1)S(1)}, bf16[4,1,1,8,96,256]{5,4,3,0,2,1:T(8,128)(2,1)}, u32[]{:S(2)}, u32[]{:S(2)}) collective-permute-start(bf16[4,1,1,8,96,256]{5,4,3,0,2,1:T(8,128)(2,1)S(1)} %fusion.142), channel_id=1, source_target_pairs={{1,0},{2,1},{3,2},{0,3},{5,4},{6,5},{7,6},{4,7},{9,8},{10,9},{11,1... | collective-permute-start | bytes 4718600 | tf_op jit(solution)/shard_map/ppermute | solution.py:21
  841.0 65.5 %slice-start.4 = ((bf16[4,1,1,8,96,256]{5,4,3,0,2,1:T(8,128)(2,1)}), bf16[4,1,1,7,96,256]{5,4,3,0,2,1:T(8,128)(2,1)S(1)}, s32[]{:S(2)}) async-start(bf16[4,1,1,8,96,256]{5,4,3,0,2,1:T(8,128)(2,1)} %copy-done.5), calls=%async_computation.6 | async-start | bytes 2752512 | tf_op jit(solution)/shard_map/jit(_roll_static)/slice | solution.py:62
  841.1 65.5 %slice-start.5 = ((bf16[4,1,1,8,96,256]{5,4,3,0,2,1:T(8,128)(2,1)}), bf16[4,1,1,1,96,256]{5,4,3,0,2,1:T(8,128)(2,1)S(1)}, s32[]{:S(2)}) async-start(bf16[4,1,1,8,96,256]{5,4,3,0,2,1:T(8,128)(2,1)} %copy-done.5), calls=%async_computation.7 | async-start | bytes 393216 | tf_op jit(solution)/shard_map/jit(_roll_static)/slice | solution.py:62
  841.1 65.5 %slice-start.6 = ((bf16[4,1,1,8,96,256]{5,4,3,0,2,1:T(8,128)(2,1)}), bf16[4,1,1,7,96,256]{5,4,3,0,2,1:T(8,128)(2,1)S(1)}, s32[]{:S(2)}) async-start(bf16[4,1,1,8,96,256]{5,4,3,0,2,1:T(8,128)(2,1)} %copy-done.6), calls=%async_computation.8 | async-start | bytes 2752512 | tf_op jit(solution)/shard_map/jit(_roll_static)/slice | solution.py:62
  841.1 65.5 %slice-start.7 = ((bf16[4,1,1,8,96,256]{5,4,3,0,2,1:T(8,128)(2,1)}), bf16[4,1,1,1,96,256]{5,4,3,0,2,1:T(8,128)(2,1)S(1)}, s32[]{:S(2)}) async-start(bf16[4,1,1,8,96,256]{5,4,3,0,2,1:T(8,128)(2,1)} %copy-done.6), calls=%async_computation.9 | async-start | bytes 393216 | tf_op jit(solution)/shard_map/jit(_roll_static)/slice | solution.py:62
  841.3 70.0 %copy-start.3 = (f32[4,1,1,8,96,256]{5,4,3,0,2,1:T(8,128)S(1)}, f32[4,1,1,8,96,256]{5,4,3,0,2,1:T(8,128)}, u32[]{:S(2)}) copy-start(f32[4,1,1,8,96,256]{5,4,3,0,2,1:T(8,128)} %get-tuple-element.96) | copy-start | bytes 9437188
  920.4 160.8 %copy-start.4 = (f32[4,1,1,8,96,256]{5,4,3,0,2,1:T(8,128)S(1)}, f32[4,1,1,8,96,256]{5,4,3,0,2,1:T(8,128)}, u32[]{:S(2)}) copy-start(f32[4,1,1,8,96,256]{5,4,3,0,2,1:T(8,128)} %get-tuple-element.96) | copy-start | bytes 9437188
  (14 other events, 114.7 us)
Sparse Core Ops, SparseCore 0:
  350.8 91.1 all-reduce.6
  917.4 88.1 all-reduce.4
where the time goes:
time: 1100 us; the launch traced here: 1090 us
  waiting for transfers between devices  749 us (68%)
  other arithmetic  171 us (16%)
  matrix products  110 us (10%)
  local copies, waits for them, and re-layouts  24.2 us (2%)
  starting transfers between devices  20.2 us (2%)
  between operations  18.5 us (2%)
    ppermute x8, waiting for transfers between devices, with_halo(): lax.ppermute(head, axis, [((i + 1) % count, i) for i in range(count)])  309 us
    ppermute x8, waiting for transfers between devices, with_halo(): lax.ppermute(tail, axis, [(i, (i + 1) % count) for i in range(count)])  264 us
    another operation x21, other arithmetic, solve_spd(): factor = jnp.linalg.cholesky(matrix)  105 us
    psum x1, waiting for transfers between devices, residual_norms(): return lax.psum(gram(residual, residual), ('ta', 'xy'))  91.2 us
    psum x1, waiting for transfers between devices, body(): lax.psum((gram(search, normal_image), gram(residual, normal_image), gram(...  85.2 us
    dot_general x36, matrix products, link_product(): jnp.einsum(einsum_form, link_field, vector, preferred_element_type=jnp.fl...  66.3 us
    another operation x7, other arithmetic, solve_spd(): return jax.scipy.linalg.cho_solve((factor, True), right_side)  62 us
  transfers between devices with their start and end apart: 18, of which 17 were waited for; matrix products, arithmetic and copies ran while one was open for 4% of the time, Pallas kernels for 0%

commit v1 on v0

v1 whole, which is shorter than its diff:
```python
import jax
import jax.numpy as jnp
from jax import lax
from jax.sharding import PartitionSpec as P

ITERS = 2
MASS = 2.0
HIGHEST = lax.Precision.HIGHEST


def shift(value, axis, step):
    count = lax.axis_size(axis)
    return lax.ppermute(value, axis, [(i, (i + step) % count) for i in range(count)])


def swap(value, axis, bit):
    return lax.ppermute(value, axis, [(i, i ^ bit) for i in range(lax.axis_size(axis))])


def reduce_all(matrix):
    times, planes = lax.axis_size("ta"), lax.axis_size("xy")
    if times & (times - 1) or planes & (planes - 1) or times < 2:
        return lax.psum(matrix, ("ta", "xy"))
    half = matrix.shape[0] // 2
    upper = lax.rem(lax.axis_index("ta"), 2) == 0
    top, bottom = matrix[:half], matrix[half:]
    part = jnp.where(upper, top, bottom) + swap(jnp.where(upper, bottom, top), "ta", 1)
    bit = 2
    while bit < times:
        part = part + swap(part, "ta", bit)
        bit *= 2
    if planes <= 4:
        arrived = [shift(part, "xy", step) for step in range(1, planes)]
        index = lax.axis_index("xy")
        stacked = jnp.stack([part] + arrived)
        order = lax.rem(index - jnp.arange(planes) + planes, planes)
        part = jnp.sum(jnp.take(stacked, order, axis=0), axis=0)
    else:
        bit = 1
        while bit < planes:
            part = part + swap(part, "xy", bit)
            bit *= 2
    other = swap(part, "ta", 1)
    return jnp.concatenate([jnp.where(upper, part, other), jnp.where(upper, other, part)], axis=0)


def forward(link, vector):
    return jnp.einsum("yzoi,yzir->yzor", link, vector, preferred_element_type=jnp.float32)


def transposed(link, vector):
    return jnp.einsum("yzoi,yzor->yzir", link, vector, preferred_element_type=jnp.float32)


def apply_forward(vector, links):
    after_t, before_t = shift(vector, "ta", -1), shift(vector, "ta", 1)
    after_x, before_x = shift(vector, "xy", -1), shift(vector, "xy", 1)
    total = MASS * vector.astype(jnp.float32) + forward(links[0], vector)
    total += forward(links[5], jnp.roll(vector, -1, 0)) + forward(links[6], jnp.roll(vector, 1, 0))
    total += forward(links[7], jnp.roll(vector, -1, 1)) + forward(links[8], jnp.roll(vector, 1, 1))
    total += forward(links[1], after_t) + forward(links[2], before_t)
    return total + forward(links[3], after_x) + forward(links[4], before_x)


def apply_adjoint(image, links):
    products = [transposed(links[number], image).astype(jnp.bfloat16) for number in range(1, 9)]
    moved = [
        shift(products[2], "xy", 1),
        shift(products[3], "xy", -1),
        shift(products[0], "ta", 1),
        shift(products[1], "ta", -1),
    ]
    total = MASS * image.astype(jnp.float32) + transposed(links[0], image)
    for number, step, dim in ((4, 1, 0), (5, -1, 0), (6, 1, 1), (7, -1, 1)):
        total += jnp.roll(products[number], step, dim).astype(jnp.float32)
    for product in moved:
        total += product.astype(jnp.float32)
    return total


def gram(vector):
    rows = vector.reshape(-1, vector.shape[-1])
    if rows.dtype == jnp.bfloat16:
        return jnp.einsum("sr,st->rt", rows, rows, preferred_element_type=jnp.float32)
    return jnp.einsum("sr,st->rt", rows, rows, precision=HIGHEST)


def combine(vector, coefficients):
    return jnp.einsum("yzir,rt->yzit", vector.astype(jnp.float32), coefficients, precision=HIGHEST)


def body(sources, links):
    shape = sources.shape
    source = sources.reshape(shape[0], shape[3], shape[4], shape[5])
    links = links.reshape(links.shape[0], shape[0], shape[3], links.shape[-2], links.shape[-1])
    residual = source.astype(jnp.float32)
    energy = reduce_all(gram(source))
    energy_factor = jnp.linalg.cholesky(energy)
    first_image = apply_forward(source, links).astype(jnp.bfloat16)
    first_curvature = reduce_all(gram(first_image))
    normal_image = apply_adjoint(first_image, links)
    alpha = jax.scipy.linalg.cho_solve((jnp.linalg.cholesky(first_curvature), True), energy)
    residual = residual - combine(normal_image, alpha)
    rounded = residual.astype(jnp.bfloat16)
    fresh = reduce_all(gram(residual))
    beta = jax.scipy.linalg.cho_solve((energy_factor, True), fresh)
    search = residual + combine(source, beta)
    second_image = (apply_forward(rounded, links) + combine(first_image, beta)).astype(jnp.bfloat16)
    second_curvature = reduce_all(gram(second_image))
    second_alpha = jax.scipy.linalg.cho_solve((jnp.linalg.cholesky(second_curvature), True), fresh)
    answer = combine(source, alpha) + combine(search, second_alpha)
    return answer.reshape(shape)


def solution(mesh):
    return jax.shard_map(
        body,
        mesh=mesh,
        in_specs=(
            P("groups", "ta", "xy", None, None, None),
            P("groups", None, "ta", "xy", None, None, None),
        ),
        out_specs=P("groups", "ta", "xy", None, None, None),
        check_vma=False,
    )
```

time: 1100 us -> 612 us (0.56)
  waiting for transfers between devices: 749 us -> 118 us
  starting transfers between devices: 20.2 us -> 73.5 us
  matrix products: 110 us -> 159 us
  local copies, waits for them, and re-layouts: 24.2 us -> 56.1 us
  other arithmetic: 171 us -> 194 us
  between operations: 18.5 us -> 4.83 us
    ppermute x16 -> x36, waiting for transfers between devices: 573 us -> 118 us  [the longest x24 74.8 us: shift(): lax.ppermute(value, axis, [(i, (i + step) % count) for i in range(count)])]
    psum x2 -> x0, waiting for transfers between devices: 176 us -> none  [the longest x1 91.2 us: residual_norms(): return lax.psum(gram(residual, residual), ('ta', 'xy'))]
    ppermute x16 -> x36, starting transfers between devices: 20.2 us -> 73.5 us  [the longest x24 65.4 us: shift(): lax.ppermute(value, axis, [(i, (i + step) % count) for i in range(count)])]
    dot_general x47 -> x35, matrix products: 99.3 us -> 134 us  [the longest x17 61 us: forward(): jnp.einsum('yzoi,yzir->yzor', link, vector, preferred_element_type=jnp.fl...]
    another operation x28 -> x30, other arithmetic: 167 us -> 185 us  [the longest x6 41.3 us: body(): energy_factor = jnp.linalg.cholesky(energy)]
    another operation x24, matrix products: 10.9 us -> 25 us  [the longest x6 7.24 us: body(): jax.scipy.linalg.cho_solve((jnp.linalg.cholesky(first_curvature), True),...]
    slice x24 -> x19, local copies, waits for them, and re-layouts: 1.39 us -> 14.5 us  [the longest x4 5.23 us: apply_forward(): jnp.roll(vector, 1, 1)]
  transfers between devices with their start and end apart: 18 -> 36, of which waited for: 17 -> 15; matrix products, arithmetic and copies ran while one was open for 4% -> 43% of each run, Pallas kernels for 0% -> 0%
where the time goes in v1:
time: 612 us; the launch traced here: 605 us
  other arithmetic  194 us (32%)
  matrix products  159 us (26%)
  waiting for transfers between devices  118 us (19%)
  starting transfers between devices  73.5 us (12%)
  local copies, waits for them, and re-layouts  56.1 us (9%)
    ppermute x24, waiting for transfers between devices, shift(): lax.ppermute(value, axis, [(i, (i + step) % count) for i in range(count)])  74.8 us
    ppermute x24, starting transfers between devices, shift(): lax.ppermute(value, axis, [(i, (i + step) % count) for i in range(count)])  65.4 us
    dot_general x17, matrix products, forward(): jnp.einsum('yzoi,yzir->yzor', link, vector, preferred_element_type=jnp.fl...  61 us
    ppermute x12, waiting for transfers between devices, swap(): lax.ppermute(value, axis, [(i, i ^ bit) for i in range(lax.axis_size(axis...  43.2 us
    another operation x6, other arithmetic, body(): energy_factor = jnp.linalg.cholesky(energy)  41.3 us
    another operation x6, other arithmetic, body(): jnp.linalg.cholesky(first_curvature)  38.4 us
    another operation x7, other arithmetic, body(): jnp.linalg.cholesky(second_curvature)  36 us
    dot_general x5, matrix products, combine(): jnp.einsum('yzir,rt->yzit', vector.astype(jnp.float32), coefficients, pre...  25 us
  transfers between devices with their start and end apart: 36, of which 15 were waited for; matrix products, arithmetic and copies ran while one was open for 43% of the time, Pallas kernels for 0%

profile of v1, /device:TPU:0, one launch (start us, length us, event | category | flops | bytes accessed | tf_op | source)
XLA Modules:
  0.0 605.0 jit_solution(118255005246383226)
XLA Ops:
  22.7 17.8 %collective-permute-done.11 = f32[128,256]{0,1:T(8,128)S(1)} collective-permute-done((f32[128,256]{0,1:T(8,128)S(1)}, f32[128,256]{0,1:T(8,128)S(1)}, u32[]{:S(2)}, u32[]{:S(2)}) %collective-permute-start.11) | collective-permute-done | bytes 131104 | tf_op jit(solution)/shard_map/ppermute | solution.py:17
  44.4 33.7 %collective-permute-done.12 = f32[128,256]{0,1:T(8,128)S(1)} collective-permute-done((f32[128,256]{0,1:T(8,128)S(1)}, f32[128,256]{0,1:T(8,128)S(1)}, u32[]{:S(2)}, u32[]{:S(2)}) %collective-permute-start.12) | collective-permute-done | bytes 131104 | tf_op jit(solution)/shard_map/ppermute | solution.py:13
  78.9 8.2 %collective-permute-done.13 = f32[128,256]{0,1:T(8,128)S(1)} collective-permute-done((f32[128,256]{0,1:T(8,128)S(1)}, f32[128,256]{0,1:T(8,128)S(1)}, u32[]{:S(2)}, u32[]{:S(2)}) %collective-permute-start.13) | collective-permute-done | bytes 131104 | tf_op jit(solution)/shard_map/ppermute | solution.py:13
  97.8 4.1 fusion.94
  101.8 4.0 fusion.96
  105.9 8.0 %fusion.6 = bf16[4,8,96,256]{3,2,1,0:T(8,128)(2,1)S(1)} fusion(f32[4,8,96,256]{3,2,1,0:T(8,128)} %fusion.96, f32[4,8,96,256]{3,2,1,0:T(8,128)S(1)} %copy-done.4, f32[4,8,96,256]{3,2,1,0:T(8,128)} %fusion.92, f32[4,8,96,256]{3,2,1,0:T(8,128)} %fusion.94, f32[4,8,256,96]{2,3,1,0:T(8,128)S(1)} %copy-done.5, f32[4,8,256,96]{2,3,1,0:T(8,128)S(1)} %copy-done.6, ...), kind=kOutput, calls=%fused_computation.18 | convolution fusion | flops 160432128 | bytes 30670848 | tf_op jit(solution)/shard_map/yzoi,yzir->yzor/dot_general | solution.py:48
  132.1 4.2 collective-permute-start.7
  140.4 4.5 collective-permute-done.7
  168.1 11.7 %cholesky.172 = f32[128,128]{1,0:T(8,128)S(1)} custom-call(f32[128,128]{1,0:T(8,128)S(1)} %cholesky.270), custom_call_target="Cholesky" | custom-call | tf_op jit(solution)/shard_map/jit(cholesky)/cholesky | solution.py:102
  181.9 11.3 %custom-call.17 = f32[1,128,128]{1,2,0:T(8,128)} custom-call(f32[1,128,128]{2,1,0:T(8,128)} %get-tuple-element.96), custom_call_target="InvertDiagBlocksLowerTriangular" | custom-call | tf_op jit(solution)/shard_map/jit(cholesky)/cholesky | solution.py:102
  196.0 13.2 %cholesky.189 = f32[128,128]{1,0:T(8,128)} custom-call(f32[128,128]{1,0:T(8,128)} %convolution_subtract_fusion.8), custom_call_target="Cholesky" | custom-call | tf_op jit(solution)/shard_map/jit(cholesky)/cholesky | solution.py:102
  214.3 5.3 while.6
  226.3 13.2 %cholesky.206 = f32[128,128]{1,0:T(8,128)} custom-call(f32[128,128]{1,0:T(8,128)} %cholesky.273), custom_call_target="Cholesky" | custom-call | tf_op jit(solution)/shard_map/jit(cholesky)/cholesky | solution.py:98
  242.5 11.3 %custom-call.19 = f32[1,128,128]{1,2,0:T(8,128)} custom-call(f32[1,128,128]{2,1,0:T(8,128)} %get-tuple-element.92), custom_call_target="InvertDiagBlocksLowerTriangular" | custom-call | tf_op jit(solution)/shard_map/jit(cholesky)/cholesky | solution.py:98
  257.2 13.2 %cholesky.223 = f32[128,128]{1,0:T(8,128)} custom-call(f32[128,128]{1,0:T(8,128)} %convolution_subtract_fusion.7), custom_call_target="Cholesky" | custom-call | tf_op jit(solution)/shard_map/jit(cholesky)/cholesky | solution.py:98
  276.3 7.1 %while.7 = (s32[]{:T(128)}, f32[256,256]{1,0:T(8,128)}, s32[2,2]{1,0:T(2,128)S(1)}, f32[2,128,128]{2,1,0:T(8,128)}, s32[]{:T(128)}) while((s32[]{:T(128)}, f32[256,256]{1,0:T(8,128)}, s32[2,2]{1,0:T(2,128)S(1)}, f32[2,128,128]{2,1,0:T(8,128)}, s32[]{:T(128)}) %tuple.84), condition=%wide.while_cond.clone, body=%wide.while_body.clone.sunk | while | flops 2 | bytes 132705 | solution.py:106
  283.3 21.3 %custom-call.18 = f32[2,128,128]{1,2,0:T(8,128)} custom-call(f32[2,128,128]{2,1,0:T(8,128)} %get-tuple-element.28), custom_call_target="InvertDiagBlocksLowerTriangular" | custom-call | tf_op jit(solution)/shard_map/jit(_cho_solve)/triangular_solve | solution.py:102
  304.6 21.1 %custom-call.20 = f32[2,128,128]{1,2,0:T(8,128)} custom-call(f32[2,128,128]{2,1,0:T(8,128)} %get-tuple-element.29), custom_call_target="InvertDiagBlocksLowerTriangular" | custom-call | tf_op jit(solution)/shard_map/jit(_cho_solve)/triangular_solve | solution.py:106
  333.1 8.6 %fusion.163 = (bf16[4,8,96,256]{3,2,1,0:T(8,128)(2,1)}, f32[4,8,96,256]{3,2,1,0:T(8,128)S(1)}) fusion(f32[128,256]{1,0:T(8,128)S(1)} %fusion.117, f32[128,256]{1,0:T(8,128)S(1)} %fusion.115, f32[4,8,256,96]{2,3,1,0:T(8,128)} %fusion.89, bf16[4,8,96,256]{3,2,1,0:T(8,128)(2,1)} %collective-permute-done.19, ...), kind=kOutput, calls=%fused_computation.286 | convolution fusion | flops 2436431872 | bytes 23855104 | tf_op jit(solution)/shard_map/yzir,rt->yzit/dot_general | solution.py:89
  354.8 5.2 convolution_bitcast_fusion.2
  371.0 17.5 %collective-permute-done.21 = f32[128,256]{0,1:T(8,128)S(1)} collective-permute-done((f32[128,256]{0,1:T(8,128)S(1)}, f32[128,256]{0,1:T(8,128)S(1)}, u32[]{:S(2)}, u32[]{:S(2)}) %collective-permute-start.21) | collective-permute-done | bytes 131104 | tf_op jit(solution)/shard_map/ppermute | solution.py:17
  397.7 4.4 collective-permute-done.23
  402.1 34.3 %collective-permute-start.29 = (bf16[4,8,96,256]{3,2,1,0:T(8,128)(2,1)}, bf16[4,8,96,256]{3,2,1,0:T(8,128)(2,1)}, u32[]{:S(2)}, u32[]{:S(2)}) collective-permute-start(bf16[4,8,96,256]{3,2,1,0:T(8,128)(2,1)} %get-tuple-element.99), channel_id=1, source_target_pairs={{0,1},{1,2},{2,3},{3,0},{4,5},{5,6},{6,7},{7,4},{8,9},{9,10},{10,1... | collective-permute-start | bytes 4718600 | tf_op jit(solution)/shard_map/ppermute | solution.py:13
  461.5 12.5 %collective-permute-done.29 = bf16[4,8,96,256]{3,2,1,0:T(8,128)(2,1)} collective-permute-done((bf16[4,8,96,256]{3,2,1,0:T(8,128)(2,1)}, bf16[4,8,96,256]{3,2,1,0:T(8,128)(2,1)}, u32[]{:S(2)}, u32[]{:S(2)}) %collective-permute-start.29) | collective-permute-done | bytes 1572896 | tf_op jit(solution)/shard_map/ppermute | solution.py:13
  474.0 21.3 %fusion.87 = f32[256,256]{0,1:T(8,128)S(1)} fusion(f32[4,8,96,256]{3,2,1,0:T(8,128)} %fusion.103, f32[4,8,256,96]{2,3,1,0:T(8,128)} %fusion.95, f32[4,8,256,96]{2,3,1,0:T(8,128)} %fusion.88, f32[4,8,256,96]{2,3,1,0:T(8,128)} %fusion.91, f32[4,8,256,96]{2,3,1,0:T(8,128)} %fusion.93, f32[4,8,256,96]{2,3,1,0:T(8,128)} %fusion.69, ...), kind=kOutput, calls=%fused_computation.117 | convolution fusion | flops 563871744 | bytes 32505856 | tf_op jit(solution)/shard_map/sr,st->rt/dot_general | solution.py:84
  510.8 4.0 collective-permute-done.33
  522.1 11.7 %cholesky.240 = f32[128,128]{1,0:T(8,128)S(1)} custom-call(f32[128,128]{1,0:T(8,128)S(1)} %cholesky.276), custom_call_target="Cholesky" | custom-call | tf_op jit(solution)/shard_map/jit(cholesky)/cholesky | solution.py:110
  534.6 10.4 %custom-call.21 = f32[1,128,128]{1,2,0:T(8,128)} custom-call(f32[1,128,128]{2,1,0:T(8,128)S(1)} %get-tuple-element.88), custom_call_target="InvertDiagBlocksLowerTriangular" | custom-call | tf_op jit(solution)/shard_map/jit(cholesky)/cholesky | solution.py:110
  547.8 11.9 %cholesky.257 = f32[128,128]{1,0:T(8,128)S(1)} custom-call(f32[128,128]{1,0:T(8,128)S(1)} %convolution_subtract_fusion.6), custom_call_target="Cholesky" | custom-call | tf_op jit(solution)/shard_map/jit(cholesky)/cholesky | solution.py:110
  564.6 5.8 while.8
  570.4 20.3 %custom-call.22 = f32[2,128,128]{1,2,0:T(8,128)} custom-call(f32[2,128,128]{2,1,0:T(8,128)S(1)} %get-tuple-element.30), custom_call_target="InvertDiagBlocksLowerTriangular" | custom-call | tf_op jit(solution)/shard_map/jit(_cho_solve)/triangular_solve | solution.py:110
  597.6 7.1 %fusion.20 = f32[4,1,1,8,96,256]{5,4,3,2,1,0:T(8,128)} fusion(f32[256,4,8,96]{0,3,2,1:T(8,128)} %fusion.105, f32[4,8,96,256]{3,2,1,0:T(8,128)S(1)} %copy-done.3, f32[256,4,8,96]{0,3,2,1:T(8,128)} %fusion.104, f32[128,256]{1,0:T(8,128)S(1)} %fusion.125, f32[128,256]{1,0:T(8,128)S(1)} %fusion.123), kind=kOutput, calls=%fused_computation.40 | convolution fusion | flops 2417557504 | bytes 12845056 | tf_op jit(solution)/shard_map/yzir,rt->yzit/dot_general | solution.py:89
  (272 shorter events, 230.0 us)
Async XLA Ops:
  0.0 93.7 %collective-permute-start = (bf16[4,8,96,256]{3,2,1,0:T(8,128)(2,1)}, bf16[4,8,96,256]{3,2,1,0:T(8,128)(2,1)}, u32[]{:S(2)}, u32[]{:S(2)}) collective-permute-start(bf16[4,8,96,256]{3,2,1,0:T(8,128)(2,1)} %bitcast.367), channel_id=1, source_target_pairs={{0,12},{4,0},{8,4},{12,8},{1,13},{5,1},{9,5},{13,9},{2,14},{6,2},{... | collective-permute-start | bytes 4718600 | tf_op jit(solution)/shard_map/ppermute | solution.py:13
  2.4 95.4 %collective-permute-start.1 = (bf16[4,8,96,256]{3,2,1,0:T(8,128)(2,1)}, bf16[4,8,96,256]{3,2,1,0:T(8,128)(2,1)}, u32[]{:S(2)}, u32[]{:S(2)}) collective-permute-start(bf16[4,8,96,256]{3,2,1,0:T(8,128)(2,1)} %bitcast.368), channel_id=1, source_target_pairs={{0,4},{4,8},{8,12},{12,0},{1,5},{5,9},{9,13},{13,1},{2,6},{6,10},{... | collective-permute-start | bytes 4718600 | tf_op jit(solution)/shard_map/ppermute | solution.py:13
  2.4 99.4 %collective-permute-start.2 = (bf16[4,8,96,256]{3,2,1,0:T(8,128)(2,1)}, bf16[4,8,96,256]{3,2,1,0:T(8,128)(2,1)}, u32[]{:S(2)}, u32[]{:S(2)}) collective-permute-start(bf16[4,8,96,256]{3,2,1,0:T(8,128)(2,1)} %bitcast.369), channel_id=1, source_target_pairs={{0,3},{1,0},{2,1},{3,2},{4,7},{5,4},{6,5},{7,6},{8,11},{9,8},{10,9... | collective-permute-start | bytes 4718600 | tf_op jit(solution)/shard_map/ppermute | solution.py:13
  6.0 99.8 %collective-permute-start.3 = (bf16[4,8,96,256]{3,2,1,0:T(8,128)(2,1)}, bf16[4,8,96,256]{3,2,1,0:T(8,128)(2,1)}, u32[]{:S(2)}, u32[]{:S(2)}) collective-permute-start(bf16[4,8,96,256]{3,2,1,0:T(8,128)(2,1)} %bitcast.370), channel_id=1, source_target_pairs={{0,1},{1,2},{2,3},{3,0},{4,5},{5,6},{6,7},{7,4},{8,9},{9,10},{10,1... | collective-permute-start | bytes 4718600 | tf_op jit(solution)/shard_map/ppermute | solution.py:13
  8.7 10.3 %collective-permute-start.10 = (f32[128,256]{0,1:T(8,128)S(1)}, f32[128,256]{0,1:T(8,128)S(1)}, u32[]{:S(2)}, u32[]{:S(2)}) collective-permute-start(f32[128,256]{0,1:T(8,128)S(1)} %slice_select_fusion.2), channel_id=1, source_target_pairs={{0,4},{4,0},{8,12},{12,8},{1,5},{5,1},{9,13},{13,9},{2,6},{6,2},{1... | collective-permute-start | bytes 393224 | tf_op jit(solution)/shard_map/ppermute | solution.py:17
  19.0 21.5 %collective-permute-start.11 = (f32[128,256]{0,1:T(8,128)S(1)}, f32[128,256]{0,1:T(8,128)S(1)}, u32[]{:S(2)}, u32[]{:S(2)}) collective-permute-start(f32[128,256]{0,1:T(8,128)S(1)} %select_add_fusion.2), channel_id=1, source_target_pairs={{0,8},{4,12},{8,0},{12,4},{1,9},{5,13},{9,1},{13,5},{2,10},{6,14},... | collective-permute-start | bytes 393224 | tf_op jit(solution)/shard_map/ppermute | solution.py:17
  40.5 37.7 %collective-permute-start.12 = (f32[128,256]{0,1:T(8,128)S(1)}, f32[128,256]{0,1:T(8,128)S(1)}, u32[]{:S(2)}, u32[]{:S(2)}) collective-permute-start(f32[128,256]{0,1:T(8,128)S(1)} %add.173), channel_id=1, source_target_pairs={{0,1},{1,2},{2,3},{3,0},{4,5},{5,6},{6,7},{7,4},{8,9},{9,10},{10,1... | collective-permute-start | bytes 393224 | tf_op jit(solution)/shard_map/ppermute | solution.py:13
  78.2 9.0 %collective-permute-start.13 = (f32[128,256]{0,1:T(8,128)S(1)}, f32[128,256]{0,1:T(8,128)S(1)}, u32[]{:S(2)}, u32[]{:S(2)}) collective-permute-start(f32[128,256]{0,1:T(8,128)S(1)} %add.173), channel_id=1, source_target_pairs={{0,2},{1,3},{2,0},{3,1},{4,6},{5,7},{6,4},{7,5},{8,10},{9,11},{10,... | collective-permute-start | bytes 393224 | tf_op jit(solution)/shard_map/ppermute | solution.py:13
  87.2 5.2 collective-permute-start.14
  126.1 6.0 collective-permute-start.5
  132.0 8.3 %collective-permute-start.6 = (f32[128,256]{0,1:T(8,128)S(1)}, f32[128,256]{0,1:T(8,128)S(1)}, u32[]{:S(2)}, u32[]{:S(2)}) collective-permute-start(f32[128,256]{0,1:T(8,128)S(1)} %add.170), channel_id=1, source_target_pairs={{0,1},{1,2},{2,3},{3,0},{4,5},{5,6},{6,7},{7,4},{8,9},{9,10},{10,1... | collective-permute-start | bytes 393224 | tf_op jit(solution)/shard_map/ppermute | solution.py:13
  132.1 12.7 %collective-permute-start.7 = (f32[128,256]{0,1:T(8,128)S(1)}, f32[128,256]{0,1:T(8,128)S(1)}, u32[]{:S(2)}, u32[]{:S(2)}) collective-permute-start(f32[128,256]{0,1:T(8,128)S(1)} %add.170), channel_id=1, source_target_pairs={{0,2},{1,3},{2,0},{3,1},{4,6},{5,7},{6,4},{7,5},{8,10},{9,11},{10,... | collective-permute-start | bytes 393224 | tf_op jit(solution)/shard_map/ppermute | solution.py:13
  136.3 8.5 %collective-permute-start.8 = (f32[128,256]{0,1:T(8,128)S(1)}, f32[128,256]{0,1:T(8,128)S(1)}, u32[]{:S(2)}, u32[]{:S(2)}) collective-permute-start(f32[128,256]{0,1:T(8,128)S(1)} %add.170), channel_id=1, source_target_pairs={{0,3},{1,0},{2,1},{3,2},{4,7},{5,4},{6,5},{7,6},{8,11},{9,8},{10,9... | collective-permute-start | bytes 393224 | tf_op jit(solution)/shard_map/ppermute | solution.py:13
  149.6 14.1 %collective-permute-start.9 = (f32[128,256]{0,1:T(8,128)S(1)}, f32[128,256]{0,1:T(8,128)S(1)}, u32[]{:S(2)}, u32[]{:S(2)}) collective-permute-start(f32[128,256]{0,1:T(8,128)S(1)} %get-tuple-element.31), channel_id=1, source_target_pairs={{0,4},{4,0},{8,12},{12,8},{1,5},{5,1},{9,13},{13,9},{2,6},{6,2},{1... | collective-permute-start | bytes 393224 | tf_op jit(solution)/shard_map/ppermute | solution.py:17
  157.7 175.3 %collective-permute-start.16 = (bf16[4,8,96,256]{3,2,1,0:T(8,128)(2,1)}, bf16[4,8,96,256]{3,2,1,0:T(8,128)(2,1)}, u32[]{:S(2)}, u32[]{:S(2)}) collective-permute-start(bf16[4,8,96,256]{3,2,1,0:T(8,128)(2,1)} %fusion.82), channel_id=1, source_target_pairs={{0,1},{1,2},{2,3},{3,0},{4,5},{5,6},{6,7},{7,4},{8,9},{9,10},{10,1... | collective-permute-start | bytes 4718600 | tf_op jit(solution)/shard_map/ppermute | solution.py:13
  161.0 172.1 %collective-permute-start.17 = (bf16[4,8,96,256]{3,2,1,0:T(8,128)(2,1)}, bf16[4,8,96,256]{3,2,1,0:T(8,128)(2,1)}, u32[]{:S(2)}, u32[]{:S(2)}) collective-permute-start(bf16[4,8,96,256]{3,2,1,0:T(8,128)(2,1)} %fusion.83), channel_id=1, source_target_pairs={{0,3},{1,0},{2,1},{3,2},{4,7},{5,4},{6,5},{7,6},{8,11},{9,8},{10,9... | collective-permute-start | bytes 4718600 | tf_op jit(solution)/shard_map/ppermute | solution.py:13
  161.5 171.5 %collective-permute-start.18 = (bf16[4,8,96,256]{3,2,1,0:T(8,128)(2,1)}, bf16[4,8,96,256]{3,2,1,0:T(8,128)(2,1)}, u32[]{:S(2)}, u32[]{:S(2)}) collective-permute-start(bf16[4,8,96,256]{3,2,1,0:T(8,128)(2,1)} %fusion.84), channel_id=1, source_target_pairs={{0,4},{4,8},{8,12},{12,0},{1,5},{5,9},{9,13},{13,1},{2,6},{6,10},{... | collective-permute-start | bytes 4718600 | tf_op jit(solution)/shard_map/ppermute | solution.py:13
  161.6 171.5 %collective-permute-start.19 = (bf16[4,8,96,256]{3,2,1,0:T(8,128)(2,1)}, bf16[4,8,96,256]{3,2,1,0:T(8,128)(2,1)}, u32[]{:S(2)}, u32[]{:S(2)}) collective-permute-start(bf16[4,8,96,256]{3,2,1,0:T(8,128)(2,1)} %fusion.85), channel_id=1, source_target_pairs={{0,12},{4,0},{8,4},{12,8},{1,13},{5,1},{9,5},{13,9},{2,14},{6,2},{... | collective-permute-start | bytes 4718600 | tf_op jit(solution)/shard_map/ppermute | solution.py:13
  163.7 55.9 %collective-permute-start.15 = (f32[128,256]{0,1:T(8,128)S(1)}, f32[128,256]{0,1:T(8,128)}, u32[]{:S(2)}, u32[]{:S(2)}) collective-permute-start(f32[128,256]{0,1:T(8,128)S(1)} %get-tuple-element.32), channel_id=1, source_target_pairs={{0,4},{4,0},{8,12},{12,8},{1,5},{5,1},{9,13},{13,9},{2,6},{6,2},{1... | collective-permute-start | bytes 393224 | tf_op jit(solution)/shard_map/ppermute | solution.py:17
  349.0 100.8 %collective-permute-start.26 = (bf16[4,8,96,256]{3,2,1,0:T(8,128)(2,1)}, bf16[4,8,96,256]{3,2,1,0:T(8,128)(2,1)}, u32[]{:S(2)}, u32[]{:S(2)}) collective-permute-start(bf16[4,8,96,256]{3,2,1,0:T(8,128)(2,1)} %get-tuple-element.99), channel_id=1, source_target_pairs={{0,12},{4,0},{8,4},{12,8},{1,13},{5,1},{9,5},{13,9},{2,14},{6,2},{... | collective-permute-start | bytes 4718600 | tf_op jit(solution)/shard_map/ppermute | solution.py:13
  350.7 103.1 %collective-permute-start.27 = (bf16[4,8,96,256]{3,2,1,0:T(8,128)(2,1)}, bf16[4,8,96,256]{3,2,1,0:T(8,128)(2,1)}, u32[]{:S(2)}, u32[]{:S(2)}) collective-permute-start(bf16[4,8,96,256]{3,2,1,0:T(8,128)(2,1)} %get-tuple-element.99), channel_id=1, source_target_pairs={{0,4},{4,8},{8,12},{12,0},{1,5},{5,9},{9,13},{13,1},{2,6},{6,10},{... | collective-permute-start | bytes 4718600 | tf_op jit(solution)/shard_map/ppermute | solution.py:13
  360.1 7.4 %collective-permute-start.20 = (f32[128,256]{0,1:T(8,128)S(1)}, f32[128,256]{0,1:T(8,128)S(1)}, u32[]{:S(2)}, u32[]{:S(2)}) collective-permute-start(f32[128,256]{0,1:T(8,128)S(1)} %slice_select_fusion.1), channel_id=1, source_target_pairs={{0,4},{4,0},{8,12},{12,8},{1,5},{5,1},{9,13},{13,9},{2,6},{6,2},{1... | collective-permute-start | bytes 393224 | tf_op jit(solution)/shard_map/ppermute | solution.py:17
  367.5 21.0 %collective-permute-start.21 = (f32[128,256]{0,1:T(8,128)S(1)}, f32[128,256]{0,1:T(8,128)S(1)}, u32[]{:S(2)}, u32[]{:S(2)}) collective-permute-start(f32[128,256]{0,1:T(8,128)S(1)} %select_add_fusion.1), channel_id=1, source_target_pairs={{0,8},{4,12},{8,0},{12,4},{1,9},{5,13},{9,1},{13,5},{2,10},{6,14},... | collective-permute-start | bytes 393224 | tf_op jit(solution)/shard_map/ppermute | solution.py:17
  388.5 8.3 %collective-permute-start.22 = (f32[128,256]{0,1:T(8,128)S(1)}, f32[128,256]{0,1:T(8,128)S(1)}, u32[]{:S(2)}, u32[]{:S(2)}) collective-permute-start(f32[128,256]{0,1:T(8,128)S(1)} %add.184), channel_id=1, source_target_pairs={{0,1},{1,2},{2,3},{3,0},{4,5},{5,6},{6,7},{7,4},{8,9},{9,10},{10,1... | collective-permute-start | bytes 393224 | tf_op jit(solution)/shard_map/ppermute | solution.py:13
  390.0 12.1 %collective-permute-start.23 = (f32[128,256]{0,1:T(8,128)S(1)}, f32[128,256]{0,1:T(8,128)S(1)}, u32[]{:S(2)}, u32[]{:S(2)}) collective-permute-start(f32[128,256]{0,1:T(8,128)S(1)} %add.184), channel_id=1, source_target_pairs={{0,2},{1,3},{2,0},{3,1},{4,6},{5,7},{6,4},{7,5},{8,10},{9,11},{10,... | collective-permute-start | bytes 393224 | tf_op jit(solution)/shard_map/ppermute | solution.py:13
  390.0 46.4 %collective-permute-start.24 = (f32[128,256]{0,1:T(8,128)S(1)}, f32[128,256]{0,1:T(8,128)S(1)}, u32[]{:S(2)}, u32[]{:S(2)}) collective-permute-start(f32[128,256]{0,1:T(8,128)S(1)} %add.184), channel_id=1, source_target_pairs={{0,3},{1,0},{2,1},{3,2},{4,7},{5,4},{6,5},{7,6},{8,11},{9,8},{10,9... | collective-permute-start | bytes 393224 | tf_op jit(solution)/shard_map/ppermute | solution.py:13
  396.8 60.9 %collective-permute-start.28 = (bf16[4,8,96,256]{3,2,1,0:T(8,128)(2,1)}, bf16[4,8,96,256]{3,2,1,0:T(8,128)(2,1)}, u32[]{:S(2)}, u32[]{:S(2)}) collective-permute-start(bf16[4,8,96,256]{3,2,1,0:T(8,128)(2,1)} %get-tuple-element.99), channel_id=1, source_target_pairs={{0,3},{1,0},{2,1},{3,2},{4,7},{5,4},{6,5},{7,6},{8,11},{9,8},{10,9... | collective-permute-start | bytes 4718600 | tf_op jit(solution)/shard_map/ppermute | solution.py:13
  402.1 71.9 %collective-permute-start.29 = (bf16[4,8,96,256]{3,2,1,0:T(8,128)(2,1)}, bf16[4,8,96,256]{3,2,1,0:T(8,128)(2,1)}, u32[]{:S(2)}, u32[]{:S(2)}) collective-permute-start(bf16[4,8,96,256]{3,2,1,0:T(8,128)(2,1)} %get-tuple-element.99), channel_id=1, source_target_pairs={{0,1},{1,2},{2,3},{3,0},{4,5},{5,6},{6,7},{7,4},{8,9},{9,10},{10,1... | collective-permute-start | bytes 4718600 | tf_op jit(solution)/shard_map/ppermute | solution.py:13
  496.8 5.6 collective-permute-start.31
  502.4 8.3 %collective-permute-start.32 = (f32[128,256]{0,1:T(8,128)S(1)}, f32[128,256]{0,1:T(8,128)S(1)}, u32[]{:S(2)}, u32[]{:S(2)}) collective-permute-start(f32[128,256]{0,1:T(8,128)S(1)} %add.200), channel_id=1, source_target_pairs={{0,1},{1,2},{2,3},{3,0},{4,5},{5,6},{6,7},{7,4},{8,9},{9,10},{10,1... | collective-permute-start | bytes 393224 | tf_op jit(solution)/shard_map/ppermute | solution.py:13
  502.5 12.3 %collective-permute-start.33 = (f32[128,256]{0,1:T(8,128)S(1)}, f32[128,256]{0,1:T(8,128)S(1)}, u32[]{:S(2)}, u32[]{:S(2)}) collective-permute-start(f32[128,256]{0,1:T(8,128)S(1)} %add.200), channel_id=1, source_target_pairs={{0,2},{1,3},{2,0},{3,1},{4,6},{5,7},{6,4},{7,5},{8,10},{9,11},{10,... | collective-permute-start | bytes 393224 | tf_op jit(solution)/shard_map/ppermute | solution.py:13
  504.8 10.0 %collective-permute-start.34 = (f32[128,256]{0,1:T(8,128)S(1)}, f32[128,256]{0,1:T(8,128)S(1)}, u32[]{:S(2)}, u32[]{:S(2)}) collective-permute-start(f32[128,256]{0,1:T(8,128)S(1)} %add.200), channel_id=1, source_target_pairs={{0,3},{1,0},{2,1},{3,2},{4,7},{5,4},{6,5},{7,6},{8,11},{9,8},{10,9... | collective-permute-start | bytes 393224 | tf_op jit(solution)/shard_map/ppermute | solution.py:13
  (36 other events, 547.5 us)

commit v2 on v1

v2 whole, which is shorter than its diff:
```python
import functools

import jax
import jax.numpy as jnp
from jax import lax
from jax.experimental import pallas as pl
from jax.experimental.pallas import tpu as pltpu
from jax.sharding import PartitionSpec as P

MASS = 2.0
PIVOTS = 8
HIGHEST = lax.Precision.HIGHEST
F32, BF16 = jnp.float32, jnp.bfloat16
VMEM_BYTES = 48 * 2**20


def shift(value, axis, step):
    count = lax.axis_size(axis)
    return lax.ppermute(value, axis, [(i, (i + step) % count) for i in range(count)])


def swap(value, axis, bit):
    return lax.ppermute(value, axis, [(i, i ^ bit) for i in range(lax.axis_size(axis))])


def turn(value, axis, size, step):
    count = lax.axis_size(axis)
    return lax.ppermute(
        value, axis, [(i, i - i % size + (i % size + step) % size) for i in range(count)]
    )


def run_length():
    count = lax.axis_size("ta")
    return 4 if count % 4 == 0 else 2 if count % 2 == 0 else 1


def is_power(count):
    return count & (count - 1) == 0


def sum_bands(bands):
    size = len(bands)
    part = bands[0]
    for step in range(1, size):
        part = part + turn(bands[step], "ta", size, step)
    times, planes = lax.axis_size("ta"), lax.axis_size("xy")
    if is_power(times):
        bit = size
        while bit < times:
            part = part + swap(part, "ta", bit)
            bit *= 2
    else:
        held = part
        for step in range(size, times, size):
            part = part + shift(held, "ta", step)
    if planes <= 4 or not is_power(planes):
        held = part
        for step in range(1, planes):
            part = part + shift(held, "xy", step)
    else:
        bit = 1
        while bit < planes:
            part = part + swap(part, "xy", bit)
            bit *= 2
    return [part] + [turn(part, "ta", size, step) for step in range(1, size)]


def call(kernel, out_shape, grid, in_specs, out_specs, flops, moved, scratch=()):
    return pl.pallas_call(
        kernel,
        out_shape=out_shape,
        grid=grid,
        in_specs=in_specs,
        out_specs=out_specs,
        scratch_shapes=scratch,
        compiler_params=pltpu.CompilerParams(vmem_limit_bytes=VMEM_BYTES),
        cost_estimate=pl.CostEstimate(flops=flops, bytes_accessed=moved, transcendentals=0),
    )


def dot(left, right):
    return jnp.dot(left, right, preferred_element_type=F32)


def dot_rows(left, right):
    return lax.dot_general(left, right, (((0,), (0,)), ((), ())), preferred_element_type=F32)


def dot_full(left, right):
    return jnp.dot(left, right, precision=HIGHEST, preferred_element_type=F32)


def split(value, pieces):
    parts = []
    for _ in range(pieces):
        part = value.astype(BF16)
        parts.append(part)
        value = value - part.astype(F32)
    return parts


def plane_spec(shape, step=0):
    count = shape[0]
    return pl.BlockSpec(
        (None,) + tuple(shape[1:]), lambda y: (lax.rem(y + (count + step) % count, count), 0, 0, 0)
    )


def link_spec(links, number, step=0):
    count = links.shape[1]
    return pl.BlockSpec(
        (None, None) + tuple(links.shape[2:]),
        lambda y: (number, lax.rem(y + (count + step) % count, count), 0, 0, 0),
    )


def matrix_spec(shape):
    return pl.BlockSpec(tuple(shape), lambda y: (0, 0))


def like(vector, dtype):
    return jax.ShapeDtypeStruct(vector.shape, dtype)


def work(vector, products):
    planes, depth, comp, rhs = vector.shape
    return 2 * products * planes * depth * comp * comp * rhs


def inner_forward_kernel(here, above, below, later, earlier, own, lt, le, ya, yb, za, zb, out):
    depth = here.shape[0]
    for z in range(depth):
        value = here[z]
        total = MASS * value.astype(F32) + dot(own[z], value)
        total += dot(ya[z], above[z]) + dot(yb[z], below[z])
        total += dot(za[z], here[(z + 1) % depth]) + dot(zb[z], here[(z - 1) % depth])
        total += dot(lt[z], later[z]) + dot(le[z], earlier[z])
        out[z] = total


def inner_forward(vector, later, earlier, links):
    spec = plane_spec(vector.shape)
    return call(
        inner_forward_kernel,
        like(vector, F32),
        (vector.shape[0],),
        [spec, plane_spec(vector.shape, 1), plane_spec(vector.shape, -1), spec, spec]
        + [link_spec(links, number) for number in (0, 1, 2, 5, 6, 7, 8)],
        spec,
        work(vector, 7),
        16 * vector.size,
    )(vector, vector, vector, later, earlier, *([links] * 7))


def first_image_kernel(partial, ahead, behind, la, lb, image, moved_a, moved_b):
    for z in range(partial.shape[0]):
        total = partial[z] + dot(la[z], ahead[z]) + dot(lb[z], behind[z])
        rounded = total.astype(BF16)
        image[z] = rounded
        moved_a[z] = dot_rows(la[z], rounded).astype(BF16)
        moved_b[z] = dot_rows(lb[z], rounded).astype(BF16)


def first_image(partial, ahead, behind, links):
    spec = plane_spec(partial.shape)
    return call(
        first_image_kernel,
        [like(partial, BF16)] * 3,
        (partial.shape[0],),
        [spec] * 3 + [link_spec(links, 3), link_spec(links, 4)],
        [spec] * 3,
        work(partial, 4),
        14 * partial.size,
    )(partial, ahead, behind, links, links)


def time_products_kernel(image, la, lb, moved_a, moved_b):
    for z in range(image.shape[0]):
        moved_a[z] = dot_rows(la[z], image[z]).astype(BF16)
        moved_b[z] = dot_rows(lb[z], image[z]).astype(BF16)


def time_products(image, links):
    spec = plane_spec(image.shape)
    return call(
        time_products_kernel,
        [like(image, BF16)] * 2,
        (image.shape[0],),
        [spec, link_spec(links, 1), link_spec(links, 2)],
        [spec] * 2,
        work(image, 2),
        8 * image.size,
    )(image, links, links)


def inner_adjoint_kernel(here, above, below, own, ya, yb, za, zb, out):
    depth = here.shape[0]
    for z in range(depth):
        value = here[z]
        front, back = (z + 1) % depth, (z - 1) % depth
        total = MASS * value.astype(F32) + dot_rows(own[z], value)
        total += dot_rows(ya[z], below[z]).astype(BF16).astype(F32)
        total += dot_rows(yb[z], above[z]).astype(BF16).astype(F32)
        total += dot_rows(za[back], here[back]).astype(BF16).astype(F32)
        total += dot_rows(zb[front], here[front]).astype(BF16).astype(F32)
        out[z] = total


def inner_adjoint(image, links):
    spec = plane_spec(image.shape)
    return call(
        inner_adjoint_kernel,
        like(image, F32),
        (image.shape[0],),
        [spec, plane_spec(image.shape, 1), plane_spec(image.shape, -1)]
        + [link_spec(links, 0), link_spec(links, 5, -1), link_spec(links, 6, 1)]
        + [link_spec(links, 7), link_spec(links, 8)],
        spec,
        work(image, 5),
        14 * image.size,
    )(image, image, image, *([links] * 5))


def residual_kernel(partial, ta, tb, xa, xb, source, alpha, residual, rounded):
    normal = partial[...]
    for term in (ta, tb, xa, xb):
        normal += term[...].astype(F32)
    rows = (normal.shape[0] * normal.shape[1], normal.shape[2])
    moved = dot_full(normal.reshape(rows), alpha[...]).reshape(normal.shape)
    value = source[...].astype(F32) - moved
    residual[...] = value
    rounded[...] = value.astype(BF16)


def next_residual(partial, terms, source, alpha):
    spec = plane_spec(partial.shape)
    return call(
        residual_kernel,
        [like(partial, F32), like(partial, BF16)],
        (partial.shape[0],),
        [spec] * 6 + [matrix_spec(alpha.shape)],
        [spec] * 2,
        12 * partial.size * alpha.shape[0],
        20 * partial.size,
    )(partial, *terms, source, alpha)


def mixed_kernel(vector, coefficients, added, out):
    value = vector[...]
    rows = value.reshape(value.shape[0] * value.shape[1], value.shape[2])
    total = sum(dot(rows, part) for part in split(coefficients[...], 3))
    total = total.reshape(value.shape)
    out[...] = total if added is None else added[...] + total


def mixed(vector, coefficients, added=None):
    spec = plane_spec(vector.shape)
    kernel = mixed_kernel
    operands = (vector, coefficients)
    if added is None:
        kernel = lambda vector, coefficients, out: mixed_kernel(vector, coefficients, None, out)
    else:
        operands += (added,)
    return call(
        kernel,
        like(vector, F32),
        (vector.shape[0],),
        [spec, matrix_spec(coefficients.shape)] + [spec] * (len(operands) - 2),
        spec,
        6 * vector.size * coefficients.shape[0],
        10 * vector.size,
    )(*operands)


def answer_kernel(vector, coefficients, added, out):
    value = vector[...]
    rows = value.reshape(value.shape[0] * value.shape[1], value.shape[2])
    out[...] = added[...] + dot_full(rows, coefficients[...]).reshape(value.shape)


def answer(vector, coefficients, added):
    spec = plane_spec(vector.shape)
    return call(
        answer_kernel,
        like(vector, F32),
        (vector.shape[0],),
        [spec, matrix_spec(coefficients.shape), spec],
        spec,
        12 * vector.size * coefficients.shape[0],
        12 * vector.size,
    )(vector, coefficients, added)


def add_gram(total, rows):
    if rows.dtype == BF16:
        total[...] += dot_rows(rows, rows)
        return
    high, low = split(rows, 2)
    total[...] += dot_rows(high, high) + dot_rows(high, low) + dot_rows(low, high)


def put_bands(place, total, bands):
    height = bands[0].shape[0]
    for step, band in enumerate(bands):
        first = lax.rem(place[0] + step, len(bands)) * height
        band[...] = total[pl.ds(pl.multiple_of(first, height), height), :]


def gram_kernel(place, vector, *rest):
    *bands, total = rest

    @pl.when(pl.program_id(0) == 0)
    def _():
        total[...] = jnp.zeros_like(total)

    value = vector[...]
    add_gram(total, value.reshape(value.shape[0] * value.shape[1], value.shape[2]))

    @pl.when(pl.program_id(0) == pl.num_programs(0) - 1)
    def _():
        put_bands(place, total, bands)


def second_image_kernel(place, partial, ahead, behind, la, lb, *rest):
    *bands, total = rest

    @pl.when(pl.program_id(0) == 0)
    def _():
        total[...] = jnp.zeros_like(total)

    pieces = []
    for z in range(partial.shape[0]):
        value = partial[z] + dot(la[z], ahead[z]) + dot(lb[z], behind[z])
        pieces.append(value.astype(BF16))
    add_gram(total, jnp.concatenate(pieces, axis=0))

    @pl.when(pl.program_id(0) == pl.num_programs(0) - 1)
    def _():
        put_bands(place, total, bands)


def band_outputs(size, rhs):
    shape = jax.ShapeDtypeStruct((rhs // size, rhs), F32)
    return [shape] * size, [matrix_spec(shape.shape)] * size


SCALAR = pl.BlockSpec(memory_space=pltpu.SMEM)


def gram(vector, place, size):
    rhs = vector.shape[-1]
    shapes, specs = band_outputs(size, rhs)
    passes = 1 if vector.dtype == BF16 else 3
    bands = call(
        gram_kernel,
        shapes,
        (vector.shape[0],),
        [SCALAR, plane_spec(vector.shape)],
        specs,
        2 * passes * vector.size * rhs,
        vector.size * vector.dtype.itemsize,
        [pltpu.VMEM((rhs, rhs), F32)],
    )(place, vector)
    return sum_bands(bands)


def second_gram(partial, ahead, behind, links, place, size):
    rhs = partial.shape[-1]
    shapes, specs = band_outputs(size, rhs)
    spec = plane_spec(partial.shape)
    bands = call(
        second_image_kernel,
        shapes,
        (partial.shape[0],),
        [SCALAR] + [spec] * 3 + [link_spec(links, 3), link_spec(links, 4)],
        specs,
        work(partial, 2) + 2 * partial.size * rhs,
        12 * partial.size,
        [pltpu.VMEM((rhs, rhs), F32)],
    )(place, partial, ahead, behind, links, links)
    return sum_bands(bands)


def inverse_block(tile):
    side = tile.shape[0]
    rows_of = [tile[8 * v : 8 * v + 8] for v in range(side // 8)]
    lane = lax.broadcasted_iota(jnp.int32, (8, side), 1)
    line = lax.broadcasted_iota(jnp.int32, (8, side), 0)
    for first in range(0, side, PIVOTS):
        keep = (lane < first) | (lane >= first + PIVOTS)
        home, top = first // 8, first % 8
        own, rows = [], []
        for k in range(PIVOTS):
            row = jnp.broadcast_to(rows_of[home][top + k : top + k + 1, :], (8, side))
            own.append(
                [
                    jnp.broadcast_to(row[:, first + m : first + m + 1], (8, side))
                    for m in range(PIVOTS)
                ]
            )
            rows.append(jnp.where(keep, row, jnp.where(lane == first + k, 1.0, 0.0)))
        columns = [
            [jnp.broadcast_to(part[:, first + k : first + k + 1], (8, side)) for k in range(PIVOTS)]
            for part in rows_of
        ]
        lower = [[None] * PIVOTS for _ in range(PIVOTS)]
        pivot = []
        for k in range(PIVOTS):
            pivot.append(1.0 / own[k][k])
            for i in range(k + 1, PIVOTS):
                lower[i][k] = own[i][k] * pivot[k]
                for m in range(k + 1, i + 1):
                    own[i][m] = own[i][m] - lower[i][k] * own[m][k]
        for k in range(PIVOTS):
            for i in range(k + 1, PIVOTS):
                rows[i] = rows[i] - lower[i][k] * rows[k]
        solved = [rows[k] * pivot[k] for k in range(PIVOTS)]
        for k in range(PIVOTS - 1, -1, -1):
            for i in range(k + 1, PIVOTS):
                solved[k] = solved[k] - lower[i][k] * solved[i]
        updated = []
        for v, part in enumerate(rows_of):
            value = jnp.where(keep, part, 0.0)
            for k in range(PIVOTS):
                value = value - columns[v][k] * solved[k]
            if v == home:
                for k in range(PIVOTS):
                    value = jnp.where(line == top + k, solved[k], value)
            updated.append(value)
        rows_of = updated
    return jnp.concatenate(rows_of, axis=0)


def solve_kernel(place, *refs, size):
    matrix_bands, side_bands = refs[:size], refs[size : 2 * size]
    out, matrix, side = refs[2 * size :]
    height = matrix_bands[0].shape[0]
    for bands, whole in ((matrix_bands, matrix), (side_bands, side)):
        for step, band in enumerate(bands):
            first = lax.rem(place[0] + (size - step) % size, size) * height
            whole[pl.ds(pl.multiple_of(first, height), height), :] = band[...]
    half = matrix.shape[0] // 2
    upper = inverse_block(matrix[:half, :half])
    across = dot_full(upper, matrix[:half, half:])
    start = dot_full(upper, side[:half, :])
    corner = matrix[half:, :half]
    lower = inverse_block(matrix[half:, half:] - dot_full(corner, across))
    bottom = dot_full(lower, side[half:, :] - dot_full(corner, start))
    out[half:, :] = bottom
    out[:half, :] = start - dot_full(across, bottom)


def solve(matrix_bands, side_bands, place):
    size = len(matrix_bands)
    rhs = matrix_bands[0].shape[1]
    vmem = pl.BlockSpec(memory_space=pltpu.VMEM)
    return pl.pallas_call(
        functools.partial(solve_kernel, size=size),
        out_shape=jax.ShapeDtypeStruct((rhs, rhs), F32),
        in_specs=[SCALAR] + [vmem] * (2 * size),
        out_specs=vmem,
        scratch_shapes=[pltpu.VMEM((rhs, rhs), F32)] * 2,
        compiler_params=pltpu.CompilerParams(vmem_limit_bytes=VMEM_BYTES),
        cost_estimate=pl.CostEstimate(
            flops=600 * rhs**3, bytes_accessed=12 * rhs * rhs, transcendentals=0
        ),
    )(place, *matrix_bands, *side_bands)


def halo(vector):
    return (
        shift(vector, "xy", -1),
        shift(vector, "xy", 1),
        shift(vector, "ta", -1),
        shift(vector, "ta", 1),
    )


def body(sources, coarse_links):
    shape = sources.shape
    assert shape[1] == shape[2] == 1
    source = sources.reshape(shape[0], shape[3], shape[4], shape[5])
    links = coarse_links.reshape(coarse_links.shape[:2] + coarse_links.shape[4:])
    size = run_length()
    place = lax.rem(lax.axis_index("ta"), size).astype(jnp.int32).reshape(1)

    ahead, behind, later, earlier = halo(source)
    energy = gram(source, place, size)
    partial = inner_forward(source, later, earlier, links)
    image, moved_a, moved_b = first_image(partial, ahead, behind, links)
    from_behind, from_ahead = shift(moved_a, "xy", 1), shift(moved_b, "xy", -1)
    time_a, time_b = time_products(image, links)
    from_earlier, from_later = shift(time_a, "ta", 1), shift(time_b, "ta", -1)
    curvature = gram(image, place, size)
    adjoint = inner_adjoint(image, links)
    alpha = solve(curvature, energy, place)
    residual, rounded = next_residual(
        adjoint, (from_earlier, from_later, from_behind, from_ahead), source, alpha
    )

    ahead, behind, later, earlier = halo(rounded)
    fresh = gram(residual, place, size)
    partial = inner_forward(rounded, later, earlier, links)
    beta = solve(energy, fresh, place)
    partial = mixed(image, beta, partial)
    curvature = second_gram(partial, ahead, behind, links, place, size)
    search = mixed(source, beta, residual)
    begun = mixed(source, alpha)
    second_alpha = solve(curvature, fresh, place)
    return answer(search, second_alpha, begun).reshape(shape)


def solution(mesh):
    return jax.shard_map(
        body,
        mesh=mesh,
        in_specs=(
            P("groups", "ta", "xy", None, None, None),
            P("groups", None, "ta", "xy", None, None, None),
        ),
        out_specs=P("groups", "ta", "xy", None, None, None),
        check_vma=False,
    )
```

time: 612 us -> 347 us (0.57)
  other arithmetic: 194 us -> 0.15 us
  matrix products: 159 us -> 0 us
  Pallas kernels: 0 us -> 94 us
  local copies, waits for them, and re-layouts: 56.1 us -> 9.5 us
  waiting for transfers between devices: 118 us -> 150 us
  starting transfers between devices: 73.5 us -> 87.7 us
    another operation x30 -> x0, other arithmetic: 185 us -> none  [the longest x6 41.3 us: body(): energy_factor = jnp.linalg.cholesky(energy)]
    dot_general x35 -> x0, matrix products: 134 us -> none  [the longest x17 61 us: forward(): jnp.einsum('yzoi,yzir->yzor', link, vector, preferred_element_type=jnp.fl...]
    pallas_call x0 -> x17, Pallas kernels: none -> 94 us  [the longest x3 35.2 us: solve(): pl.pallas_call(functools.partial(solve_kernel, size=size), out_shape=jax....]
    ppermute x24, waiting for transfers between devices: 74.8 us -> 100 us  [shift(): lax.ppermute(value, axis, [(i, (i + step) % count) for i in range(count)])]
    another operation x24 -> x0, matrix products: 25 us -> none  [the longest x6 7.24 us: body(): jax.scipy.linalg.cho_solve((jnp.linalg.cholesky(first_curvature), True),...]
    another operation x28 -> x0, local copies, waits for them, and re-layouts: 23.7 us -> none  [the longest x10 7.14 us: body(): jax.scipy.linalg.cho_solve((jnp.linalg.cholesky(first_curvature), True),...]
    ppermute x12 -> x24, starting transfers between devices: 8.04 us -> 24 us  [turn(): lax.ppermute(value, axis, [(i, i - i % size + (i % size + step) % size) f...]
    slice x19 -> x0, local copies, waits for them, and re-layouts: 14.5 us -> none  [the longest x4 5.23 us: apply_forward(): jnp.roll(vector, 1, 1)]
  transfers between devices with their start and end apart: 36 -> 48, of which waited for: 15 -> 22; matrix products, arithmetic and copies ran while one was open for 43% -> 0% of each run, Pallas kernels for 0% -> 18%
where the time goes in v2:
time: 347 us; the launch traced here: 342 us
  waiting for transfers between devices  150 us (43%)
  Pallas kernels  94 us (27%)
  starting transfers between devices  87.7 us (25%)
  local copies, waits for them, and re-layouts  9.5 us (3%)
    ppermute x24, waiting for transfers between devices, shift(): lax.ppermute(value, axis, [(i, (i + step) % count) for i in range(count)])  100 us
    ppermute x24, starting transfers between devices, shift(): lax.ppermute(value, axis, [(i, (i + step) % count) for i in range(count)])  63.7 us
    ppermute x24, waiting for transfers between devices, turn(): lax.ppermute(value, axis, [(i, i - i % size + (i % size + step) % size) f...  50 us
    pallas_call x3, Pallas kernels, solve(): pl.pallas_call(functools.partial(solve_kernel, size=size), out_shape=jax....  35.2 us
    ppermute x24, starting transfers between devices, turn(): lax.ppermute(value, axis, [(i, i - i % size + (i % size + step) % size) f...  24 us
    pallas_call x2, Pallas kernels, inner_forward(): call(inner_forward_kernel, like(vector, F32), (vector.shape[0],), [spec,...  13.4 us
    pallas_call x3, Pallas kernels, mixed(): call(kernel, like(vector, F32), (vector.shape[0],), [spec, matrix_spec(co...  9.52 us
    unnamed x16, local copies, waits for them, and re-layouts  9.5 us
  transfers between devices with their start and end apart: 48, of which 22 were waited for; matrix products, arithmetic and copies ran while one was open for 0% of the time, Pallas kernels for 18%

profile of v2, /device:TPU:0, one launch (start us, length us, event | category | flops | bytes accessed | tf_op | source)
XLA Modules:
  0.0 342.1 jit_solution(15133345598658705110)
XLA Ops:
  2.4 4.4 %collective-permute-start.11 = (bf16[4,8,96,256]{3,2,1,0:T(8,128)(2,1)}, bf16[4,8,96,256]{3,2,1,0:T(8,128)(2,1)}, u32[]{:S(2)}, u32[]{:S(2)}) collective-permute-start(bf16[4,8,96,256]{3,2,1,0:T(8,128)(2,1)} %bitcast.8), channel_id=1, source_target_pairs={{0,3},{1,0},{2,1},{3,2},{4,7},{5,4},{6,5},{7,6},{8,11},{9,8},{10,9... | collective-permute-start | bytes 4718600 | tf_op jit(solution)/shard_map/ppermute | solution.py:19
  9.7 26.6 %collective-permute-done = f32[64,256]{1,0:T(8,128)S(1)} collective-permute-done((f32[64,256]{1,0:T(8,128)S(1)}, f32[64,256]{1,0:T(8,128)S(1)}, u32[]{:S(2)}, u32[]{:S(2)}) %collective-permute-start) | collective-permute-done | bytes 65568 | tf_op jit(solution)/shard_map/ppermute | solution.py:28
  36.3 4.3 %collective-permute-start.1 = (f32[64,256]{1,0:T(8,128)S(1)}, f32[64,256]{1,0:T(8,128)S(1)}, u32[]{:S(2)}, u32[]{:S(2)}) collective-permute-start(f32[64,256]{1,0:T(8,128)S(1)} %get-tuple-element.30), channel_id=1, source_target_pairs={{0,8},{4,12},{8,0},{12,4},{1,9},{5,13},{9,1},{13,5},{2,10},{6,14},... | collective-permute-start | bytes 196616 | tf_op jit(solution)/shard_map/ppermute | solution.py:28
  40.6 2.2 collective-permute-done.1
  46.3 2.6 collective-permute-start.4
  50.2 6.7 %shard_map.29.partial = f32[4,8,96,256]{3,2,1,0:T(8,128)} custom-call(bf16[4,8,96,256]{3,2,1,0:T(8,128)(2,1)S(1)} %bitcast.12, bf16[4,8,96,256]{3,2,1,0:T(8,128)(2,1)S(1)} %bitcast.13, bf16[4,8,96,256]{3,2,1,0:T(8,128)(2,1)S(1)} %bitcast.14, bf16[4,8,96,256]{3,2,1,0:T(8,128)(2,1)S(1)} %collective-permute-done.9.later, ...), custom_call_target="tpu_custom_call" | custom-call | flops 1056964608 | bytes 12582912 | tf_op jit(solution)/shard_map/pallas_call | solution.py:144
  56.9 19.8 %collective-permute-done.12.behind = bf16[4,8,96,256]{3,2,1,0:T(8,128)(2,1)} collective-permute-done((bf16[4,8,96,256]{3,2,1,0:T(8,128)(2,1)}, bf16[4,8,96,256]{3,2,1,0:T(8,128)(2,1)}, u32[]{:S(2)}, u32[]{:S(2)}) %collective-permute-start.12) | collective-permute-done | bytes 1572896 | tf_op jit(solution)/shard_map/ppermute | solution.py:19
  76.7 5.3 %shard_map.30 = (bf16[4,8,96,256]{3,2,1,0:T(8,128)(2,1)S(1)}, bf16[4,8,96,256]{3,2,1,0:T(8,128)(2,1)S(1)}, bf16[4,8,96,256]{3,2,1,0:T(8,128)(2,1)S(1)}) custom-call(f32[4,8,96,256]{3,2,1,0:T(8,128)} %shard_map.29.partial, bf16[4,8,96,256]{3,2,1,0:T(8,128)(2,1)} %collective-permute-done.11.ahead, bf16[4,8,96,256]{3,2,1,0:T(8,128)(2,1)} %collective-permute-done.12.behind, ...), custom_call_target="tpu_custom_call" | custom-call | flops 603979776 | bytes 11010048 | tf_op jit(solution)/shard_map/pallas_call | solution.py:167
  90.5 3.3 shard_map.32
  96.2 3.5 %collective-permute-start.16 = (bf16[4,8,96,256]{3,2,1,0:T(8,128)(2,1)S(1)}, bf16[4,8,96,256]{3,2,1,0:T(8,128)(2,1)}, u32[]{:S(2)}, u32[]{:S(2)}) collective-permute-start(bf16[4,8,96,256]{3,2,1,0:T(8,128)(2,1)S(1)} %get-tuple-element.36), channel_id=1, source_target_pairs={{0,3},{1,0},{2,1},{3,2},{4,7},{5,4},{6,5},{7,6},{8,11},{9,8},{10,9... | collective-permute-start | bytes 4718600 | tf_op jit(solution)/shard_map/ppermute | solution.py:19
  99.7 69.0 %collective-permute-done.21 = f32[64,256]{1,0:T(8,128)S(1)} collective-permute-done((f32[64,256]{1,0:T(8,128)S(1)}, f32[64,256]{1,0:T(8,128)S(1)}, u32[]{:S(2)}, u32[]{:S(2)}) %collective-permute-start.21) | collective-permute-done | bytes 65568 | tf_op jit(solution)/shard_map/ppermute | solution.py:19
  169.9 3.1 collective-permute-done.22
  180.3 2.6 collective-permute-done.24.refs_2_
  183.1 4.8 %shard_map.31.partial = f32[4,8,96,256]{3,2,1,0:T(8,128)S(1)} custom-call(bf16[4,8,96,256]{3,2,1,0:T(8,128)(2,1)S(1)} %get-tuple-element.32.here.above.below.image.vector, bf16[4,8,96,256]{3,2,1,0:T(8,128)(2,1)S(1)} %get-tuple-element.32.here.above.below.image.vector, bf16[4,8,96,256]{3,2,1,0:T(8,128)(2,1)S(1)} %get-tuple-element.32.here.above.below.image.vector, ...), custom_call_target="tpu_custom_call" | custom-call | flops 754974720 | bytes 11010048 | tf_op jit(solution)/shard_map/pallas_call | solution.py:212
  189.6 11.7 %shard_map.34.alpha.coefficients = f32[256,256]{1,0:T(8,128)S(1)} custom-call(s32[1]{0:T(128)} %bitcast.1.place, f32[64,256]{1,0:T(8,128)S(1)} %add_add_fusion.4.refs_0_, f32[64,256]{1,0:T(8,128)S(1)} %collective-permute-done.23.refs_1_, f32[64,256]{1,0:T(8,128)S(1)} %collective-permute-done.24.refs_2_, f32[64,256]{1,0:T(8,128)S(1)} %collective-permute-done.25.refs_3_, ...), custom_call_target="tpu_custom_call" | custom-call | flops 10066329600 | bytes 786432 | tf_op jit(solution)/shard_map/pallas_call | solution.py:458
  202.5 7.1 %shard_map.35 = (f32[4,8,96,256]{3,2,1,0:T(8,128)}, bf16[4,8,96,256]{3,2,1,0:T(8,128)(2,1)S(1)}) custom-call(f32[4,8,96,256]{3,2,1,0:T(8,128)} %copy-done.5, bf16[4,8,96,256]{3,2,1,0:T(8,128)(2,1)S(1)} %collective-permute-done.13.ta, bf16[4,8,96,256]{3,2,1,0:T(8,128)(2,1)S(1)} %collective-permute-done.14.tb, bf16[4,8,96,256]{3,2,1,0:T(8,128)(2,1)} %copy-done.7, ...), custom_call_target="tpu_custom_call" | custom-call | flops 2415919104 | bytes 15728640 | tf_op jit(solution)/shard_map/pallas_call | solution.py:238
  211.5 2.2 shard_map.36
  219.1 3.3 collective-permute-start.30
  222.8 3.0 collective-permute-done.29
  228.2 33.1 %collective-permute-start.38 = (bf16[4,8,96,256]{3,2,1,0:T(8,128)(2,1)S(1)}, bf16[4,8,96,256]{3,2,1,0:T(8,128)(2,1)S(1)}, u32[]{:S(2)}, u32[]{:S(2)}) collective-permute-start(bf16[4,8,96,256]{3,2,1,0:T(8,128)(2,1)S(1)} %get-tuple-element.46.here.above.below), channel_id=1, source_target_pairs={{0,1},{1,2},{2,3},{3,0},{4,5},{5,6},{6,7},{7,4},{8,9},{9,10},{10,1... | collective-permute-start | bytes 4718600 | tf_op jit(solution)/shard_map/ppermute | solution.py:19
  261.3 3.7 %collective-permute-done.32.refs_5_ = f32[64,256]{1,0:T(8,128)S(1)} collective-permute-done((f32[64,256]{1,0:T(8,128)S(1)}, f32[64,256]{1,0:T(8,128)S(1)}, u32[]{:S(2)}, u32[]{:S(2)}) %collective-permute-start.32) | collective-permute-done | bytes 65568 | tf_op jit(solution)/shard_map/ppermute | solution.py:28
  266.9 2.4 collective-permute-done.33.refs_6_
  271.2 11.7 %shard_map.37.coefficients = f32[256,256]{1,0:T(8,128)S(1)} custom-call(s32[1]{0:T(128)} %bitcast.1.place, f32[64,256]{1,0:T(8,128)S(1)} %add_add_fusion.6.refs_4_.refs_0_, f32[64,256]{1,0:T(8,128)S(1)} %collective-permute-done.6.refs_5_.refs_1_, f32[64,256]{1,0:T(8,128)S(1)} %collective-permute-done.7.refs_6_.refs_2_, ...), custom_call_target="tpu_custom_call" | custom-call | flops 10066329600 | bytes 786432 | tf_op jit(solution)/shard_map/pallas_call | solution.py:458
  282.9 6.7 %shard_map.39.added = f32[4,8,96,256]{3,2,1,0:T(8,128)} custom-call(bf16[4,8,96,256]{3,2,1,0:T(8,128)(2,1)S(1)} %get-tuple-element.46.here.above.below, bf16[4,8,96,256]{3,2,1,0:T(8,128)(2,1)S(1)} %get-tuple-element.46.here.above.below, bf16[4,8,96,256]{3,2,1,0:T(8,128)(2,1)S(1)} %get-tuple-element.46.here.above.below, ...), custom_call_target="tpu_custom_call" | custom-call | flops 1056964608 | bytes 12582912 | tf_op jit(solution)/shard_map/pallas_call | solution.py:144
  289.7 3.8 %shard_map.40.partial = f32[4,8,96,256]{3,2,1,0:T(8,128)S(1)} custom-call(bf16[4,8,96,256]{3,2,1,0:T(8,128)(2,1)S(1)} %get-tuple-element.32.here.above.below.image.vector, f32[256,256]{1,0:T(8,128)S(1)} %shard_map.37.coefficients, f32[4,8,96,256]{3,2,1,0:T(8,128)} %shard_map.39.added), custom_call_target="tpu_custom_call" | custom-call | flops 1207959552 | bytes 7864320 | tf_op jit(solution)/shard_map/pallas_call | solution.py:265
  295.1 2.9 collective-permute-done.38.behind
  298.0 4.6 %shard_map.41 = (f32[64,256]{1,0:T(8,128)S(1)}, f32[64,256]{1,0:T(8,128)S(1)}, f32[64,256]{1,0:T(8,128)S(1)}, f32[64,256]{1,0:T(8,128)S(1)}) custom-call(s32[1]{0:T(128)} %bitcast.1.place, f32[4,8,96,256]{3,2,1,0:T(8,128)} %copy-done.4, bf16[4,8,96,256]{3,2,1,0:T(8,128)(2,1)S(1)} %collective-permute-done.37.ahead, ...), custom_call_target="tpu_custom_call" | custom-call | flops 704643072 | bytes 9437184 | tf_op jit(solution)/shard_map/pallas_call | solution.py:372
  302.7 2.6 collective-permute-start.40
  308.6 2.3 collective-permute-start.43
  320.5 3.8 %shard_map.38.vector = f32[4,8,96,256]{3,2,1,0:T(8,128)S(1)} custom-call(bf16[4,8,96,256]{3,2,1,0:T(8,128)(2,1)S(1)} %bitcast.16, f32[256,256]{1,0:T(8,128)S(1)} %shard_map.37.coefficients, f32[4,8,96,256]{3,2,1,0:T(8,128)} %get-tuple-element.41.vector.added), custom_call_target="tpu_custom_call" | custom-call | flops 1207959552 | bytes 7864320 | tf_op jit(solution)/shard_map/pallas_call | solution.py:265
  324.3 11.7 %shard_map.42.coefficients = f32[256,256]{1,0:T(8,128)S(1)} custom-call(s32[1]{0:T(128)} %bitcast.1.place, f32[64,256]{1,0:T(8,128)S(1)} %add_add_fusion.refs_0_, f32[64,256]{1,0:T(8,128)S(1)} %collective-permute-done.45.refs_1_, f32[64,256]{1,0:T(8,128)S(1)} %collective-permute-done.46.refs_2_, f32[64,256]{1,0:T(8,128)S(1)} %collective-permute-done.47.refs_3_, ...), custom_call_target="tpu_custom_call" | custom-call | flops 10066329600 | bytes 786432 | tf_op jit(solution)/shard_map/pallas_call | solution.py:458
  336.0 5.9 %shard_map.44 = f32[4,8,96,256]{3,2,1,0:T(8,128)} custom-call(f32[4,8,96,256]{3,2,1,0:T(8,128)S(1)} %shard_map.38.vector, f32[256,256]{1,0:T(8,128)S(1)} %shard_map.42.coefficients, f32[4,8,96,256]{3,2,1,0:T(8,128)} %copy-done.3), custom_call_target="tpu_custom_call" | custom-call | flops 2415919104 | bytes 9437184 | tf_op jit(solution)/shard_map/pallas_call | solution.py:284
  (105 shorter events, 60.8 us)
Async XLA Ops:
  0.0 46.3 %collective-permute-start.10 = (bf16[4,8,96,256]{3,2,1,0:T(8,128)(2,1)}, bf16[4,8,96,256]{3,2,1,0:T(8,128)(2,1)S(1)}, u32[]{:S(2)}, u32[]{:S(2)}) collective-permute-start(bf16[4,8,96,256]{3,2,1,0:T(8,128)(2,1)} %bitcast.6), channel_id=1, source_target_pairs={{0,4},{4,8},{8,12},{12,0},{1,5},{5,9},{9,13},{13,1},{2,6},{6,10},{... | collective-permute-start | bytes 4718600 | tf_op jit(solution)/shard_map/ppermute | solution.py:19
  0.5 48.4 %collective-permute-start.9 = (bf16[4,8,96,256]{3,2,1,0:T(8,128)(2,1)}, bf16[4,8,96,256]{3,2,1,0:T(8,128)(2,1)S(1)}, u32[]{:S(2)}, u32[]{:S(2)}) collective-permute-start(bf16[4,8,96,256]{3,2,1,0:T(8,128)(2,1)} %bitcast.7), channel_id=1, source_target_pairs={{0,12},{4,0},{8,4},{12,8},{1,13},{5,1},{9,5},{13,9},{2,14},{6,2},{... | collective-permute-start | bytes 4718600 | tf_op jit(solution)/shard_map/ppermute | solution.py:19
  2.4 54.5 %collective-permute-start.11 = (bf16[4,8,96,256]{3,2,1,0:T(8,128)(2,1)}, bf16[4,8,96,256]{3,2,1,0:T(8,128)(2,1)}, u32[]{:S(2)}, u32[]{:S(2)}) collective-permute-start(bf16[4,8,96,256]{3,2,1,0:T(8,128)(2,1)} %bitcast.8), channel_id=1, source_target_pairs={{0,3},{1,0},{2,1},{3,2},{4,7},{5,4},{6,5},{7,6},{8,11},{9,8},{10,9... | collective-permute-start | bytes 4718600 | tf_op jit(solution)/shard_map/ppermute | solution.py:19
  6.8 69.9 %collective-permute-start.12 = (bf16[4,8,96,256]{3,2,1,0:T(8,128)(2,1)}, bf16[4,8,96,256]{3,2,1,0:T(8,128)(2,1)}, u32[]{:S(2)}, u32[]{:S(2)}) collective-permute-start(bf16[4,8,96,256]{3,2,1,0:T(8,128)(2,1)} %bitcast.9), channel_id=1, source_target_pairs={{0,1},{1,2},{2,3},{3,0},{4,5},{5,6},{6,7},{7,4},{8,9},{9,10},{10,1... | collective-permute-start | bytes 4718600 | tf_op jit(solution)/shard_map/ppermute | solution.py:19
  9.6 26.7 %collective-permute-start = (f32[64,256]{1,0:T(8,128)S(1)}, f32[64,256]{1,0:T(8,128)S(1)}, u32[]{:S(2)}, u32[]{:S(2)}) collective-permute-start(f32[64,256]{1,0:T(8,128)S(1)} %get-tuple-element.29), channel_id=1, source_target_pairs={{0,4},{4,8},{8,12},{12,0},{1,5},{5,9},{9,13},{13,1},{2,6},{6,10},{... | collective-permute-start | bytes 196616 | tf_op jit(solution)/shard_map/ppermute | solution.py:28
  36.3 6.5 %collective-permute-start.1 = (f32[64,256]{1,0:T(8,128)S(1)}, f32[64,256]{1,0:T(8,128)S(1)}, u32[]{:S(2)}, u32[]{:S(2)}) collective-permute-start(f32[64,256]{1,0:T(8,128)S(1)} %get-tuple-element.30), channel_id=1, source_target_pairs={{0,8},{4,12},{8,0},{12,4},{1,9},{5,13},{9,1},{13,5},{2,10},{6,14},... | collective-permute-start | bytes 196616 | tf_op jit(solution)/shard_map/ppermute | solution.py:28
  44.7 40.2 %collective-permute-start.3 = (f32[64,256]{1,0:T(8,128)S(1)}, f32[64,256]{1,0:T(8,128)S(1)}, u32[]{:S(2)}, u32[]{:S(2)}) collective-permute-start(f32[64,256]{1,0:T(8,128)S(1)} %add_add_fusion.7), channel_id=1, source_target_pairs={{0,1},{1,2},{2,3},{3,0},{4,5},{5,6},{6,7},{7,4},{8,9},{9,10},{10,1... | collective-permute-start | bytes 196616 | tf_op jit(solution)/shard_map/ppermute | solution.py:19
  46.3 40.1 %collective-permute-start.4 = (f32[64,256]{1,0:T(8,128)S(1)}, f32[64,256]{1,0:T(8,128)S(1)}, u32[]{:S(2)}, u32[]{:S(2)}) collective-permute-start(f32[64,256]{1,0:T(8,128)S(1)} %add_add_fusion.7), channel_id=1, source_target_pairs={{0,2},{1,3},{2,0},{3,1},{4,6},{5,7},{6,4},{7,5},{8,10},{9,11},{10,... | collective-permute-start | bytes 196616 | tf_op jit(solution)/shard_map/ppermute | solution.py:19
  48.9 37.5 %collective-permute-start.5 = (f32[64,256]{1,0:T(8,128)S(1)}, f32[64,256]{1,0:T(8,128)S(1)}, u32[]{:S(2)}, u32[]{:S(2)}) collective-permute-start(f32[64,256]{1,0:T(8,128)S(1)} %add_add_fusion.7), channel_id=1, source_target_pairs={{0,3},{1,0},{2,1},{3,2},{4,7},{5,4},{6,5},{7,6},{8,11},{9,8},{10,9... | collective-permute-start | bytes 196616 | tf_op jit(solution)/shard_map/ppermute | solution.py:19
  86.4 9.5 %collective-permute-start.6 = (f32[64,256]{1,0:T(8,128)S(1)}, f32[64,256]{1,0:T(8,128)S(1)}, u32[]{:S(2)}, u32[]{:S(2)}) collective-permute-start(f32[64,256]{1,0:T(8,128)S(1)} %add_add_fusion.6.refs_4_.refs_0_), channel_id=1, source_target_pairs={{0,4},{4,8},{8,12},{12,0},{1,5},{5,9},{9,13},{13,1},{2,6},{6,10},{... | collective-permute-start | bytes 196616 | tf_op jit(solution)/shard_map/ppermute | solution.py:28
  86.5 9.7 %collective-permute-start.7 = (f32[64,256]{1,0:T(8,128)S(1)}, f32[64,256]{1,0:T(8,128)S(1)}, u32[]{:S(2)}, u32[]{:S(2)}) collective-permute-start(f32[64,256]{1,0:T(8,128)S(1)} %add_add_fusion.6.refs_4_.refs_0_), channel_id=1, source_target_pairs={{0,8},{4,12},{8,0},{12,4},{1,9},{5,13},{9,1},{13,5},{2,10},{6,14},... | collective-permute-start | bytes 196616 | tf_op jit(solution)/shard_map/ppermute | solution.py:28
  88.9 10.7 %collective-permute-start.20 = (f32[64,256]{1,0:T(8,128)S(1)}, f32[64,256]{1,0:T(8,128)S(1)}, u32[]{:S(2)}, u32[]{:S(2)}) collective-permute-start(f32[64,256]{1,0:T(8,128)S(1)} %add_add_fusion.5), channel_id=1, source_target_pairs={{0,1},{1,2},{2,3},{3,0},{4,5},{5,6},{6,7},{7,4},{8,9},{9,10},{10,1... | collective-permute-start | bytes 196616 | tf_op jit(solution)/shard_map/ppermute | solution.py:19
  93.8 107.5 %collective-permute-start.13 = (bf16[4,8,96,256]{3,2,1,0:T(8,128)(2,1)S(1)}, bf16[4,8,96,256]{3,2,1,0:T(8,128)(2,1)S(1)}, u32[]{:S(2)}, u32[]{:S(2)}) collective-permute-start(bf16[4,8,96,256]{3,2,1,0:T(8,128)(2,1)S(1)} %get-tuple-element.33), channel_id=1, source_target_pairs={{0,4},{4,8},{8,12},{12,0},{1,5},{5,9},{9,13},{13,1},{2,6},{6,10},{... | collective-permute-start | bytes 4718600 | tf_op jit(solution)/shard_map/ppermute | solution.py:19
  93.9 107.4 %collective-permute-start.14 = (bf16[4,8,96,256]{3,2,1,0:T(8,128)(2,1)S(1)}, bf16[4,8,96,256]{3,2,1,0:T(8,128)(2,1)S(1)}, u32[]{:S(2)}, u32[]{:S(2)}) collective-permute-start(bf16[4,8,96,256]{3,2,1,0:T(8,128)(2,1)S(1)} %get-tuple-element.34), channel_id=1, source_target_pairs={{0,12},{4,0},{8,4},{12,8},{1,13},{5,1},{9,5},{13,9},{2,14},{6,2},{... | collective-permute-start | bytes 4718600 | tf_op jit(solution)/shard_map/ppermute | solution.py:19
  95.9 105.5 %collective-permute-start.15 = (bf16[4,8,96,256]{3,2,1,0:T(8,128)(2,1)S(1)}, bf16[4,8,96,256]{3,2,1,0:T(8,128)(2,1)S(1)}, u32[]{:S(2)}, u32[]{:S(2)}) collective-permute-start(bf16[4,8,96,256]{3,2,1,0:T(8,128)(2,1)S(1)} %get-tuple-element.35), channel_id=1, source_target_pairs={{0,1},{1,2},{2,3},{3,0},{4,5},{5,6},{6,7},{7,4},{8,9},{9,10},{10,1... | collective-permute-start | bytes 4718600 | tf_op jit(solution)/shard_map/ppermute | solution.py:19
  96.2 105.2 %collective-permute-start.16 = (bf16[4,8,96,256]{3,2,1,0:T(8,128)(2,1)S(1)}, bf16[4,8,96,256]{3,2,1,0:T(8,128)(2,1)}, u32[]{:S(2)}, u32[]{:S(2)}) collective-permute-start(bf16[4,8,96,256]{3,2,1,0:T(8,128)(2,1)S(1)} %get-tuple-element.36), channel_id=1, source_target_pairs={{0,3},{1,0},{2,1},{3,2},{4,7},{5,4},{6,5},{7,6},{8,11},{9,8},{10,9... | collective-permute-start | bytes 4718600 | tf_op jit(solution)/shard_map/ppermute | solution.py:19
  99.7 69.0 %collective-permute-start.21 = (f32[64,256]{1,0:T(8,128)S(1)}, f32[64,256]{1,0:T(8,128)S(1)}, u32[]{:S(2)}, u32[]{:S(2)}) collective-permute-start(f32[64,256]{1,0:T(8,128)S(1)} %add_add_fusion.5), channel_id=1, source_target_pairs={{0,2},{1,3},{2,0},{3,1},{4,6},{5,7},{6,4},{7,5},{8,10},{9,11},{10,... | collective-permute-start | bytes 196616 | tf_op jit(solution)/shard_map/ppermute | solution.py:19
  182.9 6.7 %collective-permute-start.25 = (f32[64,256]{1,0:T(8,128)S(1)}, f32[64,256]{1,0:T(8,128)S(1)}, u32[]{:S(2)}, u32[]{:S(2)}) collective-permute-start(f32[64,256]{1,0:T(8,128)S(1)} %add_add_fusion.4.refs_0_), channel_id=1, source_target_pairs={{0,12},{4,0},{8,4},{12,8},{1,13},{5,1},{9,5},{13,9},{2,14},{6,2},{... | collective-permute-start | bytes 196616 | tf_op jit(solution)/shard_map/ppermute | solution.py:28
  216.9 66.0 %collective-permute-start.35 = (bf16[4,8,96,256]{3,2,1,0:T(8,128)(2,1)S(1)}, bf16[4,8,96,256]{3,2,1,0:T(8,128)(2,1)S(1)}, u32[]{:S(2)}, u32[]{:S(2)}) collective-permute-start(bf16[4,8,96,256]{3,2,1,0:T(8,128)(2,1)S(1)} %get-tuple-element.46.here.above.below), channel_id=1, source_target_pairs={{0,12},{4,0},{8,4},{12,8},{1,13},{5,1},{9,5},{13,9},{2,14},{6,2},{... | collective-permute-start | bytes 4718600 | tf_op jit(solution)/shard_map/ppermute | solution.py:19
  217.3 65.6 %collective-permute-start.36 = (bf16[4,8,96,256]{3,2,1,0:T(8,128)(2,1)S(1)}, bf16[4,8,96,256]{3,2,1,0:T(8,128)(2,1)S(1)}, u32[]{:S(2)}, u32[]{:S(2)}) collective-permute-start(bf16[4,8,96,256]{3,2,1,0:T(8,128)(2,1)S(1)} %get-tuple-element.46.here.above.below), channel_id=1, source_target_pairs={{0,4},{4,8},{8,12},{12,0},{1,5},{5,9},{9,13},{13,1},{2,6},{6,10},{... | collective-permute-start | bytes 4718600 | tf_op jit(solution)/shard_map/ppermute | solution.py:19
  219.0 6.9 %collective-permute-start.29 = (f32[64,256]{1,0:T(8,128)S(1)}, f32[64,256]{1,0:T(8,128)S(1)}, u32[]{:S(2)}, u32[]{:S(2)}) collective-permute-start(f32[64,256]{1,0:T(8,128)S(1)} %add_add_fusion.3), channel_id=1, source_target_pairs={{0,1},{1,2},{2,3},{3,0},{4,5},{5,6},{6,7},{7,4},{8,9},{9,10},{10,1... | collective-permute-start | bytes 196616 | tf_op jit(solution)/shard_map/ppermute | solution.py:19
  219.1 9.0 %collective-permute-start.30 = (f32[64,256]{1,0:T(8,128)S(1)}, f32[64,256]{1,0:T(8,128)S(1)}, u32[]{:S(2)}, u32[]{:S(2)}) collective-permute-start(f32[64,256]{1,0:T(8,128)S(1)} %add_add_fusion.3), channel_id=1, source_target_pairs={{0,2},{1,3},{2,0},{3,1},{4,6},{5,7},{6,4},{7,5},{8,10},{9,11},{10,... | collective-permute-start | bytes 196616 | tf_op jit(solution)/shard_map/ppermute | solution.py:19
  222.5 38.8 %collective-permute-start.31 = (f32[64,256]{1,0:T(8,128)S(1)}, f32[64,256]{1,0:T(8,128)S(1)}, u32[]{:S(2)}, u32[]{:S(2)}) collective-permute-start(f32[64,256]{1,0:T(8,128)S(1)} %add_add_fusion.3), channel_id=1, source_target_pairs={{0,3},{1,0},{2,1},{3,2},{4,7},{5,4},{6,5},{7,6},{8,11},{9,8},{10,9... | collective-permute-start | bytes 196616 | tf_op jit(solution)/shard_map/ppermute | solution.py:19
  225.9 69.3 %collective-permute-start.37 = (bf16[4,8,96,256]{3,2,1,0:T(8,128)(2,1)S(1)}, bf16[4,8,96,256]{3,2,1,0:T(8,128)(2,1)S(1)}, u32[]{:S(2)}, u32[]{:S(2)}) collective-permute-start(bf16[4,8,96,256]{3,2,1,0:T(8,128)(2,1)S(1)} %get-tuple-element.46.here.above.below), channel_id=1, source_target_pairs={{0,3},{1,0},{2,1},{3,2},{4,7},{5,4},{6,5},{7,6},{8,11},{9,8},{10,9... | collective-permute-start | bytes 4718600 | tf_op jit(solution)/shard_map/ppermute | solution.py:19
  228.2 69.9 %collective-permute-start.38 = (bf16[4,8,96,256]{3,2,1,0:T(8,128)(2,1)S(1)}, bf16[4,8,96,256]{3,2,1,0:T(8,128)(2,1)S(1)}, u32[]{:S(2)}, u32[]{:S(2)}) collective-permute-start(bf16[4,8,96,256]{3,2,1,0:T(8,128)(2,1)S(1)} %get-tuple-element.46.here.above.below), channel_id=1, source_target_pairs={{0,1},{1,2},{2,3},{3,0},{4,5},{5,6},{6,7},{7,4},{8,9},{9,10},{10,1... | collective-permute-start | bytes 4718600 | tf_op jit(solution)/shard_map/ppermute | solution.py:19
  302.7 5.0 %collective-permute-start.40 = (f32[64,256]{1,0:T(8,128)S(1)}, f32[64,256]{1,0:T(8,128)S(1)}, u32[]{:S(2)}, u32[]{:S(2)}) collective-permute-start(f32[64,256]{1,0:T(8,128)S(1)} %get-tuple-element.49), channel_id=1, source_target_pairs={{0,8},{4,12},{8,0},{12,4},{1,9},{5,13},{9,1},{13,5},{2,10},{6,14},... | collective-permute-start | bytes 196616 | tf_op jit(solution)/shard_map/ppermute | solution.py:28
  308.6 8.1 %collective-permute-start.42 = (f32[64,256]{1,0:T(8,128)S(1)}, f32[64,256]{1,0:T(8,128)S(1)}, u32[]{:S(2)}, u32[]{:S(2)}) collective-permute-start(f32[64,256]{1,0:T(8,128)S(1)} %add_add_fusion.1), channel_id=1, source_target_pairs={{0,1},{1,2},{2,3},{3,0},{4,5},{5,6},{6,7},{7,4},{8,9},{9,10},{10,1... | collective-permute-start | bytes 196616 | tf_op jit(solution)/shard_map/ppermute | solution.py:19
  308.6 8.7 %collective-permute-start.43 = (f32[64,256]{1,0:T(8,128)S(1)}, f32[64,256]{1,0:T(8,128)S(1)}, u32[]{:S(2)}, u32[]{:S(2)}) collective-permute-start(f32[64,256]{1,0:T(8,128)S(1)} %add_add_fusion.1), channel_id=1, source_target_pairs={{0,2},{1,3},{2,0},{3,1},{4,6},{5,7},{6,4},{7,5},{8,10},{9,11},{10,... | collective-permute-start | bytes 196616 | tf_op jit(solution)/shard_map/ppermute | solution.py:19
  310.9 6.4 %collective-permute-start.44 = (f32[64,256]{1,0:T(8,128)S(1)}, f32[64,256]{1,0:T(8,128)S(1)}, u32[]{:S(2)}, u32[]{:S(2)}) collective-permute-start(f32[64,256]{1,0:T(8,128)S(1)} %add_add_fusion.1), channel_id=1, source_target_pairs={{0,3},{1,0},{2,1},{3,2},{4,7},{5,4},{6,5},{7,6},{8,11},{9,8},{10,9... | collective-permute-start | bytes 196616 | tf_op jit(solution)/shard_map/ppermute | solution.py:19
  317.3 7.0 %collective-permute-start.45 = (f32[64,256]{1,0:T(8,128)S(1)}, f32[64,256]{1,0:T(8,128)S(1)}, u32[]{:S(2)}, u32[]{:S(2)}) collective-permute-start(f32[64,256]{1,0:T(8,128)S(1)} %add_add_fusion.refs_0_), channel_id=1, source_target_pairs={{0,4},{4,8},{8,12},{12,0},{1,5},{5,9},{9,13},{13,1},{2,6},{6,10},{... | collective-permute-start | bytes 196616 | tf_op jit(solution)/shard_map/ppermute | solution.py:28
  317.4 6.9 %collective-permute-start.46 = (f32[64,256]{1,0:T(8,128)S(1)}, f32[64,256]{1,0:T(8,128)S(1)}, u32[]{:S(2)}, u32[]{:S(2)}) collective-permute-start(f32[64,256]{1,0:T(8,128)S(1)} %add_add_fusion.refs_0_), channel_id=1, source_target_pairs={{0,8},{4,12},{8,0},{12,4},{1,9},{5,13},{9,1},{13,5},{2,10},{6,14},... | collective-permute-start | bytes 196616 | tf_op jit(solution)/shard_map/ppermute | solution.py:28
  319.1 5.2 %collective-permute-start.47 = (f32[64,256]{1,0:T(8,128)S(1)}, f32[64,256]{1,0:T(8,128)S(1)}, u32[]{:S(2)}, u32[]{:S(2)}) collective-permute-start(f32[64,256]{1,0:T(8,128)S(1)} %add_add_fusion.refs_0_), channel_id=1, source_target_pairs={{0,12},{4,0},{8,4},{12,8},{1,13},{5,1},{9,5},{13,9},{2,14},{6,2},{... | collective-permute-start | bytes 196616 | tf_op jit(solution)/shard_map/ppermute | solution.py:28
  (24 other events, 127.0 us)

commit v3 on v2

--- a/solution.py
+++ b/solution.py
@@ -11,7 +11,7 @@
 PIVOTS = 8
 HIGHEST = lax.Precision.HIGHEST
 F32, BF16 = jnp.float32, jnp.bfloat16
-VMEM_BYTES = 48 * 2**20
+VMEM_BYTES = 20 * 2**20
 
 
 def shift(value, axis, step):
@@ -39,11 +39,14 @@
     return count & (count - 1) == 0
 
 
-def sum_bands(bands):
-    size = len(bands)
+def first_stage(bands):
     part = bands[0]
-    for step in range(1, size):
-        part = part + turn(bands[step], "ta", size, step)
+    for step in range(1, len(bands)):
+        part = part + turn(bands[step], "ta", len(bands), step)
+    return part
+
+
+def second_stage(part, size):
     times, planes = lax.axis_size("ta"), lax.axis_size("xy")
     if is_power(times):
         bit = size
@@ -63,10 +66,19 @@
         while bit < planes:
             part = part + swap(part, "xy", bit)
             bit *= 2
+    return part
+
+
+def third_stage(part, size):
     return [part] + [turn(part, "ta", size, step) for step in range(1, size)]
 
 
-def call(kernel, out_shape, grid, in_specs, out_specs, flops, moved, scratch=()):
+def after(values, *earlier):
+    held = lax.optimization_barrier((tuple(values), tuple(earlier)))[0]
+    return held
+
+
+def call(kernel, out_shape, grid, in_specs, out_specs, scratch=()):
     return pl.pallas_call(
         kernel,
         out_shape=out_shape,
@@ -75,7 +87,7 @@
         out_specs=out_specs,
         scratch_shapes=scratch,
         compiler_params=pltpu.CompilerParams(vmem_limit_bytes=VMEM_BYTES),
-        cost_estimate=pl.CostEstimate(flops=flops, bytes_accessed=moved, transcendentals=0),
+        cost_estimate=pl.CostEstimate(flops=1, bytes_accessed=1, transcendentals=0),
     )
 
 
@@ -123,75 +135,103 @@
     return jax.ShapeDtypeStruct(vector.shape, dtype)
 
 
-def work(vector, products):
-    planes, depth, comp, rhs = vector.shape
-    return 2 * products * planes * depth * comp * comp * rhs
-
-
-def inner_forward_kernel(here, above, below, later, earlier, own, lt, le, ya, yb, za, zb, out):
+def inner_forward_kernel(here, above, below, own, ya, yb, za, zb, out):
     depth = here.shape[0]
     for z in range(depth):
         value = here[z]
         total = MASS * value.astype(F32) + dot(own[z], value)
         total += dot(ya[z], above[z]) + dot(yb[z], below[z])
         total += dot(za[z], here[(z + 1) % depth]) + dot(zb[z], here[(z - 1) % depth])
-        total += dot(lt[z], later[z]) + dot(le[z], earlier[z])
         out[z] = total
 
 
-def inner_forward(vector, later, earlier, links):
+def inner_forward(vector, links):
     spec = plane_spec(vector.shape)
     return call(
         inner_forward_kernel,
         like(vector, F32),
         (vector.shape[0],),
-        [spec, plane_spec(vector.shape, 1), plane_spec(vector.shape, -1), spec, spec]
-        + [link_spec(links, number) for number in (0, 1, 2, 5, 6, 7, 8)],
+        [spec, plane_spec(vector.shape, 1), plane_spec(vector.shape, -1)]
+        + [link_spec(links, number) for number in (0, 5, 6, 7, 8)],
         spec,
-        work(vector, 7),
-        16 * vector.size,
-    )(vector, vector, vector, later, earlier, *([links] * 7))
-
-
-def first_image_kernel(partial, ahead, behind, la, lb, image, moved_a, moved_b):
-    for z in range(partial.shape[0]):
-        total = partial[z] + dot(la[z], ahead[z]) + dot(lb[z], behind[z])
-        rounded = total.astype(BF16)
-        image[z] = rounded
-        moved_a[z] = dot_rows(la[z], rounded).astype(BF16)
-        moved_b[z] = dot_rows(lb[z], rounded).astype(BF16)
-
-
-def first_image(partial, ahead, behind, links):
+    )(vector, vector, vector, *([links] * 5))
+
+
+def time_terms_kernel(partial, later, earlier, la, lb, *rest):
+    out = rest[-1]
+    depth, comp, rhs = partial.shape
+    if len(rest) > 1:
+        image, beta = rest[:2]
+        rows = image[...].reshape(depth * comp, rhs)
+        extra = sum(dot(rows, part) for part in split(beta[...], 2)).reshape(partial.shape)
+    for z in range(depth):
+        total = partial[z] + dot(la[z], later[z]) + dot(lb[z], earlier[z])
+        out[z] = total + extra[z] if len(rest) > 1 else total
+
+
+def time_terms(partial, later, earlier, links, image=None, beta=None):
     spec = plane_spec(partial.shape)
-    return call(
+    specs = [spec] * 3 + [link_spec(links, 1), link_spec(links, 2)]
+    operands = [partial, later, earlier, links, links]
+    if image is not None:
+        specs += [spec, matrix_spec(beta.shape)]
+        operands += [image, beta]
+    return call(
+        time_terms_kernel, like(partial, F32), (partial.shape[0],), specs, spec
+    )(*operands)
+
+
+def packed(energy, curvature):
+    row = lax.broadcasted_iota(jnp.int32, energy.shape, 0)
+    column = lax.broadcasted_iota(jnp.int32, energy.shape, 1)
+    diagonal = jnp.sum(jnp.where(row == column, curvature, 0.0), axis=0, keepdims=True)
+    return jnp.where(row <= column, energy, curvature), diagonal
+
+
+def unpacked(pair, diagonal):
+    row = lax.broadcasted_iota(jnp.int32, pair.shape, 0)
+    column = lax.broadcasted_iota(jnp.int32, pair.shape, 1)
+    turned = pair.T
+    energy = jnp.where(row <= column, pair, turned)
+    curvature = jnp.where(row > column, pair, jnp.where(row == column, diagonal, turned))
+    return energy, curvature
+
+
+def first_image_kernel(place, partial, ahead, behind, energy, la, lb, lc, ld, image, *rest):
+    products, bands, total = rest[:4], rest[4:-1], rest[-1]
+    on_first(total)
+    depth, comp, rhs = partial.shape
+    for z in range(depth):
+        value = partial[z] + dot(la[z], ahead[z]) + dot(lb[z], behind[z])
+        image[z] = value.astype(BF16)
+    for link, product in zip((la, lb, lc, ld), products):
+        for z in range(depth):
+            product[z] = dot_rows(link[z], image[z]).astype(BF16)
+    add_planes(total, image)
+
+    @pl.when(pl.program_id(0) == pl.num_programs(0) - 1)
+    def _():
+        pair, diagonal = packed(energy[...], total[...])
+        total[...] = pair
+        height = rhs // len(bands)
+        put_bands(place, total, [band.at[pl.ds(0, height), :] for band in bands])
+        for band in bands:
+            band[pl.ds(height, 8), :] = jnp.broadcast_to(diagonal, (8, rhs))
+
+
+def first_image(partial, ahead, behind, energy, links, place, size):
+    spec, rhs = plane_spec(partial.shape), partial.shape[-1]
+    shapes, specs = band_outputs(size, rhs, 8)
+    outputs = call(
         first_image_kernel,
-        [like(partial, BF16)] * 3,
+        [like(partial, BF16)] * 5 + shapes,
         (partial.shape[0],),
-        [spec] * 3 + [link_spec(links, 3), link_spec(links, 4)],
-        [spec] * 3,
-        work(partial, 4),
-        14 * partial.size,
-    )(partial, ahead, behind, links, links)
-
-
-def time_products_kernel(image, la, lb, moved_a, moved_b):
-    for z in range(image.shape[0]):
-        moved_a[z] = dot_rows(la[z], image[z]).astype(BF16)
-        moved_b[z] = dot_rows(lb[z], image[z]).astype(BF16)
-
-
-def time_products(image, links):
-    spec = plane_spec(image.shape)
-    return call(
-        time_products_kernel,
-        [like(image, BF16)] * 2,
-        (image.shape[0],),
-        [spec, link_spec(links, 1), link_spec(links, 2)],
-        [spec] * 2,
-        work(image, 2),
-        8 * image.size,
-    )(image, links, links)
+        [SCALAR] + [spec] * 3 + [matrix_spec(energy.shape)]
+        + [link_spec(links, number) for number in (3, 4, 1, 2)],
+        [spec] * 5 + specs,
+        [pltpu.VMEM((rhs, rhs), F32)],
+    )(place, partial, ahead, behind, energy, *([links] * 4))
+    return outputs[0], outputs[1:5], outputs[5:]
 
 
 def inner_adjoint_kernel(here, above, below, own, ya, yb, za, zb, out):
@@ -217,12 +257,12 @@
         + [link_spec(links, 0), link_spec(links, 5, -1), link_spec(links, 6, 1)]
         + [link_spec(links, 7), link_spec(links, 8)],
         spec,
-        work(image, 5),
-        14 * image.size,
     )(image, image, image, *([links] * 5))
 
 
-def residual_kernel(partial, ta, tb, xa, xb, source, alpha, residual, rounded):
+def residual_kernel(place, partial, ta, tb, xa, xb, source, alpha, residual, rounded, *rest):
+    *bands, total = rest
+    on_first(total)
     normal = partial[...]
     for term in (ta, tb, xa, xb):
         normal += term[...].astype(F32)
@@ -231,19 +271,22 @@
     value = source[...].astype(F32) - moved
     residual[...] = value
     rounded[...] = value.astype(BF16)
-
-
-def next_residual(partial, terms, source, alpha):
-    spec = plane_spec(partial.shape)
-    return call(
+    add_planes(total, residual)
+    on_last(place, total, bands)
+
+
+def next_residual(partial, terms, source, alpha, place, size):
+    spec, rhs = plane_spec(partial.shape), partial.shape[-1]
+    shapes, specs = band_outputs(size, rhs)
+    outputs = call(
         residual_kernel,
-        [like(partial, F32), like(partial, BF16)],
+        [like(partial, F32), like(partial, BF16)] + shapes,
         (partial.shape[0],),
-        [spec] * 6 + [matrix_spec(alpha.shape)],
-        [spec] * 2,
-        12 * partial.size * alpha.shape[0],
-        20 * partial.size,
-    )(partial, *terms, source, alpha)
+        [SCALAR] + [spec] * 6 + [matrix_spec(alpha.shape)],
+        [spec] * 2 + specs,
+        [pltpu.VMEM((rhs, rhs), F32)],
+    )(place, partial, *terms, source, alpha)
+    return outputs[0], outputs[1], outputs[2:]
 
 
 def mixed_kernel(vector, coefficients, added, out):
@@ -268,8 +311,6 @@
         (vector.shape[0],),
         [spec, matrix_spec(coefficients.shape)] + [spec] * (len(operands) - 2),
         spec,
-        6 * vector.size * coefficients.shape[0],
-        10 * vector.size,
     )(*operands)
 
 
@@ -287,8 +328,6 @@
         (vector.shape[0],),
         [spec, matrix_spec(coefficients.shape), spec],
         spec,
-        12 * vector.size * coefficients.shape[0],
-        12 * vector.size,
     )(vector, coefficients, added)
 
 
@@ -307,79 +346,74 @@
         band[...] = total[pl.ds(pl.multiple_of(first, height), height), :]
 
 
-def gram_kernel(place, vector, *rest):
-    *bands, total = rest
-
+def on_first(total):
     @pl.when(pl.program_id(0) == 0)
     def _():
         total[...] = jnp.zeros_like(total)
 
-    value = vector[...]
-    add_gram(total, value.reshape(value.shape[0] * value.shape[1], value.shape[2]))
-
+
+def on_last(place, total, bands):
     @pl.when(pl.program_id(0) == pl.num_programs(0) - 1)
     def _():
         put_bands(place, total, bands)
 
 
-def second_image_kernel(place, partial, ahead, behind, la, lb, *rest):
-    *bands, total = rest
-
-    @pl.when(pl.program_id(0) == 0)
-    def _():
-        total[...] = jnp.zeros_like(total)
-
+def add_planes(total, vector):
+    value = vector[...]
+    add_gram(total, value.reshape(value.shape[0] * value.shape[1], value.shape[2]))
+
+
+def gram_kernel(vector, total):
+    on_first(total)
+    add_planes(total, vector)
+
+
+def gram(vector):
+    rhs = vector.shape[-1]
+    return call(
+        gram_kernel,
+        jax.ShapeDtypeStruct((rhs, rhs), F32),
+        (vector.shape[0],),
+        [plane_spec(vector.shape)],
+        matrix_spec((rhs, rhs)),
+    )(vector)
+
+
+def second_image(partial, ahead, behind, la, lb):
     pieces = []
     for z in range(partial.shape[0]):
         value = partial[z] + dot(la[z], ahead[z]) + dot(lb[z], behind[z])
         pieces.append(value.astype(BF16))
-    add_gram(total, jnp.concatenate(pieces, axis=0))
-
-    @pl.when(pl.program_id(0) == pl.num_programs(0) - 1)
-    def _():
-        put_bands(place, total, bands)
-
-
-def band_outputs(size, rhs):
-    shape = jax.ShapeDtypeStruct((rhs // size, rhs), F32)
+    return jnp.concatenate(pieces, axis=0)
+
+
+def second_gram_kernel(place, partial, ahead, behind, la, lb, *rest):
+    *bands, total = rest
+    on_first(total)
+    add_gram(total, second_image(partial, ahead, behind, la, lb))
+    on_last(place, total, bands)
+
+
+def band_outputs(size, rhs, extra=0):
+    shape = jax.ShapeDtypeStruct((rhs // size + extra, rhs), F32)
     return [shape] * size, [matrix_spec(shape.shape)] * size
 
 
 SCALAR = pl.BlockSpec(memory_space=pltpu.SMEM)
-
-
-def gram(vector, place, size):
-    rhs = vector.shape[-1]
-    shapes, specs = band_outputs(size, rhs)
-    passes = 1 if vector.dtype == BF16 else 3
-    bands = call(
-        gram_kernel,
-        shapes,
-        (vector.shape[0],),
-        [SCALAR, plane_spec(vector.shape)],
-        specs,
-        2 * passes * vector.size * rhs,
-        vector.size * vector.dtype.itemsize,
-        [pltpu.VMEM((rhs, rhs), F32)],
-    )(place, vector)
-    return sum_bands(bands)
 
 
 def second_gram(partial, ahead, behind, links, place, size):
     rhs = partial.shape[-1]
-    shapes, specs = band_outputs(size, rhs)
     spec = plane_spec(partial.shape)
-    bands = call(
-        second_image_kernel,
+    shapes, out_specs = band_outputs(size, rhs)
+    return call(
+        second_gram_kernel,
         shapes,
         (partial.shape[0],),
         [SCALAR] + [spec] * 3 + [link_spec(links, 3), link_spec(links, 4)],
-        specs,
-        work(partial, 2) + 2 * partial.size * rhs,
-        12 * partial.size,
+        out_specs,
         [pltpu.VMEM((rhs, rhs), F32)],
     )(place, partial, ahead, behind, links, links)
-    return sum_bands(bands)
 
 
 def inverse_block(tile):
@@ -432,14 +466,15 @@
     return jnp.concatenate(rows_of, axis=0)
 
 
-def solve_kernel(place, *refs, size):
-    matrix_bands, side_bands = refs[:size], refs[size : 2 * size]
-    out, matrix, side = refs[2 * size :]
-    height = matrix_bands[0].shape[0]
-    for bands, whole in ((matrix_bands, matrix), (side_bands, side)):
-        for step, band in enumerate(bands):
-            first = lax.rem(place[0] + (size - step) % size, size) * height
-            whole[pl.ds(pl.multiple_of(first, height), height), :] = band[...]
+def assemble(place, bands, whole):
+    size = len(bands)
+    height = whole.shape[0] // size
+    for step, band in enumerate(bands):
+        first = lax.rem(place[0] + (size - step) % size, size) * height
+        whole[pl.ds(pl.multiple_of(first, height), height), :] = band[:height, :]
+
+
+def solve_into(out, matrix, side):
     half = matrix.shape[0] // 2
     upper = inverse_block(matrix[:half, :half])
     across = dot_full(upper, matrix[:half, half:])
@@ -451,30 +486,44 @@
     out[:half, :] = start - dot_full(across, bottom)
 
 
-def solve(matrix_bands, side_bands, place):
-    size = len(matrix_bands)
-    rhs = matrix_bands[0].shape[1]
+def solve_both_kernel(place, *refs, size):
+    bands = refs[:size]
+    out, side, matrix = refs[size:]
+    assemble(place, bands, side)
+    height = side.shape[0] // size
+    energy, curvature = unpacked(side[...], bands[0][height : height + 1, :])
+    side[...] = energy
+    matrix[...] = curvature
+    solve_into(out, matrix, side)
+
+
+def solve_side_kernel(place, matrix, *refs, size):
+    out, side = refs[size:]
+    assemble(place, refs[:size], side)
+    solve_into(out, matrix, side)
+
+
+def solve_matrix_kernel(place, side, *refs, size):
+    out, matrix = refs[size:]
+    assemble(place, refs[:size], matrix)
+    solve_into(out, matrix, side)
+
+
+def solve_call(kernel, outputs, scratch, place, operands, bands):
+    rhs = bands[0].shape[1]
     vmem = pl.BlockSpec(memory_space=pltpu.VMEM)
+    square = jax.ShapeDtypeStruct((rhs, rhs), F32)
     return pl.pallas_call(
-        functools.partial(solve_kernel, size=size),
-        out_shape=jax.ShapeDtypeStruct((rhs, rhs), F32),
-        in_specs=[SCALAR] + [vmem] * (2 * size),
-        out_specs=vmem,
-        scratch_shapes=[pltpu.VMEM((rhs, rhs), F32)] * 2,
+        functools.partial(kernel, size=len(bands)),
+        out_shape=[square] * outputs,
+        in_specs=[SCALAR] + [vmem] * (len(operands) + len(bands)),
+        out_specs=[vmem] * outputs,
+        scratch_shapes=[pltpu.VMEM((rhs, rhs), F32)] * scratch,
         compiler_params=pltpu.CompilerParams(vmem_limit_bytes=VMEM_BYTES),
         cost_estimate=pl.CostEstimate(
-            flops=600 * rhs**3, bytes_accessed=12 * rhs * rhs, transcendentals=0
+            flops=1, bytes_accessed=1, transcendentals=0
         ),
-    )(place, *matrix_bands, *side_bands)
-
-
-def halo(vector):
-    return (
-        shift(vector, "xy", -1),
-        shift(vector, "xy", 1),
-        shift(vector, "ta", -1),
-        shift(vector, "ta", 1),
-    )
+    )(place, *operands, *bands)
 
 
 def body(sources, coarse_links):
@@ -485,29 +534,44 @@
     size = run_length()
     place = lax.rem(lax.axis_index("ta"), size).astype(jnp.int32).reshape(1)
 
-    ahead, behind, later, earlier = halo(source)
-    energy = gram(source, place, size)
-    partial = inner_forward(source, later, earlier, links)
-    image, moved_a, moved_b = first_image(partial, ahead, behind, links)
-    from_behind, from_ahead = shift(moved_a, "xy", 1), shift(moved_b, "xy", -1)
-    time_a, time_b = time_products(image, links)
-    from_earlier, from_later = shift(time_a, "ta", 1), shift(time_b, "ta", -1)
-    curvature = gram(image, place, size)
-    adjoint = inner_adjoint(image, links)
-    alpha = solve(curvature, energy, place)
-    residual, rounded = next_residual(
-        adjoint, (from_earlier, from_later, from_behind, from_ahead), source, alpha
-    )
-
-    ahead, behind, later, earlier = halo(rounded)
-    fresh = gram(residual, place, size)
-    partial = inner_forward(rounded, later, earlier, links)
-    beta = solve(energy, fresh, place)
-    partial = mixed(image, beta, partial)
-    curvature = second_gram(partial, ahead, behind, links, place, size)
+    ahead, behind = shift(source, "xy", -1), shift(source, "xy", 1)
+    later, earlier = shift(source, "ta", -1), shift(source, "ta", 1)
+    energy = gram(source)
+    partial = time_terms(inner_forward(source, links), later, earlier, links)
+    image, products, bands = first_image(partial, ahead, behind, energy, links, place, size)
+    to_ahead, to_behind, to_later, to_earlier = products
+
+    part = first_stage(bands)
+    from_behind, from_earlier = shift(to_ahead, "xy", 1), shift(to_later, "ta", 1)
+    part, still_image = after((part, image), part)
+    adjoint = inner_adjoint(still_image, links)
+    (part,) = after((part,), from_behind, from_earlier, adjoint)
+    part = second_stage(part, size)
+    from_ahead = shift(*after((to_behind,), part), "xy", -1)
+    bands = third_stage(part, size)
+    from_later = shift(*after((to_earlier,), *bands), "ta", -1)
+    alpha, energy = solve_call(solve_both_kernel, 2, 1, place, (), bands)
+    terms = from_earlier, from_later, from_behind, from_ahead
+    residual, rounded, bands = next_residual(adjoint, terms, source, alpha, place, size)
+
+    part = first_stage(bands)
+    ahead, later = shift(rounded, "xy", -1), shift(rounded, "ta", -1)
+    part, still_rounded, still_source = after((part, rounded, source), part)
+    partial = inner_forward(still_rounded, links)
+    begun = mixed(still_source, alpha)
+    (part,) = after((part,), ahead, later, partial, begun)
+    part = second_stage(part, size)
+    behind = shift(*after((rounded,), part), "xy", 1)
+    bands = third_stage(part, size)
+    earlier = shift(*after((rounded,), *bands), "ta", 1)
+    beta, fresh = solve_call(solve_side_kernel, 2, 0, place, (energy,), bands)
+
+    partial = time_terms(partial, later, earlier, links, image, beta)
     search = mixed(source, beta, residual)
-    begun = mixed(source, alpha)
-    second_alpha = solve(curvature, fresh, place)
+    ahead, behind = after((ahead, behind), search, begun)
+    bands = second_gram(partial, ahead, behind, links, place, size)
+    bands = third_stage(second_stage(first_stage(bands), size), size)
+    (second_alpha,) = solve_call(solve_matrix_kernel, 1, 1, place, (fresh,), bands)
     return answer(search, second_alpha, begun).reshape(shape)
 
 

time: 347 us -> 303 us (0.87)
  starting transfers between devices: 87.7 us -> 33.7 us
  waiting for transfers between devices: 150 us -> 183 us
  Pallas kernels: 94 us -> 73.9 us
    ppermute x24 -> x21, starting transfers between devices: 63.7 us -> 22.9 us  [shift(): lax.ppermute(value, axis, [(i, (i + step) % count) for i in range(count)])]
    ppermute x24 -> x21, waiting for transfers between devices: 100 us -> 132 us  [shift(): lax.ppermute(value, axis, [(i, (i + step) % count) for i in range(count)])]
    ppermute x24 -> x18, starting transfers between devices: 24 us -> 10.8 us  [turn(): lax.ppermute(value, axis, [(i, i - i % size + (i % size + step) % size) f...]
    pallas_call x2, Pallas kernels: 13.4 us -> 5.48 us  [inner_forward(): call(inner_forward_kernel, like(vector, F32), (vector.shape[0],), [spec,...]
    pallas_call x3 -> x2, Pallas kernels: 9.52 us -> 3.89 us  [mixed(): call(kernel, like(vector, F32), (vector.shape[0],), [spec, matrix_spec(co...]
    pallas_call x10 -> x9, Pallas kernels: 60.3 us -> 57.5 us  [the longest x3 35.3 us: solve_call(): pl.pallas_call(functools.partial(kernel, size=len(bands)), out_shape=[squ...]
    unnamed x16 -> x12, local copies, waits for them, and re-layouts: 9.5 us -> 7.52 us
    ppermute x24 -> x18, waiting for transfers between devices: 50 us -> 50.4 us  [turn(): lax.ppermute(value, axis, [(i, i - i % size + (i % size + step) % size) f...]
  transfers between devices with their start and end apart: 48 -> 39, of which waited for: 22 -> 28; matrix products, arithmetic and copies ran while one was open for 0% -> 0% of each run, Pallas kernels for 18% -> 14%
where the time goes in v3:
time: 303 us; the launch traced here: 299 us
  waiting for transfers between devices  183 us (60%)
  Pallas kernels  73.9 us (24%)
  starting transfers between devices  33.7 us (11%)
  local copies, waits for them, and re-layouts  7.52 us (2%)
    ppermute x21, waiting for transfers between devices, shift(): lax.ppermute(value, axis, [(i, (i + step) % count) for i in range(count)])  132 us
    ppermute x18, waiting for transfers between devices, turn(): lax.ppermute(value, axis, [(i, i - i % size + (i % size + step) % size) f...  50.4 us
    pallas_call x3, Pallas kernels, solve_call(): pl.pallas_call(functools.partial(kernel, size=len(bands)), out_shape=[squ...  35.3 us
    ppermute x21, starting transfers between devices, shift(): lax.ppermute(value, axis, [(i, (i + step) % count) for i in range(count)])  22.9 us
    ppermute x18, starting transfers between devices, turn(): lax.ppermute(value, axis, [(i, i - i % size + (i % size + step) % size) f...  10.8 us
    unnamed x12, local copies, waits for them, and re-layouts  7.52 us
    pallas_call x1, Pallas kernels, next_residual(): call(residual_kernel, [like(partial, F32), like(partial, BF16)] + shapes,...  7.14 us
  transfers between devices with their start and end apart: 39, of which 28 were waited for; matrix products, arithmetic and copies ran while one was open for 0% of the time, Pallas kernels for 14%

profile of v3, /device:TPU:0, one launch (start us, length us, event | category | flops | bytes accessed | tf_op | source)
XLA Modules:
  0.0 298.7 jit_solution(14639721763861584309)
XLA Ops:
  2.4 2.4 collective-permute-start.3
  9.6 3.0 %copy-done = bf16[9,4,1,1,8,96,96]{6,5,4,3,2,1,0:T(8,128)(2,1)S(1)} copy-done((bf16[9,4,1,1,8,96,96]{6,5,4,3,2,1,0:T(8,128)(2,1)S(1)}, bf16[9,4,1,1,8,96,96]{6,5,4,3,2,1,0:T(8,128)(2,1)}, u32[]{:S(2)}) %copy-start) | copy-done | bytes 5308440
  12.6 2.7 shard_map.28.partial
  15.3 19.7 %collective-permute-done.1.earlier = bf16[4,8,96,256]{3,2,1,0:T(8,128)(2,1)} collective-permute-done((bf16[4,8,96,256]{3,2,1,0:T(8,128)(2,1)}, bf16[4,8,96,256]{3,2,1,0:T(8,128)(2,1)}, u32[]{:S(2)}, u32[]{:S(2)}) %collective-permute-start.1) | collective-permute-done | bytes 1572896 | tf_op jit(solution)/shard_map/ppermute | solution.py:19
  35.0 2.5 collective-permute-done.later
  37.5 3.0 %copy-done.1 = bf16[9,4,1,1,8,96,96]{6,5,4,3,2,1,0:T(8,128)(2,1)S(1)} copy-done((bf16[9,4,1,1,8,96,96]{6,5,4,3,2,1,0:T(8,128)(2,1)S(1)}, bf16[9,4,1,1,8,96,96]{6,5,4,3,2,1,0:T(8,128)(2,1)}, u32[]{:S(2)}) %copy-start.1) | copy-done | bytes 5308440
  40.5 3.4 %shard_map.29.partial = f32[4,8,96,256]{3,2,1,0:T(8,128)S(1)} custom-call(f32[4,8,96,256]{3,2,1,0:T(8,128)S(1)} %shard_map.28.partial, bf16[4,8,96,256]{3,2,1,0:T(8,128)(2,1)} %collective-permute-done.later, bf16[4,8,96,256]{3,2,1,0:T(8,128)(2,1)} %collective-permute-done.1.earlier, bf16[9,4,8,96,96]{4,3,2,1,0:T(8,128)(2,1)S(1)} %bitcast.11, ...), custom_call_target="tpu_custom_call" | custom-call | flops 1 | bytes 1 | tf_op jit(solution)/shard_map/pallas_call | solution.py:179
  44.0 30.7 %collective-permute-done.2.ahead = bf16[4,8,96,256]{3,2,1,0:T(8,128)(2,1)} collective-permute-done((bf16[4,8,96,256]{3,2,1,0:T(8,128)(2,1)}, bf16[4,8,96,256]{3,2,1,0:T(8,128)(2,1)}, u32[]{:S(2)}, u32[]{:S(2)}) %collective-permute-start.2) | collective-permute-done | bytes 1572896 | tf_op jit(solution)/shard_map/ppermute | solution.py:19
  74.7 5.5 %shard_map.31 = (bf16[4,8,96,256]{3,2,1,0:T(8,128)(2,1)S(1)}, bf16[4,8,96,256]{3,2,1,0:T(8,128)(2,1)S(1)}, bf16[4,8,96,256]{3,2,1,0:T(8,128)(2,1)S(1)}, bf16[4,8...) custom-call(s32[1]{0:T(128)} %bitcast.1.place, ...), custom_call_target="tpu_custom_call" | custom-call | flops 1 | bytes 1 | tf_op jit(solution)/shard_map/pallas_call | solution.py:225
  83.5 20.1 %collective-permute-done.4 = f32[72,256]{1,0:T(8,128)S(1)} collective-permute-done((f32[72,256]{1,0:T(8,128)S(1)}, f32[72,256]{1,0:T(8,128)S(1)}, u32[]{:S(2)}, u32[]{:S(2)}) %collective-permute-start.4) | collective-permute-done | bytes 73760 | tf_op jit(solution)/shard_map/ppermute | solution.py:28
  103.7 2.9 shard_map.32.partial
  106.6 11.1 %collective-permute-done.7.xa = bf16[4,8,96,256]{3,2,1,0:T(8,128)(2,1)S(1)} collective-permute-done((bf16[4,8,96,256]{3,2,1,0:T(8,128)(2,1)S(1)}, bf16[4,8,96,256]{3,2,1,0:T(8,128)(2,1)S(1)}, u32[]{:S(2)}, u32[]{:S(2)}) %collective-permute-start.7) | collective-permute-done | bytes 1572896 | tf_op jit(solution)/shard_map/ppermute | solution.py:19
  119.7 2.3 collective-permute-done.11
  122.1 3.4 %collective-permute-done.10 = f32[72,256]{1,0:T(8,128)S(1)} collective-permute-done((f32[72,256]{1,0:T(8,128)S(1)}, f32[72,256]{1,0:T(8,128)S(1)}, u32[]{:S(2)}, u32[]{:S(2)}) %collective-permute-start.10) | collective-permute-done | bytes 73760 | tf_op jit(solution)/shard_map/ppermute | solution.py:19
  128.2 2.5 collective-permute-done.13.refs_2_
  131.2 11.9 %shard_map.33 = (f32[256,256]{1,0:T(8,128)S(1)}, f32[256,256]{1,0:T(8,128)S(1)}) custom-call(s32[1]{0:T(128)} %bitcast.1.place, f32[72,256]{1,0:T(8,128)S(1)} %add_add_fusion.refs_0_, f32[72,256]{1,0:T(8,128)S(1)} %collective-permute-done.12.refs_1_, f32[72,256]{1,0:T(8,128)S(1)} %collective-permute-done.13.refs_2_, ...), custom_call_target="tpu_custom_call" | custom-call | flops 1 | bytes 1 | tf_op jit(solution)/shard_map/pallas_call | solution.py:516
  143.1 20.0 %collective-permute-done.16.xb = bf16[4,8,96,256]{3,2,1,0:T(8,128)(2,1)S(1)} collective-permute-done((bf16[4,8,96,256]{3,2,1,0:T(8,128)(2,1)S(1)}, bf16[4,8,96,256]{3,2,1,0:T(8,128)(2,1)S(1)}, u32[]{:S(2)}, u32[]{:S(2)}) %collective-permute-start.16) | collective-permute-done | bytes 1572896 | tf_op jit(solution)/shard_map/ppermute | solution.py:19
  163.1 7.1 %shard_map.34 = (f32[4,8,96,256]{3,2,1,0:T(8,128)S(1)}, bf16[4,8,96,256]{3,2,1,0:T(8,128)(2,1)S(1)}, f32[64,256]{1,0:T(8,128)S(1)}, f32[64,256]{1,0:T(8,128)S(1)...) custom-call(s32[1]{0:T(128)} %bitcast.1.place, f32[4,8,96,256]{3,2,1,0:T(8,128)S(1)} %shard_map.32.partial, ...), custom_call_target="tpu_custom_call" | custom-call | flops 1 | bytes 1 | tf_op jit(solution)/shard_map/pallas_call | solution.py:281
  171.0 3.1 %collective-permute-start.20 = (bf16[4,8,96,256]{3,2,1,0:T(8,128)(2,1)S(1)}, bf16[4,8,96,256]{3,2,1,0:T(8,128)(2,1)S(1)}, u32[]{:S(2)}, u32[]{:S(2)}) collective-permute-start(bf16[4,8,96,256]{3,2,1,0:T(8,128)(2,1)S(1)} %get-tuple-element.70.here.above.below), channel_id=1, source_target_pairs={{0,3},{1,0},{2,1},{3,2},{4,7},{5,4},{6,5},{7,6},{8,11},{9,8},{10,9... | collective-permute-start | bytes 4718600 | tf_op jit(solution)/shard_map/ppermute | solution.py:19
  178.6 14.1 %collective-permute-done.18 = f32[64,256]{1,0:T(8,128)S(1)} collective-permute-done((f32[64,256]{1,0:T(8,128)S(1)}, f32[64,256]{1,0:T(8,128)S(1)}, u32[]{:S(2)}, u32[]{:S(2)}) %collective-permute-start.18) | collective-permute-done | bytes 65568 | tf_op jit(solution)/shard_map/ppermute | solution.py:28
  194.7 2.8 shard_map.35.partial
  197.5 10.3 %collective-permute-done.20.ahead = bf16[4,8,96,256]{3,2,1,0:T(8,128)(2,1)S(1)} collective-permute-done((bf16[4,8,96,256]{3,2,1,0:T(8,128)(2,1)S(1)}, bf16[4,8,96,256]{3,2,1,0:T(8,128)(2,1)S(1)}, u32[]{:S(2)}, u32[]{:S(2)}) %collective-permute-start.20) | collective-permute-done | bytes 1572896 | tf_op jit(solution)/shard_map/ppermute | solution.py:19
  207.8 4.3 %collective-permute-start.24 = (f32[64,256]{1,0:T(8,128)S(1)}, f32[64,256]{1,0:T(8,128)S(1)}, u32[]{:S(2)}, u32[]{:S(2)}) collective-permute-start(f32[64,256]{1,0:T(8,128)S(1)} %add_add_fusion.5), channel_id=1, source_target_pairs={{0,3},{1,0},{2,1},{3,2},{4,7},{5,4},{6,5},{7,6},{8,11},{9,8},{10,9... | collective-permute-start | bytes 196616 | tf_op jit(solution)/shard_map/ppermute | solution.py:19
  214.0 3.3 %collective-permute-done.23 = f32[64,256]{1,0:T(8,128)S(1)} collective-permute-done((f32[64,256]{1,0:T(8,128)S(1)}, f32[64,256]{1,0:T(8,128)S(1)}, u32[]{:S(2)}, u32[]{:S(2)}) %collective-permute-start.23) | collective-permute-done | bytes 65568 | tf_op jit(solution)/shard_map/ppermute | solution.py:19
  220.1 3.8 %collective-permute-done.26.refs_2_ = f32[64,256]{1,0:T(8,128)S(1)} collective-permute-done((f32[64,256]{1,0:T(8,128)S(1)}, f32[64,256]{1,0:T(8,128)S(1)}, u32[]{:S(2)}, u32[]{:S(2)}) %collective-permute-start.26) | collective-permute-done | bytes 65568 | tf_op jit(solution)/shard_map/ppermute | solution.py:28
  224.3 11.7 %shard_map.37 = (f32[256,256]{1,0:T(8,128)S(1)}, f32[256,256]{1,0:T(8,128)S(1)}) custom-call(s32[1]{0:T(128)} %bitcast.1.place, f32[256,256]{1,0:T(8,128)S(1)} %get-tuple-element.51.matrix, f32[64,256]{1,0:T(8,128)S(1)} %add_add_fusion.4.refs_0_, f32[64,256]{1,0:T(8,128)S(1)} %collective-permute-done.25.refs_1_, ...), custom_call_target="tpu_custom_call" | custom-call | flops 1 | bytes 1 | tf_op jit(solution)/shard_map/pallas_call | solution.py:516
  237.9 20.6 %collective-permute-done.29.behind = bf16[4,8,96,256]{3,2,1,0:T(8,128)(2,1)S(1)} collective-permute-done((bf16[4,8,96,256]{3,2,1,0:T(8,128)(2,1)S(1)}, bf16[4,8,96,256]{3,2,1,0:T(8,128)(2,1)S(1)}, u32[]{:S(2)}, u32[]{:S(2)}) %collective-permute-start.29) | collective-permute-done | bytes 1572896 | tf_op jit(solution)/shard_map/ppermute | solution.py:19
  260.8 2.6 shard_map.40
  270.9 3.4 %collective-permute-done.35 = f32[64,256]{1,0:T(8,128)S(1)} collective-permute-done((f32[64,256]{1,0:T(8,128)S(1)}, f32[64,256]{1,0:T(8,128)S(1)}, u32[]{:S(2)}, u32[]{:S(2)}) %collective-permute-start.35) | collective-permute-done | bytes 65568 | tf_op jit(solution)/shard_map/ppermute | solution.py:19
  274.3 2.7 collective-permute-done.34
  282.3 11.7 %shard_map.41.coefficients = f32[256,256]{1,0:T(8,128)S(1)} custom-call(s32[1]{0:T(128)} %bitcast.1.place, f32[256,256]{1,0:T(8,128)S(1)} %get-tuple-element.68.side, f32[64,256]{1,0:T(8,128)S(1)} %add_add_fusion.2.refs_0_, f32[64,256]{1,0:T(8,128)S(1)} %collective-permute-done.36.refs_1_, f32[64,256]{1,0:T(8,128)S(1)} %collective-permute-done.37.refs_2_, ...), custom_call_target="tpu_custom_call" | custom-call | flops 1 | bytes 1 | tf_op jit(solution)/shard_map/pallas_call | solution.py:516
  294.0 4.2 %shard_map.42 = f32[4,8,96,256]{3,2,1,0:T(8,128)} custom-call(f32[4,8,96,256]{3,2,1,0:T(8,128)S(1)} %shard_map.38.vector, f32[256,256]{1,0:T(8,128)S(1)} %shard_map.41.coefficients, f32[4,8,96,256]{3,2,1,0:T(8,128)S(1)} %shard_map.36.added), custom_call_target="tpu_custom_call" | custom-call | flops 1 | bytes 1 | tf_op jit(solution)/shard_map/pallas_call | solution.py:325
  (80 shorter events, 45.2 us)
Async XLA Ops:
  0.0 35.0 %collective-permute-start.1 = (bf16[4,8,96,256]{3,2,1,0:T(8,128)(2,1)}, bf16[4,8,96,256]{3,2,1,0:T(8,128)(2,1)}, u32[]{:S(2)}, u32[]{:S(2)}) collective-permute-start(bf16[4,8,96,256]{3,2,1,0:T(8,128)(2,1)} %bitcast.33), channel_id=1, source_target_pairs={{0,4},{4,8},{8,12},{12,0},{1,5},{5,9},{9,13},{13,1},{2,6},{6,10},{... | collective-permute-start | bytes 4718600 | tf_op jit(solution)/shard_map/ppermute | solution.py:19
  0.5 37.0 %collective-permute-start = (bf16[4,8,96,256]{3,2,1,0:T(8,128)(2,1)}, bf16[4,8,96,256]{3,2,1,0:T(8,128)(2,1)}, u32[]{:S(2)}, u32[]{:S(2)}) collective-permute-start(bf16[4,8,96,256]{3,2,1,0:T(8,128)(2,1)} %bitcast.34), channel_id=1, source_target_pairs={{0,12},{4,0},{8,4},{12,8},{1,13},{5,1},{9,5},{13,9},{2,14},{6,2},{... | collective-permute-start | bytes 4718600 | tf_op jit(solution)/shard_map/ppermute | solution.py:19
  2.4 41.5 %collective-permute-start.3 = (bf16[4,8,96,256]{3,2,1,0:T(8,128)(2,1)}, bf16[4,8,96,256]{3,2,1,0:T(8,128)(2,1)}, u32[]{:S(2)}, u32[]{:S(2)}) collective-permute-start(bf16[4,8,96,256]{3,2,1,0:T(8,128)(2,1)} %bitcast.35), channel_id=1, source_target_pairs={{0,1},{1,2},{2,3},{3,0},{4,5},{5,6},{6,7},{7,4},{8,9},{9,10},{10,1... | collective-permute-start | bytes 4718600 | tf_op jit(solution)/shard_map/ppermute | solution.py:19
  4.8 69.9 %collective-permute-start.2 = (bf16[4,8,96,256]{3,2,1,0:T(8,128)(2,1)}, bf16[4,8,96,256]{3,2,1,0:T(8,128)(2,1)}, u32[]{:S(2)}, u32[]{:S(2)}) collective-permute-start(bf16[4,8,96,256]{3,2,1,0:T(8,128)(2,1)} %bitcast.36), channel_id=1, source_target_pairs={{0,3},{1,0},{2,1},{3,2},{4,7},{5,4},{6,5},{7,6},{8,11},{9,8},{10,9... | collective-permute-start | bytes 4718600 | tf_op jit(solution)/shard_map/ppermute | solution.py:19
  80.2 37.5 %collective-permute-start.7 = (bf16[4,8,96,256]{3,2,1,0:T(8,128)(2,1)S(1)}, bf16[4,8,96,256]{3,2,1,0:T(8,128)(2,1)S(1)}, u32[]{:S(2)}, u32[]{:S(2)}) collective-permute-start(bf16[4,8,96,256]{3,2,1,0:T(8,128)(2,1)S(1)} %get-tuple-element.47), channel_id=1, source_target_pairs={{0,1},{1,2},{2,3},{3,0},{4,5},{5,6},{6,7},{7,4},{8,9},{9,10},{10,1... | collective-permute-start | bytes 4718600 | tf_op jit(solution)/shard_map/ppermute | solution.py:19
  81.4 36.3 %collective-permute-start.8 = (bf16[4,8,96,256]{3,2,1,0:T(8,128)(2,1)S(1)}, bf16[4,8,96,256]{3,2,1,0:T(8,128)(2,1)S(1)}, u32[]{:S(2)}, u32[]{:S(2)}) collective-permute-start(bf16[4,8,96,256]{3,2,1,0:T(8,128)(2,1)S(1)} %get-tuple-element.48), channel_id=1, source_target_pairs={{0,4},{4,8},{8,12},{12,0},{1,5},{5,9},{9,13},{13,1},{2,6},{6,10},{... | collective-permute-start | bytes 4718600 | tf_op jit(solution)/shard_map/ppermute | solution.py:19
  81.4 22.2 %collective-permute-start.4 = (f32[72,256]{1,0:T(8,128)S(1)}, f32[72,256]{1,0:T(8,128)S(1)}, u32[]{:S(2)}, u32[]{:S(2)}) collective-permute-start(f32[72,256]{1,0:T(8,128)S(1)} %get-tuple-element.42), channel_id=1, source_target_pairs={{0,4},{4,8},{8,12},{12,0},{1,5},{5,9},{9,13},{13,1},{2,6},{6,10},{... | collective-permute-start | bytes 221192 | tf_op jit(solution)/shard_map/ppermute | solution.py:28
  82.0 21.6 %collective-permute-start.5 = (f32[72,256]{1,0:T(8,128)S(1)}, f32[72,256]{1,0:T(8,128)S(1)}, u32[]{:S(2)}, u32[]{:S(2)}) collective-permute-start(f32[72,256]{1,0:T(8,128)S(1)} %get-tuple-element.43), channel_id=1, source_target_pairs={{0,8},{4,12},{8,0},{12,4},{1,9},{5,13},{9,1},{13,5},{2,10},{6,14},... | collective-permute-start | bytes 221192 | tf_op jit(solution)/shard_map/ppermute | solution.py:28
  83.5 20.1 %collective-permute-start.6 = (f32[72,256]{1,0:T(8,128)S(1)}, f32[72,256]{1,0:T(8,128)S(1)}, u32[]{:S(2)}, u32[]{:S(2)}) collective-permute-start(f32[72,256]{1,0:T(8,128)S(1)} %get-tuple-element.44), channel_id=1, source_target_pairs={{0,12},{4,0},{8,4},{12,8},{1,13},{5,1},{9,5},{13,9},{2,14},{6,2},{... | collective-permute-start | bytes 221192 | tf_op jit(solution)/shard_map/ppermute | solution.py:28
  117.7 7.7 %collective-permute-start.10 = (f32[72,256]{1,0:T(8,128)S(1)}, f32[72,256]{1,0:T(8,128)S(1)}, u32[]{:S(2)}, u32[]{:S(2)}) collective-permute-start(f32[72,256]{1,0:T(8,128)S(1)} %add_add_fusion.1), channel_id=1, source_target_pairs={{0,2},{1,3},{2,0},{3,1},{4,6},{5,7},{6,4},{7,5},{8,10},{9,11},{10,... | collective-permute-start | bytes 221192 | tf_op jit(solution)/shard_map/ppermute | solution.py:19
  119.2 6.3 %collective-permute-start.9 = (f32[72,256]{1,0:T(8,128)S(1)}, f32[72,256]{1,0:T(8,128)S(1)}, u32[]{:S(2)}, u32[]{:S(2)}) collective-permute-start(f32[72,256]{1,0:T(8,128)S(1)} %add_add_fusion.1), channel_id=1, source_target_pairs={{0,1},{1,2},{2,3},{3,0},{4,5},{5,6},{6,7},{7,4},{8,9},{9,10},{10,1... | collective-permute-start | bytes 221192 | tf_op jit(solution)/shard_map/ppermute | solution.py:19
  125.5 5.1 %collective-permute-start.13 = (f32[72,256]{1,0:T(8,128)S(1)}, f32[72,256]{1,0:T(8,128)S(1)}, u32[]{:S(2)}, u32[]{:S(2)}) collective-permute-start(f32[72,256]{1,0:T(8,128)S(1)} %add_add_fusion.refs_0_), channel_id=1, source_target_pairs={{0,8},{4,12},{8,0},{12,4},{1,9},{5,13},{9,1},{13,5},{2,10},{6,14},... | collective-permute-start | bytes 221192 | tf_op jit(solution)/shard_map/ppermute | solution.py:28
  126.1 4.9 %collective-permute-start.12 = (f32[72,256]{1,0:T(8,128)S(1)}, f32[72,256]{1,0:T(8,128)S(1)}, u32[]{:S(2)}, u32[]{:S(2)}) collective-permute-start(f32[72,256]{1,0:T(8,128)S(1)} %add_add_fusion.refs_0_), channel_id=1, source_target_pairs={{0,4},{4,8},{8,12},{12,0},{1,5},{5,9},{9,13},{13,1},{2,6},{6,10},{... | collective-permute-start | bytes 221192 | tf_op jit(solution)/shard_map/ppermute | solution.py:28
  126.3 36.8 %collective-permute-start.16 = (bf16[4,8,96,256]{3,2,1,0:T(8,128)(2,1)S(1)}, bf16[4,8,96,256]{3,2,1,0:T(8,128)(2,1)S(1)}, u32[]{:S(2)}, u32[]{:S(2)}) collective-permute-start(bf16[4,8,96,256]{3,2,1,0:T(8,128)(2,1)S(1)} %get-tuple-element.55), channel_id=1, source_target_pairs={{0,3},{1,0},{2,1},{3,2},{4,7},{5,4},{6,5},{7,6},{8,11},{9,8},{10,9... | collective-permute-start | bytes 4718600 | tf_op jit(solution)/shard_map/ppermute | solution.py:19
  131.0 32.1 %collective-permute-start.15 = (bf16[4,8,96,256]{3,2,1,0:T(8,128)(2,1)S(1)}, bf16[4,8,96,256]{3,2,1,0:T(8,128)(2,1)S(1)}, u32[]{:S(2)}, u32[]{:S(2)}) collective-permute-start(bf16[4,8,96,256]{3,2,1,0:T(8,128)(2,1)S(1)} %get-tuple-element.53), channel_id=1, source_target_pairs={{0,12},{4,0},{8,4},{12,8},{1,13},{5,1},{9,5},{13,9},{2,14},{6,2},{... | collective-permute-start | bytes 4718600 | tf_op jit(solution)/shard_map/ppermute | solution.py:19
  170.3 27.2 %collective-permute-start.21 = (bf16[4,8,96,256]{3,2,1,0:T(8,128)(2,1)S(1)}, bf16[4,8,96,256]{3,2,1,0:T(8,128)(2,1)S(1)}, u32[]{:S(2)}, u32[]{:S(2)}) collective-permute-start(bf16[4,8,96,256]{3,2,1,0:T(8,128)(2,1)S(1)} %get-tuple-element.70.here.above.below), channel_id=1, source_target_pairs={{0,12},{4,0},{8,4},{12,8},{1,13},{5,1},{9,5},{13,9},{2,14},{6,2},{... | collective-permute-start | bytes 4718600 | tf_op jit(solution)/shard_map/ppermute | solution.py:19
  171.0 36.7 %collective-permute-start.20 = (bf16[4,8,96,256]{3,2,1,0:T(8,128)(2,1)S(1)}, bf16[4,8,96,256]{3,2,1,0:T(8,128)(2,1)S(1)}, u32[]{:S(2)}, u32[]{:S(2)}) collective-permute-start(bf16[4,8,96,256]{3,2,1,0:T(8,128)(2,1)S(1)} %get-tuple-element.70.here.above.below), channel_id=1, source_target_pairs={{0,3},{1,0},{2,1},{3,2},{4,7},{5,4},{6,5},{7,6},{8,11},{9,8},{10,9... | collective-permute-start | bytes 4718600 | tf_op jit(solution)/shard_map/ppermute | solution.py:19
  174.1 4.5 %collective-permute-start.17 = (f32[64,256]{1,0:T(8,128)S(1)}, f32[64,256]{1,0:T(8,128)S(1)}, u32[]{:S(2)}, u32[]{:S(2)}) collective-permute-start(f32[64,256]{1,0:T(8,128)S(1)} %get-tuple-element.58), channel_id=1, source_target_pairs={{0,4},{4,8},{8,12},{12,0},{1,5},{5,9},{9,13},{13,1},{2,6},{6,10},{... | collective-permute-start | bytes 196616 | tf_op jit(solution)/shard_map/ppermute | solution.py:28
  174.1 18.6 %collective-permute-start.18 = (f32[64,256]{1,0:T(8,128)S(1)}, f32[64,256]{1,0:T(8,128)S(1)}, u32[]{:S(2)}, u32[]{:S(2)}) collective-permute-start(f32[64,256]{1,0:T(8,128)S(1)} %get-tuple-element.59), channel_id=1, source_target_pairs={{0,8},{4,12},{8,0},{12,4},{1,9},{5,13},{9,1},{13,5},{2,10},{6,14},... | collective-permute-start | bytes 196616 | tf_op jit(solution)/shard_map/ppermute | solution.py:28
  175.4 17.3 %collective-permute-start.19 = (f32[64,256]{1,0:T(8,128)S(1)}, f32[64,256]{1,0:T(8,128)S(1)}, u32[]{:S(2)}, u32[]{:S(2)}) collective-permute-start(f32[64,256]{1,0:T(8,128)S(1)} %get-tuple-element.60), channel_id=1, source_target_pairs={{0,12},{4,0},{8,4},{12,8},{1,13},{5,1},{9,5},{13,9},{2,14},{6,2},{... | collective-permute-start | bytes 196616 | tf_op jit(solution)/shard_map/ppermute | solution.py:28
  207.8 6.2 %collective-permute-start.24 = (f32[64,256]{1,0:T(8,128)S(1)}, f32[64,256]{1,0:T(8,128)S(1)}, u32[]{:S(2)}, u32[]{:S(2)}) collective-permute-start(f32[64,256]{1,0:T(8,128)S(1)} %add_add_fusion.5), channel_id=1, source_target_pairs={{0,3},{1,0},{2,1},{3,2},{4,7},{5,4},{6,5},{7,6},{8,11},{9,8},{10,9... | collective-permute-start | bytes 196616 | tf_op jit(solution)/shard_map/ppermute | solution.py:19
  212.1 5.2 %collective-permute-start.23 = (f32[64,256]{1,0:T(8,128)S(1)}, f32[64,256]{1,0:T(8,128)S(1)}, u32[]{:S(2)}, u32[]{:S(2)}) collective-permute-start(f32[64,256]{1,0:T(8,128)S(1)} %add_add_fusion.5), channel_id=1, source_target_pairs={{0,2},{1,3},{2,0},{3,1},{4,6},{5,7},{6,4},{7,5},{8,10},{9,11},{10,... | collective-permute-start | bytes 196616 | tf_op jit(solution)/shard_map/ppermute | solution.py:19
  212.1 6.1 %collective-permute-start.22 = (f32[64,256]{1,0:T(8,128)S(1)}, f32[64,256]{1,0:T(8,128)S(1)}, u32[]{:S(2)}, u32[]{:S(2)}) collective-permute-start(f32[64,256]{1,0:T(8,128)S(1)} %add_add_fusion.5), channel_id=1, source_target_pairs={{0,1},{1,2},{2,3},{3,0},{4,5},{5,6},{6,7},{7,4},{8,9},{9,10},{10,1... | collective-permute-start | bytes 196616 | tf_op jit(solution)/shard_map/ppermute | solution.py:19
  218.2 5.7 %collective-permute-start.26 = (f32[64,256]{1,0:T(8,128)S(1)}, f32[64,256]{1,0:T(8,128)S(1)}, u32[]{:S(2)}, u32[]{:S(2)}) collective-permute-start(f32[64,256]{1,0:T(8,128)S(1)} %add_add_fusion.4.refs_0_), channel_id=1, source_target_pairs={{0,8},{4,12},{8,0},{12,4},{1,9},{5,13},{9,1},{13,5},{2,10},{6,14},... | collective-permute-start | bytes 196616 | tf_op jit(solution)/shard_map/ppermute | solution.py:28
  219.9 38.6 %collective-permute-start.29 = (bf16[4,8,96,256]{3,2,1,0:T(8,128)(2,1)S(1)}, bf16[4,8,96,256]{3,2,1,0:T(8,128)(2,1)S(1)}, u32[]{:S(2)}, u32[]{:S(2)}) collective-permute-start(bf16[4,8,96,256]{3,2,1,0:T(8,128)(2,1)S(1)} %get-tuple-element.70.here.above.below), channel_id=1, source_target_pairs={{0,1},{1,2},{2,3},{3,0},{4,5},{5,6},{6,7},{7,4},{8,9},{9,10},{10,1... | collective-permute-start | bytes 4718600 | tf_op jit(solution)/shard_map/ppermute | solution.py:19
  224.1 34.5 %collective-permute-start.28 = (bf16[4,8,96,256]{3,2,1,0:T(8,128)(2,1)S(1)}, bf16[4,8,96,256]{3,2,1,0:T(8,128)(2,1)S(1)}, u32[]{:S(2)}, u32[]{:S(2)}) collective-permute-start(bf16[4,8,96,256]{3,2,1,0:T(8,128)(2,1)S(1)} %get-tuple-element.70.here.above.below), channel_id=1, source_target_pairs={{0,4},{4,8},{8,12},{12,0},{1,5},{5,9},{9,13},{13,1},{2,6},{6,10},{... | collective-permute-start | bytes 4718600 | tf_op jit(solution)/shard_map/ppermute | solution.py:19
  263.5 5.0 %collective-permute-start.31 = (f32[64,256]{1,0:T(8,128)S(1)}, f32[64,256]{1,0:T(8,128)S(1)}, u32[]{:S(2)}, u32[]{:S(2)}) collective-permute-start(f32[64,256]{1,0:T(8,128)S(1)} %get-tuple-element.75), channel_id=1, source_target_pairs={{0,8},{4,12},{8,0},{12,4},{1,9},{5,13},{9,1},{13,5},{2,10},{6,14},... | collective-permute-start | bytes 196616 | tf_op jit(solution)/shard_map/ppermute | solution.py:28
  268.5 5.8 %collective-permute-start.35 = (f32[64,256]{1,0:T(8,128)S(1)}, f32[64,256]{1,0:T(8,128)S(1)}, u32[]{:S(2)}, u32[]{:S(2)}) collective-permute-start(f32[64,256]{1,0:T(8,128)S(1)} %add_add_fusion.3), channel_id=1, source_target_pairs={{0,3},{1,0},{2,1},{3,2},{4,7},{5,4},{6,5},{7,6},{8,11},{9,8},{10,9... | collective-permute-start | bytes 196616 | tf_op jit(solution)/shard_map/ppermute | solution.py:19
  268.5 8.4 %collective-permute-start.34 = (f32[64,256]{1,0:T(8,128)S(1)}, f32[64,256]{1,0:T(8,128)S(1)}, u32[]{:S(2)}, u32[]{:S(2)}) collective-permute-start(f32[64,256]{1,0:T(8,128)S(1)} %add_add_fusion.3), channel_id=1, source_target_pairs={{0,2},{1,3},{2,0},{3,1},{4,6},{5,7},{6,4},{7,5},{8,10},{9,11},{10,... | collective-permute-start | bytes 196616 | tf_op jit(solution)/shard_map/ppermute | solution.py:19
  268.9 8.1 %collective-permute-start.33 = (f32[64,256]{1,0:T(8,128)S(1)}, f32[64,256]{1,0:T(8,128)S(1)}, u32[]{:S(2)}, u32[]{:S(2)}) collective-permute-start(f32[64,256]{1,0:T(8,128)S(1)} %add_add_fusion.3), channel_id=1, source_target_pairs={{0,1},{1,2},{2,3},{3,0},{4,5},{5,6},{6,7},{7,4},{8,9},{9,10},{10,1... | collective-permute-start | bytes 196616 | tf_op jit(solution)/shard_map/ppermute | solution.py:19
  277.4 4.7 %collective-permute-start.37 = (f32[64,256]{1,0:T(8,128)S(1)}, f32[64,256]{1,0:T(8,128)S(1)}, u32[]{:S(2)}, u32[]{:S(2)}) collective-permute-start(f32[64,256]{1,0:T(8,128)S(1)} %add_add_fusion.2.refs_0_), channel_id=1, source_target_pairs={{0,8},{4,12},{8,0},{12,4},{1,9},{5,13},{9,1},{13,5},{2,10},{6,14},... | collective-permute-start | bytes 196616 | tf_op jit(solution)/shard_map/ppermute | solution.py:28
  277.9 4.4 %collective-permute-start.36 = (f32[64,256]{1,0:T(8,128)S(1)}, f32[64,256]{1,0:T(8,128)S(1)}, u32[]{:S(2)}, u32[]{:S(2)}) collective-permute-start(f32[64,256]{1,0:T(8,128)S(1)} %add_add_fusion.2.refs_0_), channel_id=1, source_target_pairs={{0,4},{4,8},{8,12},{12,0},{1,5},{5,9},{9,13},{13,1},{2,6},{6,10},{... | collective-permute-start | bytes 196616 | tf_op jit(solution)/shard_map/ppermute | solution.py:28
  (13 other events, 302.1 us)

commit v4 on v3

--- a/solution.py
+++ b/solution.py
@@ -11,7 +11,7 @@
 PIVOTS = 8
 HIGHEST = lax.Precision.HIGHEST
 F32, BF16 = jnp.float32, jnp.bfloat16
-VMEM_BYTES = 20 * 2**20
+VMEM_BYTES = 14 * 2**20
 
 
 def shift(value, axis, step):
@@ -157,28 +157,41 @@
     )(vector, vector, vector, *([links] * 5))
 
 
-def time_terms_kernel(partial, later, earlier, la, lb, *rest):
-    out = rest[-1]
-    depth, comp, rhs = partial.shape
-    if len(rest) > 1:
-        image, beta = rest[:2]
-        rows = image[...].reshape(depth * comp, rhs)
-        extra = sum(dot(rows, part) for part in split(beta[...], 2)).reshape(partial.shape)
-    for z in range(depth):
-        total = partial[z] + dot(la[z], later[z]) + dot(lb[z], earlier[z])
-        out[z] = total + extra[z] if len(rest) > 1 else total
-
-
-def time_terms(partial, later, earlier, links, image=None, beta=None):
+def time_terms_kernel(partial, later, earlier, la, lb, out):
+    for z in range(partial.shape[0]):
+        out[z] = partial[z] + dot(la[z], later[z]) + dot(lb[z], earlier[z])
+
+
+def time_terms(partial, later, earlier, links):
     spec = plane_spec(partial.shape)
-    specs = [spec] * 3 + [link_spec(links, 1), link_spec(links, 2)]
-    operands = [partial, later, earlier, links, links]
-    if image is not None:
-        specs += [spec, matrix_spec(beta.shape)]
-        operands += [image, beta]
-    return call(
-        time_terms_kernel, like(partial, F32), (partial.shape[0],), specs, spec
-    )(*operands)
+    return call(
+        time_terms_kernel,
+        like(partial, F32),
+        (partial.shape[0],),
+        [spec] * 3 + [link_spec(links, 1), link_spec(links, 2)],
+        spec,
+    )(partial, later, earlier, links, links)
+
+
+def joined_links_kernel(xa, xb, ta, tb, out):
+    for z in range(xa.shape[0]):
+        out[z] = jnp.concatenate([xa[z], xb[z], ta[z], tb[z]], axis=1)
+
+
+def joined_links(links):
+    shape = links.shape[1:4] + (4 * links.shape[4],)
+    return call(
+        joined_links_kernel,
+        jax.ShapeDtypeStruct(shape, links.dtype),
+        (shape[0],),
+        [link_spec(links, number) for number in (3, 4, 1, 2)],
+        plane_spec(shape),
+    )(*([links] * 4))
+
+
+def outer_terms(joined, vectors, z):
+    stacked = jnp.concatenate([vector[z] for vector in vectors], axis=0)
+    return dot(joined[z, :, : stacked.shape[0]], stacked)
 
 
 def packed(energy, curvature):
@@ -197,40 +210,33 @@
     return energy, curvature
 
 
-def first_image_kernel(place, partial, ahead, behind, energy, la, lb, lc, ld, image, *rest):
-    products, bands, total = rest[:4], rest[4:-1], rest[-1]
+def first_image_kernel(place, partial, energy, *rest):
+    vectors, joined, image, products = rest[:2], rest[2], rest[3], rest[4:8]
+    bands, total = rest[8:-1], rest[-1]
     on_first(total)
-    depth, comp, rhs = partial.shape
+    depth, comp, _ = partial.shape
     for z in range(depth):
-        value = partial[z] + dot(la[z], ahead[z]) + dot(lb[z], behind[z])
-        image[z] = value.astype(BF16)
-    for link, product in zip((la, lb, lc, ld), products):
-        for z in range(depth):
-            product[z] = dot_rows(link[z], image[z]).astype(BF16)
+        image[z] = (partial[z] + outer_terms(joined, vectors, z)).astype(BF16)
+    for z in range(depth):
+        moved = dot_rows(joined[z], image[z]).astype(BF16)
+        for number, product in enumerate(products):
+            product[z] = moved[number * comp : (number + 1) * comp]
     add_planes(total, image)
 
-    @pl.when(pl.program_id(0) == pl.num_programs(0) - 1)
-    def _():
-        pair, diagonal = packed(energy[...], total[...])
-        total[...] = pair
-        height = rhs // len(bands)
-        put_bands(place, total, [band.at[pl.ds(0, height), :] for band in bands])
-        for band in bands:
-            band[pl.ds(height, 8), :] = jnp.broadcast_to(diagonal, (8, rhs))
-
-
-def first_image(partial, ahead, behind, energy, links, place, size):
+    on_last(place, energy, total, bands)
+
+
+def first_image(partial, halo, energy, joined, place, size):
     spec, rhs = plane_spec(partial.shape), partial.shape[-1]
     shapes, specs = band_outputs(size, rhs, 8)
     outputs = call(
         first_image_kernel,
         [like(partial, BF16)] * 5 + shapes,
         (partial.shape[0],),
-        [SCALAR] + [spec] * 3 + [matrix_spec(energy.shape)]
-        + [link_spec(links, number) for number in (3, 4, 1, 2)],
+        [SCALAR, spec, matrix_spec(energy.shape)] + [spec] * 2 + [plane_spec(joined.shape)],
         [spec] * 5 + specs,
         [pltpu.VMEM((rhs, rhs), F32)],
-    )(place, partial, ahead, behind, energy, *([links] * 4))
+    )(place, partial, energy, *halo, joined)
     return outputs[0], outputs[1:5], outputs[5:]
 
 
@@ -260,75 +266,66 @@
     )(image, image, image, *([links] * 5))
 
 
-def residual_kernel(place, partial, ta, tb, xa, xb, source, alpha, residual, rounded, *rest):
-    *bands, total = rest
-    on_first(total)
-    normal = partial[...]
-    for term in (ta, tb, xa, xb):
-        normal += term[...].astype(F32)
+def begun_residual_kernel(partial, first, second, source, alpha, out):
+    normal = partial[...] + first[...].astype(F32) + second[...].astype(F32)
     rows = (normal.shape[0] * normal.shape[1], normal.shape[2])
     moved = dot_full(normal.reshape(rows), alpha[...]).reshape(normal.shape)
-    value = source[...].astype(F32) - moved
-    residual[...] = value
-    rounded[...] = value.astype(BF16)
-    add_planes(total, residual)
-    on_last(place, total, bands)
-
-
-def next_residual(partial, terms, source, alpha, place, size):
-    spec, rhs = plane_spec(partial.shape), partial.shape[-1]
-    shapes, specs = band_outputs(size, rhs)
-    outputs = call(
+    out[...] = source[...].astype(F32) - moved
+
+
+def begun_residual(partial, terms, source, alpha):
+    spec = plane_spec(partial.shape)
+    return call(
+        begun_residual_kernel,
+        like(partial, F32),
+        (partial.shape[0],),
+        [spec] * 4 + [matrix_spec(alpha.shape)],
+        spec,
+    )(partial, *terms, source, alpha)
+
+
+def residual_kernel(begun, first, second, alpha, residual, rounded):
+    value = first[...].astype(F32) + second[...].astype(F32)
+    rows = (value.shape[0] * value.shape[1], value.shape[2])
+    high, low = split(value.reshape(rows), 2)
+    upper, middle, lower = split(alpha[...], 3)
+    moved = dot(high, upper) + (dot(high, middle) + dot(low, upper))
+    moved += dot(high, lower) + dot(low, middle)
+    total = begun[...] - moved.reshape(value.shape)
+    residual[...] = total
+    rounded[...] = total.astype(BF16)
+
+
+def next_residual(begun, first, second, alpha):
+    spec = plane_spec(begun.shape)
+    return call(
         residual_kernel,
-        [like(partial, F32), like(partial, BF16)] + shapes,
-        (partial.shape[0],),
-        [SCALAR] + [spec] * 6 + [matrix_spec(alpha.shape)],
-        [spec] * 2 + specs,
-        [pltpu.VMEM((rhs, rhs), F32)],
-    )(place, partial, *terms, source, alpha)
-    return outputs[0], outputs[1], outputs[2:]
-
-
-def mixed_kernel(vector, coefficients, added, out):
-    value = vector[...]
-    rows = value.reshape(value.shape[0] * value.shape[1], value.shape[2])
-    total = sum(dot(rows, part) for part in split(coefficients[...], 3))
-    total = total.reshape(value.shape)
-    out[...] = total if added is None else added[...] + total
-
-
-def mixed(vector, coefficients, added=None):
-    spec = plane_spec(vector.shape)
-    kernel = mixed_kernel
-    operands = (vector, coefficients)
-    if added is None:
-        kernel = lambda vector, coefficients, out: mixed_kernel(vector, coefficients, None, out)
-    else:
-        operands += (added,)
-    return call(
-        kernel,
-        like(vector, F32),
-        (vector.shape[0],),
-        [spec, matrix_spec(coefficients.shape)] + [spec] * (len(operands) - 2),
+        [like(begun, F32), like(begun, BF16)],
+        (begun.shape[0],),
+        [spec] * 3 + [matrix_spec(alpha.shape)],
+        [spec] * 2,
+    )(begun, first, second, alpha)
+
+
+def answer_kernel(source, residual, first, second, out):
+    rows = (source.shape[0] * source.shape[1], source.shape[2])
+    value = source[...].reshape(rows)
+    total = sum(dot(value, part) for part in split(first[...], 3))
+    high, low = split(residual[...].reshape(rows), 2)
+    upper, lower = split(second[...], 2)
+    total += dot(high, upper) + (dot(high, lower) + dot(low, upper))
+    out[...] = total.reshape(source.shape)
+
+
+def answer(source, residual, first, second):
+    spec = plane_spec(source.shape)
+    return call(
+        answer_kernel,
+        like(source, F32),
+        (source.shape[0],),
+        [spec] * 2 + [matrix_spec(first.shape)] * 2,
         spec,
-    )(*operands)
-
-
-def answer_kernel(vector, coefficients, added, out):
-    value = vector[...]
-    rows = value.reshape(value.shape[0] * value.shape[1], value.shape[2])
-    out[...] = added[...] + dot_full(rows, coefficients[...]).reshape(value.shape)
-
-
-def answer(vector, coefficients, added):
-    spec = plane_spec(vector.shape)
-    return call(
-        answer_kernel,
-        like(vector, F32),
-        (vector.shape[0],),
-        [spec, matrix_spec(coefficients.shape), spec],
-        spec,
-    )(vector, coefficients, added)
+    )(source, residual, first, second)
 
 
 def add_gram(total, rows):
@@ -352,10 +349,16 @@
         total[...] = jnp.zeros_like(total)
 
 
-def on_last(place, total, bands):
+def on_last(place, other, total, bands):
     @pl.when(pl.program_id(0) == pl.num_programs(0) - 1)
     def _():
-        put_bands(place, total, bands)
+        pair, diagonal = packed(other[...], total[...])
+        total[...] = pair
+        rhs = total.shape[0]
+        height = rhs // len(bands)
+        put_bands(place, total, [band.at[pl.ds(0, height), :] for band in bands])
+        for band in bands:
+            band[pl.ds(height, 8), :] = jnp.broadcast_to(diagonal, (8, rhs))
 
 
 def add_planes(total, vector):
@@ -379,22 +382,21 @@
     )(vector)
 
 
-def second_image(partial, ahead, behind, la, lb):
+def second_image(partial, vectors, joined):
     pieces = []
     for z in range(partial.shape[0]):
-        value = partial[z] + dot(la[z], ahead[z]) + dot(lb[z], behind[z])
-        pieces.append(value.astype(BF16))
+        pieces.append((partial[z] + outer_terms(joined, vectors, z)).astype(BF16))
     return jnp.concatenate(pieces, axis=0)
 
 
-def second_gram_kernel(place, partial, ahead, behind, la, lb, *rest):
-    *bands, total = rest
+def second_gram_kernel(place, partial, fresh, *rest):
+    vectors, joined, bands, total = rest[:4], rest[4], rest[5:-1], rest[-1]
     on_first(total)
-    add_gram(total, second_image(partial, ahead, behind, la, lb))
-    on_last(place, total, bands)
-
-
-def band_outputs(size, rhs, extra=0):
+    add_gram(total, second_image(partial, vectors, joined))
+    on_last(place, fresh, total, bands)
+
+
+def band_outputs(size, rhs, extra):
     shape = jax.ShapeDtypeStruct((rhs // size + extra, rhs), F32)
     return [shape] * size, [matrix_spec(shape.shape)] * size
 
@@ -402,18 +404,18 @@
 SCALAR = pl.BlockSpec(memory_space=pltpu.SMEM)
 
 
-def second_gram(partial, ahead, behind, links, place, size):
+def second_gram(partial, halo, fresh, joined, place, size):
     rhs = partial.shape[-1]
     spec = plane_spec(partial.shape)
-    shapes, out_specs = band_outputs(size, rhs)
+    shapes, out_specs = band_outputs(size, rhs, 8)
     return call(
         second_gram_kernel,
         shapes,
         (partial.shape[0],),
-        [SCALAR] + [spec] * 3 + [link_spec(links, 3), link_spec(links, 4)],
+        [SCALAR, spec, matrix_spec(fresh.shape)] + [spec] * 4 + [plane_spec(joined.shape)],
         out_specs,
         [pltpu.VMEM((rhs, rhs), F32)],
-    )(place, partial, ahead, behind, links, links)
+    )(place, partial, fresh, *halo, joined)
 
 
 def inverse_block(tile):
@@ -486,44 +488,53 @@
     out[:half, :] = start - dot_full(across, bottom)
 
 
-def solve_both_kernel(place, *refs, size):
+def unpack_bands(place, bands, scratch):
+    assemble(place, bands, scratch)
+    height = scratch.shape[0] // len(bands)
+    return unpacked(scratch[...], bands[0][height : height + 1, :])
+
+
+def first_solve_kernel(place, *refs, size):
     bands = refs[:size]
-    out, side, matrix = refs[size:]
-    assemble(place, bands, side)
-    height = side.shape[0] // size
-    energy, curvature = unpacked(side[...], bands[0][height : height + 1, :])
-    side[...] = energy
-    matrix[...] = curvature
-    solve_into(out, matrix, side)
-
-
-def solve_side_kernel(place, matrix, *refs, size):
-    out, side = refs[size:]
-    assemble(place, refs[:size], side)
-    solve_into(out, matrix, side)
-
-
-def solve_matrix_kernel(place, side, *refs, size):
-    out, matrix = refs[size:]
-    assemble(place, refs[:size], matrix)
-    solve_into(out, matrix, side)
-
-
-def solve_call(kernel, outputs, scratch, place, operands, bands):
-    rhs = bands[0].shape[1]
+    alpha, energy, curvature = refs[size:]
+    energy[...], curvature[...] = unpack_bands(place, bands, alpha)
+    solve_into(alpha, curvature, energy)
+
+
+def inverse_kernel(place, matrix, out, unit):
+    row = lax.broadcasted_iota(jnp.int32, unit.shape, 0)
+    column = lax.broadcasted_iota(jnp.int32, unit.shape, 1)
+    unit[...] = jnp.where(row == column, 1.0, 0.0)
+    solve_into(out, matrix, unit)
+
+
+def second_solve_kernel(place, inverse, first, alpha, *refs, size):
+    bands = refs[:size]
+    out, weights, matrix, fresh = refs[size:]
+    fresh[...], image_gram = unpack_bands(place, bands, matrix)
+    beta = dot_full(inverse[...], fresh[...])
+    moved = dot_full(first[...], beta)
+    less = lax.dot_general(
+        beta, moved, (((0,), (0,)), ((), ())), precision=HIGHEST, preferred_element_type=F32
+    )
+    matrix[...] = image_gram - less
+    solve_into(out, matrix, fresh)
+    weights[...] = alpha[...] + dot_full(beta, out[...])
+
+
+def solve_call(kernel, outputs, scratch, place, *operands):
+    rhs = operands[-1].shape[1]
     vmem = pl.BlockSpec(memory_space=pltpu.VMEM)
     square = jax.ShapeDtypeStruct((rhs, rhs), F32)
     return pl.pallas_call(
-        functools.partial(kernel, size=len(bands)),
+        kernel,
         out_shape=[square] * outputs,
-        in_specs=[SCALAR] + [vmem] * (len(operands) + len(bands)),
+        in_specs=[SCALAR] + [vmem] * len(operands),
         out_specs=[vmem] * outputs,
         scratch_shapes=[pltpu.VMEM((rhs, rhs), F32)] * scratch,
         compiler_params=pltpu.CompilerParams(vmem_limit_bytes=VMEM_BYTES),
-        cost_estimate=pl.CostEstimate(
-            flops=1, bytes_accessed=1, transcendentals=0
-        ),
-    )(place, *operands, *bands)
+        cost_estimate=pl.CostEstimate(flops=1, bytes_accessed=1, transcendentals=0),
+    )(place, *operands)
 
 
 def body(sources, coarse_links):
@@ -537,8 +548,12 @@
     ahead, behind = shift(source, "xy", -1), shift(source, "xy", 1)
     later, earlier = shift(source, "ta", -1), shift(source, "ta", 1)
     energy = gram(source)
-    partial = time_terms(inner_forward(source, links), later, earlier, links)
-    image, products, bands = first_image(partial, ahead, behind, energy, links, place, size)
+    partial = inner_forward(source, links)
+    (late_links,) = after((links,), later, earlier)
+    partial = time_terms(partial, later, earlier, late_links)
+    joined = joined_links(late_links)
+    x_halo = after((ahead, behind), partial, energy, joined)
+    image, products, bands = first_image(partial, x_halo, energy, joined, place, size)
     to_ahead, to_behind, to_later, to_earlier = products
 
     part = first_stage(bands)
@@ -550,29 +565,26 @@
     from_ahead = shift(*after((to_behind,), part), "xy", -1)
     bands = third_stage(part, size)
     from_later = shift(*after((to_earlier,), *bands), "ta", -1)
-    alpha, energy = solve_call(solve_both_kernel, 2, 1, place, (), bands)
-    terms = from_earlier, from_later, from_behind, from_ahead
-    residual, rounded, bands = next_residual(adjoint, terms, source, alpha, place, size)
-
-    part = first_stage(bands)
-    ahead, later = shift(rounded, "xy", -1), shift(rounded, "ta", -1)
-    part, still_rounded, still_source = after((part, rounded, source), part)
-    partial = inner_forward(still_rounded, links)
-    begun = mixed(still_source, alpha)
-    (part,) = after((part,), ahead, later, partial, begun)
-    part = second_stage(part, size)
-    behind = shift(*after((rounded,), part), "xy", 1)
-    bands = third_stage(part, size)
-    earlier = shift(*after((rounded,), *bands), "ta", 1)
-    beta, fresh = solve_call(solve_side_kernel, 2, 0, place, (energy,), bands)
-
-    partial = time_terms(partial, later, earlier, links, image, beta)
-    search = mixed(source, beta, residual)
-    ahead, behind = after((ahead, behind), search, begun)
-    bands = second_gram(partial, ahead, behind, links, place, size)
+    first_solve = functools.partial(first_solve_kernel, size=size)
+    alpha, energy, curvature = solve_call(first_solve, 3, 0, place, *bands)
+    begun = begun_residual(adjoint, (from_earlier, from_behind), source, alpha)
+    from_ahead, from_later = after((from_ahead, from_later), begun)
+    residual, rounded = next_residual(begun, from_ahead, from_later, alpha)
+
+    ahead, behind = shift(rounded, "xy", -1), shift(rounded, "xy", 1)
+    later, earlier = shift(rounded, "ta", -1), shift(rounded, "ta", 1)
+    partial = inner_forward(rounded, links)
+    fresh = gram(residual)
+    (inverse,) = solve_call(inverse_kernel, 1, 1, place, energy)
+    x_halo = after((ahead, behind), partial, fresh, inverse)
+    t_halo = after((later, earlier), *x_halo)
+    bands = second_gram(partial, x_halo + t_halo, fresh, joined, place, size)
     bands = third_stage(second_stage(first_stage(bands), size), size)
-    (second_alpha,) = solve_call(solve_matrix_kernel, 1, 1, place, (fresh,), bands)
-    return answer(search, second_alpha, begun).reshape(shape)
+    second_solve = functools.partial(second_solve_kernel, size=size)
+    second_alpha, weights = solve_call(
+        second_solve, 2, 2, place, inverse, curvature, alpha, *bands
+    )
+    return answer(source, residual, weights, second_alpha).reshape(shape)
 
 
 def solution(mesh):

time: 303 us -> 288 us (0.950)
  waiting for transfers between devices: 183 us -> 173 us
  starting transfers between devices: 33.7 us -> 29 us
    ppermute x18 -> x12, waiting for transfers between devices: 50.4 us -> 29 us  [turn(): lax.ppermute(value, axis, [(i, i - i % size + (i % size + step) % size) f...]
    ppermute x21 -> x18, waiting for transfers between devices: 132 us -> 144 us  [shift(): lax.ppermute(value, axis, [(i, (i + step) % count) for i in range(count)])]
    ppermute x18 -> x12, starting transfers between devices: 10.8 us -> 7.65 us  [turn(): lax.ppermute(value, axis, [(i, i - i % size + (i % size + step) % size) f...]
    pallas_call x10 -> x9, Pallas kernels: 58.8 us -> 56.5 us  [the longest x3 38.6 us: solve_call(): pl.pallas_call(kernel, out_shape=[square] * outputs, in_specs=[SCALAR] +...]
    ppermute x21 -> x18, starting transfers between devices: 22.9 us -> 21.4 us  [shift(): lax.ppermute(value, axis, [(i, (i + step) % count) for i in range(count)])]
  transfers between devices with their start and end apart: 39 -> 30, of which waited for: 28 -> 19; matrix products, arithmetic and copies ran while one was open for 0% -> 0% of each run, Pallas kernels for 14% -> 15%
where the time goes in v4:
time: 288 us; the launch traced here: 284 us
  waiting for transfers between devices  173 us (60%)
  Pallas kernels  73.5 us (26%)
  starting transfers between devices  29 us (10%)
  local copies, waits for them, and re-layouts  7.52 us (3%)
    ppermute x18, waiting for transfers between devices, shift(): lax.ppermute(value, axis, [(i, (i + step) % count) for i in range(count)])  144 us
    pallas_call x3, Pallas kernels, solve_call(): pl.pallas_call(kernel, out_shape=[square] * outputs, in_specs=[SCALAR] +...  38.6 us
    ppermute x12, waiting for transfers between devices, turn(): lax.ppermute(value, axis, [(i, i - i % size + (i % size + step) % size) f...  29 us
    ppermute x18, starting transfers between devices, shift(): lax.ppermute(value, axis, [(i, (i + step) % count) for i in range(count)])  21.4 us
    ppermute x12, starting transfers between devices, turn(): lax.ppermute(value, axis, [(i, i - i % size + (i % size + step) % size) f...  7.65 us
    unnamed x12, local copies, waits for them, and re-layouts  7.52 us
  transfers between devices with their start and end apart: 30, of which 19 were waited for; matrix products, arithmetic and copies ran while one was open for 0% of the time, Pallas kernels for 15%

profile of v4, /device:TPU:0, one launch (start us, length us, event | category | flops | bytes accessed | tf_op | source)
XLA Modules:
  0.0 284.0 jit_solution(64000701767100273)
XLA Ops:
  2.4 2.4 collective-permute-start.3
  4.8 2.0 collective-permute-start.2
  9.6 3.0 %copy-done = bf16[9,4,1,1,8,96,96]{6,5,4,3,2,1,0:T(8,128)(2,1)S(1)} copy-done((bf16[9,4,1,1,8,96,96]{6,5,4,3,2,1,0:T(8,128)(2,1)S(1)}, bf16[9,4,1,1,8,96,96]{6,5,4,3,2,1,0:T(8,128)(2,1)}, u32[]{:S(2)}) %copy-start) | copy-done | bytes 5308440
  12.6 2.7 shard_map.28.partial
  15.3 19.7 %collective-permute-done.1.earlier = bf16[4,8,96,256]{3,2,1,0:T(8,128)(2,1)} collective-permute-done((bf16[4,8,96,256]{3,2,1,0:T(8,128)(2,1)}, bf16[4,8,96,256]{3,2,1,0:T(8,128)(2,1)}, u32[]{:S(2)}, u32[]{:S(2)}) %collective-permute-start.1) | collective-permute-done | bytes 1572896 | tf_op jit(solution)/shard_map/ppermute | solution.py:19
  35.0 2.5 collective-permute-done.later
  37.5 3.0 %copy-done.1 = bf16[9,4,1,1,8,96,96]{6,5,4,3,2,1,0:T(8,128)(2,1)S(1)} copy-done((bf16[9,4,1,1,8,96,96]{6,5,4,3,2,1,0:T(8,128)(2,1)S(1)}, bf16[9,4,1,1,8,96,96]{6,5,4,3,2,1,0:T(8,128)(2,1)}, u32[]{:S(2)}) %copy-start.1) | copy-done | bytes 5308440
  41.5 3.8 %shard_map.29.partial = f32[4,8,96,256]{3,2,1,0:T(8,128)S(1)} custom-call(f32[4,8,96,256]{3,2,1,0:T(8,128)S(1)} %shard_map.28.partial, bf16[4,8,96,256]{3,2,1,0:T(8,128)(2,1)} %collective-permute-done.later, bf16[4,8,96,256]{3,2,1,0:T(8,128)(2,1)} %collective-permute-done.1.earlier, bf16[9,4,8,96,96]{4,3,2,1,0:T(8,128)(2,1)S(1)} %bitcast.15, ...), custom_call_target="tpu_custom_call" | custom-call | flops 1 | bytes 1 | tf_op jit(solution)/shard_map/pallas_call | solution.py:167
  45.3 29.4 %collective-permute-done.2.rest_0_ = bf16[4,8,96,256]{3,2,1,0:T(8,128)(2,1)} collective-permute-done((bf16[4,8,96,256]{3,2,1,0:T(8,128)(2,1)}, bf16[4,8,96,256]{3,2,1,0:T(8,128)(2,1)}, u32[]{:S(2)}, u32[]{:S(2)}) %collective-permute-start.2) | collective-permute-done | bytes 1572896 | tf_op jit(solution)/shard_map/ppermute | solution.py:19
  74.7 5.1 %shard_map.32 = (bf16[4,8,96,256]{3,2,1,0:T(8,128)(2,1)S(1)}, bf16[4,8,96,256]{3,2,1,0:T(8,128)(2,1)S(1)}, bf16[4,8,96,256]{3,2,1,0:T(8,128)(2,1)S(1)}, bf16[4,8...) custom-call(s32[1]{0:T(128)} %bitcast.1.place, ...), custom_call_target="tpu_custom_call" | custom-call | flops 1 | bytes 1 | tf_op jit(solution)/shard_map/pallas_call | solution.py:232
  83.1 19.0 %collective-permute-done.4 = f32[72,256]{1,0:T(8,128)S(1)} collective-permute-done((f32[72,256]{1,0:T(8,128)S(1)}, f32[72,256]{1,0:T(8,128)S(1)}, u32[]{:S(2)}, u32[]{:S(2)}) %collective-permute-start.4) | collective-permute-done | bytes 73760 | tf_op jit(solution)/shard_map/ppermute | solution.py:28
  102.2 2.9 %shard_map.33.partial = f32[4,8,96,256]{3,2,1,0:T(8,128)S(1)} custom-call(bf16[4,8,96,256]{3,2,1,0:T(8,128)(2,1)S(1)} %get-tuple-element.47.here.above.below, bf16[4,8,96,256]{3,2,1,0:T(8,128)(2,1)S(1)} %get-tuple-element.47.here.above.below, bf16[4,8,96,256]{3,2,1,0:T(8,128)(2,1)S(1)} %get-tuple-element.47.here.above.below, ...), custom_call_target="tpu_custom_call" | custom-call | flops 1 | bytes 1 | tf_op jit(solution)/shard_map/pallas_call | solution.py:258
  105.1 13.5 %collective-permute-done.8.second = bf16[4,8,96,256]{3,2,1,0:T(8,128)(2,1)S(1)} collective-permute-done((bf16[4,8,96,256]{3,2,1,0:T(8,128)(2,1)S(1)}, bf16[4,8,96,256]{3,2,1,0:T(8,128)(2,1)S(1)}, u32[]{:S(2)}, u32[]{:S(2)}) %collective-permute-start.8) | collective-permute-done | bytes 1572896 | tf_op jit(solution)/shard_map/ppermute | solution.py:19
  120.6 3.0 %collective-permute-done.11 = f32[72,256]{1,0:T(8,128)S(1)} collective-permute-done((f32[72,256]{1,0:T(8,128)S(1)}, f32[72,256]{1,0:T(8,128)S(1)}, u32[]{:S(2)}, u32[]{:S(2)}) %collective-permute-start.11) | collective-permute-done | bytes 73760 | tf_op jit(solution)/shard_map/ppermute | solution.py:19
  123.7 3.3 %collective-permute-done.10 = f32[72,256]{1,0:T(8,128)S(1)} collective-permute-done((f32[72,256]{1,0:T(8,128)S(1)}, f32[72,256]{1,0:T(8,128)S(1)}, u32[]{:S(2)}, u32[]{:S(2)}) %collective-permute-start.10) | collective-permute-done | bytes 73760 | tf_op jit(solution)/shard_map/ppermute | solution.py:19
  129.7 2.5 collective-permute-done.13.refs_2_
  132.8 11.9 %shard_map.34 = (f32[256,256]{1,0:T(8,128)S(1)}, f32[256,256]{1,0:T(8,128)S(1)}, f32[256,256]{1,0:T(8,128)S(1)}) custom-call(s32[1]{0:T(128)} %bitcast.1.place, f32[72,256]{1,0:T(8,128)S(1)} %add_add_fusion.2.refs_0_, f32[72,256]{1,0:T(8,128)S(1)} %collective-permute-done.12.refs_1_, f32[72,256]{1,0:T(8,128)S(1)} %collective-permute-done.13.refs_2_, ...), custom_call_target="tpu_custom_call" | custom-call | flops 1 | bytes 1 | tf_op jit(solution)/shard_map/pallas_call | solution.py:529
  144.8 3.4 %shard_map.35.begun = f32[4,8,96,256]{3,2,1,0:T(8,128)S(1)} custom-call(f32[4,8,96,256]{3,2,1,0:T(8,128)S(1)} %shard_map.33.partial, bf16[4,8,96,256]{3,2,1,0:T(8,128)(2,1)S(1)} %collective-permute-done.7.first, bf16[4,8,96,256]{3,2,1,0:T(8,128)(2,1)S(1)} %collective-permute-done.8.second, bf16[4,8,96,256]{3,2,1,0:T(8,128)(2,1)S(1)} %bitcast.37, ...), custom_call_target="tpu_custom_call" | custom-call | flops 1 | bytes 1 | tf_op jit(solution)/shard_map/pallas_call | solution.py:278
  148.2 17.2 %collective-permute-done.15.first = bf16[4,8,96,256]{3,2,1,0:T(8,128)(2,1)S(1)} collective-permute-done((bf16[4,8,96,256]{3,2,1,0:T(8,128)(2,1)S(1)}, bf16[4,8,96,256]{3,2,1,0:T(8,128)(2,1)S(1)}, u32[]{:S(2)}, u32[]{:S(2)}) %collective-permute-start.15) | collective-permute-done | bytes 1572896 | tf_op jit(solution)/shard_map/ppermute | solution.py:19
  165.4 2.8 shard_map.36
  168.8 3.3 %collective-permute-start.17 = (bf16[4,8,96,256]{3,2,1,0:T(8,128)(2,1)S(1)}, bf16[4,8,96,256]{3,2,1,0:T(8,128)(2,1)S(1)}, u32[]{:S(2)}, u32[]{:S(2)}) collective-permute-start(bf16[4,8,96,256]{3,2,1,0:T(8,128)(2,1)S(1)} %get-tuple-element.62.here.above.below), channel_id=1, source_target_pairs={{0,3},{1,0},{2,1},{3,2},{4,7},{5,4},{6,5},{7,6},{8,11},{9,8},{10,9... | collective-permute-start | bytes 4718600 | tf_op jit(solution)/shard_map/ppermute | solution.py:19
  174.0 11.7 %shard_map.37.inverse = f32[256,256]{1,0:T(8,128)S(1)} custom-call(s32[1]{0:T(128)} %bitcast.1.place, f32[256,256]{1,0:T(8,128)S(1)} %get-tuple-element.60.matrix), custom_call_target="tpu_custom_call" | custom-call | flops 1 | bytes 1 | tf_op jit(solution)/shard_map/pallas_call | solution.py:529
  185.7 2.7 shard_map.38.partial
  188.4 2.2 shard_map.39.fresh
  190.7 16.7 %collective-permute-done.18.rest_1_ = bf16[4,8,96,256]{3,2,1,0:T(8,128)(2,1)S(1)} collective-permute-done((bf16[4,8,96,256]{3,2,1,0:T(8,128)(2,1)S(1)}, bf16[4,8,96,256]{3,2,1,0:T(8,128)(2,1)S(1)}, u32[]{:S(2)}, u32[]{:S(2)}) %collective-permute-start.18) | collective-permute-done | bytes 1572896 | tf_op jit(solution)/shard_map/ppermute | solution.py:19
  207.4 31.7 %collective-permute-done.17.rest_0_ = bf16[4,8,96,256]{3,2,1,0:T(8,128)(2,1)S(1)} collective-permute-done((bf16[4,8,96,256]{3,2,1,0:T(8,128)(2,1)S(1)}, bf16[4,8,96,256]{3,2,1,0:T(8,128)(2,1)S(1)}, u32[]{:S(2)}, u32[]{:S(2)}) %collective-permute-start.17) | collective-permute-done | bytes 1572896 | tf_op jit(solution)/shard_map/ppermute | solution.py:19
  239.1 2.8 shard_map.40
  247.2 2.7 collective-permute-start.26
  252.5 5.5 %collective-permute-done.25 = f32[72,256]{1,0:T(8,128)S(1)} collective-permute-done((f32[72,256]{1,0:T(8,128)S(1)}, f32[72,256]{1,0:T(8,128)S(1)}, u32[]{:S(2)}, u32[]{:S(2)}) %collective-permute-start.25) | collective-permute-done | bytes 73760 | tf_op jit(solution)/shard_map/ppermute | solution.py:19
  261.4 2.7 collective-permute-done.28.refs_2_
  264.4 15.0 %shard_map.41 = (f32[256,256]{1,0:T(8,128)S(1)}, f32[256,256]{1,0:T(8,128)S(1)}) custom-call(s32[1]{0:T(128)} %bitcast.1.place, f32[256,256]{1,0:T(8,128)S(1)} %shard_map.37.inverse, f32[256,256]{1,0:T(8,128)S(1)} %get-tuple-element.61.first, f32[256,256]{1,0:T(8,128)S(1)} %get-tuple-element.52.alpha, f32[72,256]{1,0:T(8,128)S(1)} %add_add_fusion.refs_0_, ...), custom_call_target="tpu_custom_call" | custom-call | flops 1 | bytes 1 | tf_op jit(solution)/shard_map/pallas_call | solution.py:529
  279.4 4.2 %shard_map.42 = f32[4,8,96,256]{3,2,1,0:T(8,128)} custom-call(bf16[4,8,96,256]{3,2,1,0:T(8,128)(2,1)S(1)} %bitcast.38, f32[4,8,96,256]{3,2,1,0:T(8,128)S(1)} %get-tuple-element.59.vector.residual, f32[256,256]{1,0:T(8,128)S(1)} %get-tuple-element.71.first, f32[256,256]{1,0:T(8,128)S(1)} %get-tuple-element.72.second), custom_call_target="tpu_custom_call" | custom-call | flops 1 | bytes 1 | tf_op jit(solution)/shard_map/pallas_call | solution.py:322
  (60 shorter events, 28.8 us)
Async XLA Ops:
  0.0 35.0 %collective-permute-start.1 = (bf16[4,8,96,256]{3,2,1,0:T(8,128)(2,1)}, bf16[4,8,96,256]{3,2,1,0:T(8,128)(2,1)}, u32[]{:S(2)}, u32[]{:S(2)}) collective-permute-start(bf16[4,8,96,256]{3,2,1,0:T(8,128)(2,1)} %bitcast.29), channel_id=1, source_target_pairs={{0,4},{4,8},{8,12},{12,0},{1,5},{5,9},{9,13},{13,1},{2,6},{6,10},{... | collective-permute-start | bytes 4718600 | tf_op jit(solution)/shard_map/ppermute | solution.py:19
  0.5 37.0 %collective-permute-start = (bf16[4,8,96,256]{3,2,1,0:T(8,128)(2,1)}, bf16[4,8,96,256]{3,2,1,0:T(8,128)(2,1)}, u32[]{:S(2)}, u32[]{:S(2)}) collective-permute-start(bf16[4,8,96,256]{3,2,1,0:T(8,128)(2,1)} %bitcast.30), channel_id=1, source_target_pairs={{0,12},{4,0},{8,4},{12,8},{1,13},{5,1},{9,5},{13,9},{2,14},{6,2},{... | collective-permute-start | bytes 4718600 | tf_op jit(solution)/shard_map/ppermute | solution.py:19
  2.4 42.8 %collective-permute-start.3 = (bf16[4,8,96,256]{3,2,1,0:T(8,128)(2,1)}, bf16[4,8,96,256]{3,2,1,0:T(8,128)(2,1)}, u32[]{:S(2)}, u32[]{:S(2)}) collective-permute-start(bf16[4,8,96,256]{3,2,1,0:T(8,128)(2,1)} %bitcast.31), channel_id=1, source_target_pairs={{0,1},{1,2},{2,3},{3,0},{4,5},{5,6},{6,7},{7,4},{8,9},{9,10},{10,1... | collective-permute-start | bytes 4718600 | tf_op jit(solution)/shard_map/ppermute | solution.py:19
  4.8 69.9 %collective-permute-start.2 = (bf16[4,8,96,256]{3,2,1,0:T(8,128)(2,1)}, bf16[4,8,96,256]{3,2,1,0:T(8,128)(2,1)}, u32[]{:S(2)}, u32[]{:S(2)}) collective-permute-start(bf16[4,8,96,256]{3,2,1,0:T(8,128)(2,1)} %bitcast.32), channel_id=1, source_target_pairs={{0,3},{1,0},{2,1},{3,2},{4,7},{5,4},{6,5},{7,6},{8,11},{9,8},{10,9... | collective-permute-start | bytes 4718600 | tf_op jit(solution)/shard_map/ppermute | solution.py:19
  40.5 61.6 %slice-start = ((s8[7077888]{0:T(1024)(128)(4,1)}), s8[4194304]{0:T(1024)(128)(4,1)S(1)}, s32[]{:S(2)}) async-start(s8[7077888]{0:T(1024)(128)(4,1)} %bitcast.17), calls=%async_computation | async-start | bytes 8388608
  41.5 60.7 %slice-start.1 = ((s8[7077888]{0:T(1024)(128)(4,1)}), s8[2883584]{0:T(1024)(128)(4,1)S(1)}, s32[]{:S(2)}) async-start(s8[7077888]{0:T(1024)(128)(4,1)} %bitcast.17), calls=%async_computation.1 | async-start | bytes 5767168
  79.8 25.3 %collective-permute-start.7 = (bf16[4,8,96,256]{3,2,1,0:T(8,128)(2,1)S(1)}, bf16[4,8,96,256]{3,2,1,0:T(8,128)(2,1)S(1)}, u32[]{:S(2)}, u32[]{:S(2)}) collective-permute-start(bf16[4,8,96,256]{3,2,1,0:T(8,128)(2,1)S(1)} %get-tuple-element.48), channel_id=1, source_target_pairs={{0,4},{4,8},{8,12},{12,0},{1,5},{5,9},{9,13},{13,1},{2,6},{6,10},{... | collective-permute-start | bytes 4718600 | tf_op jit(solution)/shard_map/ppermute | solution.py:19
  79.9 38.7 %collective-permute-start.8 = (bf16[4,8,96,256]{3,2,1,0:T(8,128)(2,1)S(1)}, bf16[4,8,96,256]{3,2,1,0:T(8,128)(2,1)S(1)}, u32[]{:S(2)}, u32[]{:S(2)}) collective-permute-start(bf16[4,8,96,256]{3,2,1,0:T(8,128)(2,1)S(1)} %get-tuple-element.49), channel_id=1, source_target_pairs={{0,1},{1,2},{2,3},{3,0},{4,5},{5,6},{6,7},{7,4},{8,9},{9,10},{10,1... | collective-permute-start | bytes 4718600 | tf_op jit(solution)/shard_map/ppermute | solution.py:19
  81.1 21.0 %collective-permute-start.4 = (f32[72,256]{1,0:T(8,128)S(1)}, f32[72,256]{1,0:T(8,128)S(1)}, u32[]{:S(2)}, u32[]{:S(2)}) collective-permute-start(f32[72,256]{1,0:T(8,128)S(1)} %get-tuple-element.43), channel_id=1, source_target_pairs={{0,4},{4,8},{8,12},{12,0},{1,5},{5,9},{9,13},{13,1},{2,6},{6,10},{... | collective-permute-start | bytes 221192 | tf_op jit(solution)/shard_map/ppermute | solution.py:28
  81.4 20.7 %collective-permute-start.5 = (f32[72,256]{1,0:T(8,128)S(1)}, f32[72,256]{1,0:T(8,128)S(1)}, u32[]{:S(2)}, u32[]{:S(2)}) collective-permute-start(f32[72,256]{1,0:T(8,128)S(1)} %get-tuple-element.44), channel_id=1, source_target_pairs={{0,8},{4,12},{8,0},{12,4},{1,9},{5,13},{9,1},{13,5},{2,10},{6,14},... | collective-permute-start | bytes 221192 | tf_op jit(solution)/shard_map/ppermute | solution.py:28
  82.9 19.2 %collective-permute-start.6 = (f32[72,256]{1,0:T(8,128)S(1)}, f32[72,256]{1,0:T(8,128)S(1)}, u32[]{:S(2)}, u32[]{:S(2)}) collective-permute-start(f32[72,256]{1,0:T(8,128)S(1)} %get-tuple-element.45), channel_id=1, source_target_pairs={{0,12},{4,0},{8,4},{12,8},{1,13},{5,1},{9,5},{13,9},{2,14},{6,2},{... | collective-permute-start | bytes 221192 | tf_op jit(solution)/shard_map/ppermute | solution.py:28
  118.6 5.1 %collective-permute-start.11 = (f32[72,256]{1,0:T(8,128)S(1)}, f32[72,256]{1,0:T(8,128)S(1)}, u32[]{:S(2)}, u32[]{:S(2)}) collective-permute-start(f32[72,256]{1,0:T(8,128)S(1)} %add_add_fusion.3), channel_id=1, source_target_pairs={{0,3},{1,0},{2,1},{3,2},{4,7},{5,4},{6,5},{7,6},{8,11},{9,8},{10,9... | collective-permute-start | bytes 221192 | tf_op jit(solution)/shard_map/ppermute | solution.py:19
  119.1 7.9 %collective-permute-start.10 = (f32[72,256]{1,0:T(8,128)S(1)}, f32[72,256]{1,0:T(8,128)S(1)}, u32[]{:S(2)}, u32[]{:S(2)}) collective-permute-start(f32[72,256]{1,0:T(8,128)S(1)} %add_add_fusion.3), channel_id=1, source_target_pairs={{0,2},{1,3},{2,0},{3,1},{4,6},{5,7},{6,4},{7,5},{8,10},{9,11},{10,... | collective-permute-start | bytes 221192 | tf_op jit(solution)/shard_map/ppermute | solution.py:19
  119.4 7.6 %collective-permute-start.9 = (f32[72,256]{1,0:T(8,128)S(1)}, f32[72,256]{1,0:T(8,128)S(1)}, u32[]{:S(2)}, u32[]{:S(2)}) collective-permute-start(f32[72,256]{1,0:T(8,128)S(1)} %add_add_fusion.3), channel_id=1, source_target_pairs={{0,1},{1,2},{2,3},{3,0},{4,5},{5,6},{6,7},{7,4},{8,9},{9,10},{10,1... | collective-permute-start | bytes 221192 | tf_op jit(solution)/shard_map/ppermute | solution.py:19
  127.0 2.7 collective-permute-start.14
  127.1 5.1 %collective-permute-start.13 = (f32[72,256]{1,0:T(8,128)S(1)}, f32[72,256]{1,0:T(8,128)S(1)}, u32[]{:S(2)}, u32[]{:S(2)}) collective-permute-start(f32[72,256]{1,0:T(8,128)S(1)} %add_add_fusion.2.refs_0_), channel_id=1, source_target_pairs={{0,8},{4,12},{8,0},{12,4},{1,9},{5,13},{9,1},{13,5},{2,10},{6,14},... | collective-permute-start | bytes 221192 | tf_op jit(solution)/shard_map/ppermute | solution.py:28
  128.0 4.6 %collective-permute-start.12 = (f32[72,256]{1,0:T(8,128)S(1)}, f32[72,256]{1,0:T(8,128)S(1)}, u32[]{:S(2)}, u32[]{:S(2)}) collective-permute-start(f32[72,256]{1,0:T(8,128)S(1)} %add_add_fusion.2.refs_0_), channel_id=1, source_target_pairs={{0,4},{4,8},{8,12},{12,0},{1,5},{5,9},{9,13},{13,1},{2,6},{6,10},{... | collective-permute-start | bytes 221192 | tf_op jit(solution)/shard_map/ppermute | solution.py:28
  128.2 37.1 %collective-permute-start.15 = (bf16[4,8,96,256]{3,2,1,0:T(8,128)(2,1)S(1)}, bf16[4,8,96,256]{3,2,1,0:T(8,128)(2,1)S(1)}, u32[]{:S(2)}, u32[]{:S(2)}) collective-permute-start(bf16[4,8,96,256]{3,2,1,0:T(8,128)(2,1)S(1)} %get-tuple-element.54), channel_id=1, source_target_pairs={{0,3},{1,0},{2,1},{3,2},{4,7},{5,4},{6,5},{7,6},{8,11},{9,8},{10,9... | collective-permute-start | bytes 4718600 | tf_op jit(solution)/shard_map/ppermute | solution.py:19
  132.7 32.7 %collective-permute-start.16 = (bf16[4,8,96,256]{3,2,1,0:T(8,128)(2,1)S(1)}, bf16[4,8,96,256]{3,2,1,0:T(8,128)(2,1)S(1)}, u32[]{:S(2)}, u32[]{:S(2)}) collective-permute-start(bf16[4,8,96,256]{3,2,1,0:T(8,128)(2,1)S(1)} %get-tuple-element.56), channel_id=1, source_target_pairs={{0,12},{4,0},{8,4},{12,8},{1,13},{5,1},{9,5},{13,9},{2,14},{6,2},{... | collective-permute-start | bytes 4718600 | tf_op jit(solution)/shard_map/ppermute | solution.py:19
  168.2 39.1 %collective-permute-start.18 = (bf16[4,8,96,256]{3,2,1,0:T(8,128)(2,1)S(1)}, bf16[4,8,96,256]{3,2,1,0:T(8,128)(2,1)S(1)}, u32[]{:S(2)}, u32[]{:S(2)}) collective-permute-start(bf16[4,8,96,256]{3,2,1,0:T(8,128)(2,1)S(1)} %get-tuple-element.62.here.above.below), channel_id=1, source_target_pairs={{0,1},{1,2},{2,3},{3,0},{4,5},{5,6},{6,7},{7,4},{8,9},{9,10},{10,1... | collective-permute-start | bytes 4718600 | tf_op jit(solution)/shard_map/ppermute | solution.py:19
  168.8 70.3 %collective-permute-start.17 = (bf16[4,8,96,256]{3,2,1,0:T(8,128)(2,1)S(1)}, bf16[4,8,96,256]{3,2,1,0:T(8,128)(2,1)S(1)}, u32[]{:S(2)}, u32[]{:S(2)}) collective-permute-start(bf16[4,8,96,256]{3,2,1,0:T(8,128)(2,1)S(1)} %get-tuple-element.62.here.above.below), channel_id=1, source_target_pairs={{0,3},{1,0},{2,1},{3,2},{4,7},{5,4},{6,5},{7,6},{8,11},{9,8},{10,9... | collective-permute-start | bytes 4718600 | tf_op jit(solution)/shard_map/ppermute | solution.py:19
  172.1 67.0 %collective-permute-start.20 = (bf16[4,8,96,256]{3,2,1,0:T(8,128)(2,1)S(1)}, bf16[4,8,96,256]{3,2,1,0:T(8,128)(2,1)S(1)}, u32[]{:S(2)}, u32[]{:S(2)}) collective-permute-start(bf16[4,8,96,256]{3,2,1,0:T(8,128)(2,1)S(1)} %get-tuple-element.62.here.above.below), channel_id=1, source_target_pairs={{0,4},{4,8},{8,12},{12,0},{1,5},{5,9},{9,13},{13,1},{2,6},{6,10},{... | collective-permute-start | bytes 4718600 | tf_op jit(solution)/shard_map/ppermute | solution.py:19
  172.1 67.0 %collective-permute-start.19 = (bf16[4,8,96,256]{3,2,1,0:T(8,128)(2,1)S(1)}, bf16[4,8,96,256]{3,2,1,0:T(8,128)(2,1)S(1)}, u32[]{:S(2)}, u32[]{:S(2)}) collective-permute-start(bf16[4,8,96,256]{3,2,1,0:T(8,128)(2,1)S(1)} %get-tuple-element.62.here.above.below), channel_id=1, source_target_pairs={{0,12},{4,0},{8,4},{12,8},{1,13},{5,1},{9,5},{13,9},{2,14},{6,2},{... | collective-permute-start | bytes 4718600 | tf_op jit(solution)/shard_map/ppermute | solution.py:19
  241.9 4.0 %collective-permute-start.21 = (f32[72,256]{1,0:T(8,128)S(1)}, f32[72,256]{1,0:T(8,128)S(1)}, u32[]{:S(2)}, u32[]{:S(2)}) collective-permute-start(f32[72,256]{1,0:T(8,128)S(1)} %get-tuple-element.68), channel_id=1, source_target_pairs={{0,4},{4,8},{8,12},{12,0},{1,5},{5,9},{9,13},{13,1},{2,6},{6,10},{... | collective-permute-start | bytes 221192 | tf_op jit(solution)/shard_map/ppermute | solution.py:28
  242.0 5.2 %collective-permute-start.22 = (f32[72,256]{1,0:T(8,128)S(1)}, f32[72,256]{1,0:T(8,128)S(1)}, u32[]{:S(2)}, u32[]{:S(2)}) collective-permute-start(f32[72,256]{1,0:T(8,128)S(1)} %get-tuple-element.69), channel_id=1, source_target_pairs={{0,8},{4,12},{8,0},{12,4},{1,9},{5,13},{9,1},{13,5},{2,10},{6,14},... | collective-permute-start | bytes 221192 | tf_op jit(solution)/shard_map/ppermute | solution.py:28
  243.1 4.1 %collective-permute-start.23 = (f32[72,256]{1,0:T(8,128)S(1)}, f32[72,256]{1,0:T(8,128)S(1)}, u32[]{:S(2)}, u32[]{:S(2)}) collective-permute-start(f32[72,256]{1,0:T(8,128)S(1)} %get-tuple-element.70), channel_id=1, source_target_pairs={{0,12},{4,0},{8,4},{12,8},{1,13},{5,1},{9,5},{13,9},{2,14},{6,2},{... | collective-permute-start | bytes 221192 | tf_op jit(solution)/shard_map/ppermute | solution.py:28
  247.2 5.4 %collective-permute-start.26 = (f32[72,256]{1,0:T(8,128)S(1)}, f32[72,256]{1,0:T(8,128)S(1)}, u32[]{:S(2)}, u32[]{:S(2)}) collective-permute-start(f32[72,256]{1,0:T(8,128)S(1)} %add_add_fusion.1), channel_id=1, source_target_pairs={{0,3},{1,0},{2,1},{3,2},{4,7},{5,4},{6,5},{7,6},{8,11},{9,8},{10,9... | collective-permute-start | bytes 221192 | tf_op jit(solution)/shard_map/ppermute | solution.py:19
  249.8 8.2 %collective-permute-start.25 = (f32[72,256]{1,0:T(8,128)S(1)}, f32[72,256]{1,0:T(8,128)S(1)}, u32[]{:S(2)}, u32[]{:S(2)}) collective-permute-start(f32[72,256]{1,0:T(8,128)S(1)} %add_add_fusion.1), channel_id=1, source_target_pairs={{0,2},{1,3},{2,0},{3,1},{4,6},{5,7},{6,4},{7,5},{8,10},{9,11},{10,... | collective-permute-start | bytes 221192 | tf_op jit(solution)/shard_map/ppermute | solution.py:19
  250.4 7.7 %collective-permute-start.24 = (f32[72,256]{1,0:T(8,128)S(1)}, f32[72,256]{1,0:T(8,128)S(1)}, u32[]{:S(2)}, u32[]{:S(2)}) collective-permute-start(f32[72,256]{1,0:T(8,128)S(1)} %add_add_fusion.1), channel_id=1, source_target_pairs={{0,1},{1,2},{2,3},{3,0},{4,5},{5,6},{6,7},{7,4},{8,9},{9,10},{10,1... | collective-permute-start | bytes 221192 | tf_op jit(solution)/shard_map/ppermute | solution.py:19
  258.1 3.3 %collective-permute-start.29 = (f32[72,256]{1,0:T(8,128)S(1)}, f32[72,256]{1,0:T(8,128)S(1)}, u32[]{:S(2)}, u32[]{:S(2)}) collective-permute-start(f32[72,256]{1,0:T(8,128)S(1)} %add_add_fusion.refs_0_), channel_id=1, source_target_pairs={{0,12},{4,0},{8,4},{12,8},{1,13},{5,1},{9,5},{13,9},{2,14},{6,2},{... | collective-permute-start | bytes 221192 | tf_op jit(solution)/shard_map/ppermute | solution.py:28
  258.9 5.2 %collective-permute-start.28 = (f32[72,256]{1,0:T(8,128)S(1)}, f32[72,256]{1,0:T(8,128)S(1)}, u32[]{:S(2)}, u32[]{:S(2)}) collective-permute-start(f32[72,256]{1,0:T(8,128)S(1)} %add_add_fusion.refs_0_), channel_id=1, source_target_pairs={{0,8},{4,12},{8,0},{12,4},{1,9},{5,13},{9,1},{13,5},{2,10},{6,14},... | collective-permute-start | bytes 221192 | tf_op jit(solution)/shard_map/ppermute | solution.py:28
  259.9 4.6 %collective-permute-start.27 = (f32[72,256]{1,0:T(8,128)S(1)}, f32[72,256]{1,0:T(8,128)S(1)}, u32[]{:S(2)}, u32[]{:S(2)}) collective-permute-start(f32[72,256]{1,0:T(8,128)S(1)} %add_add_fusion.refs_0_), channel_id=1, source_target_pairs={{0,4},{4,8},{8,12},{12,0},{1,5},{5,9},{9,13},{13,1},{2,6},{6,10},{... | collective-permute-start | bytes 221192 | tf_op jit(solution)/shard_map/ppermute | solution.py:28
  (4 other events, 50.1 us)
